TPU v7x, 512 devices: a whole 4x8x8 slice. The times are simulated.
512 devices in a mesh: batch: 16 (over z, core), proto: 32 (over x, y).
Axes of the slice: x: 4, y: 8, z: 8, core: 2. Of those that a mesh axis runs over, the one named last changes fastest.
Arguments:
- student_feat: bfloat16 [16384, 256], P('batch', 'proto'), may hold values from -60 to 60
- teacher_feat: bfloat16 [16384, 256], P('batch', 'proto'), may hold values from -60 to 60
- student_proto: bfloat16 [256, 65536], P(None, 'proto'), may hold values from -60 to 60
- teacher_proto: bfloat16 [256, 65536], P(None, 'proto'), may hold values from -60 to 60
Outputs:
- loss_value: float32 [], replicated
- feat_grad: float32 [16384, 256], P('batch', 'proto')
- proto_grad: float32 [256, 65536], P('batch', 'proto')
All inputs are finite; a program needn't handle non-finite values.
Results may differ from a plain program's by a relative error of at most 0.0024.
Values may be sent and summed in bfloat16 or wider, within the bound.
No kernel may reach another device: no remote copies, remote signals or barrier semaphores. Data moves between devices by JAX's collectives and lax.ppermute only.
A program may use at most 64 MiB of HBM per device.

v0:
```python
import jax
import jax.numpy as jnp
from jax import lax
from jax.sharding import PartitionSpec as P

SWEEPS = 3


student_temp = 0.1
teacher_temp = 0.07


def unit_rows(raw):
    floated = raw.astype(jnp.float32)
    inverse = lax.rsqrt(jnp.sum(floated * floated, axis=1, keepdims=True) + 1e-06)
    normed = floated * inverse
    return (normed, normed.astype(jnp.bfloat16))


def unit_cols(raw):
    floated = raw.astype(jnp.float32)
    inverse = lax.rsqrt(jnp.sum(floated * floated, axis=0, keepdims=True) + 1e-06)
    normed = floated * inverse
    return (normed, normed.astype(jnp.bfloat16))


def per_device(student_feat, teacher_feat, student_proto, teacher_proto):
    row_count = student_feat.shape[0]
    feat_width = student_proto.shape[0]
    local_protos = student_proto.shape[1]
    crop_total = row_count * lax.axis_size("batch")
    protos = local_protos * lax.axis_size("proto")
    gathered_s, gathered_t = (
        lax.all_gather(student_feat, "proto", axis=1, tiled=True),
        lax.all_gather(teacher_feat, "proto", axis=1, tiled=True),
    )
    feat_unit, feat_round = unit_rows(gathered_s)
    teach_normed, teach_round = unit_rows(gathered_t)
    proto_unit, proto_round = unit_cols(student_proto)
    teach_cols_f, teacher_cols = unit_cols(teacher_proto)
    teacher_exp = jnp.exp(
        jnp.dot(teach_round, teacher_cols, preferred_element_type=jnp.float32) / teacher_temp
    )
    logits = jnp.dot(feat_round, proto_round, preferred_element_type=jnp.float32) / student_temp
    exp_local = jnp.sum(jnp.exp(logits), axis=1)
    row_scale = jnp.ones((row_count,), jnp.float32)
    col_scale = jnp.ones((local_protos,), jnp.float32)
    for sweep_index in range(SWEEPS):
        column_sum = lax.psum(
            jnp.dot(row_scale, teacher_exp, precision=lax.Precision.HIGHEST), "batch"
        )
        col_scale = 1.0 / (protos * column_sum)
        row_local = jnp.dot(teacher_exp, col_scale, precision=lax.Precision.HIGHEST)
        row_sum = lax.psum(row_local, "proto")
        row_scale = 1.0 / (crop_total * row_sum)
    exp_total = lax.psum(exp_local, "proto")
    log_total = jnp.log(exp_total)
    target = crop_total * teacher_exp * col_scale[None, :] * row_scale[:, None]
    leader = lax.axis_index("proto") == 0
    local_term = jnp.where(leader, jnp.sum(log_total), 0.0) - jnp.sum(target * logits)
    loss_value = lax.psum(local_term, ("batch", "proto")) / crop_total
    softmax_p = jnp.exp(logits - log_total[:, None])
    grad_logit = (protos * (softmax_p - target)).astype(jnp.bfloat16)
    feat_cols = feat_width // lax.axis_size("proto")
    proto_rows = feat_width // lax.axis_size("batch")
    feat_start = lax.axis_index("proto") * feat_cols
    row_start = lax.axis_index("batch") * proto_rows
    grad_local = lax.dot_general(
        grad_logit, proto_round, (((1,), (1,)), ((), ())), preferred_element_type=jnp.float32
    )
    grad_feat = lax.psum(grad_local, "proto")
    tangent = grad_feat - feat_unit * jnp.sum(feat_unit * grad_feat, axis=1, keepdims=True)
    feat_out = lax.dynamic_slice_in_dim(tangent, feat_start, feat_cols, 1)
    cols_local = lax.dot_general(
        feat_round, grad_logit, (((0,), (0,)), ((), ())), preferred_element_type=jnp.float32
    )
    grad_cols = lax.psum(cols_local, "batch")
    proto_tangent = grad_cols - proto_unit * jnp.sum(proto_unit * grad_cols, axis=0, keepdims=True)
    proto_out = lax.dynamic_slice_in_dim(proto_tangent, row_start, proto_rows, 0)
    return (loss_value, feat_out, proto_out)


def solution(mesh):
    placed = (P("batch", "proto"), P("batch", "proto"), P(None, "proto"), P(None, "proto"))
    return jax.shard_map(
        per_device,
        mesh=mesh,
        in_specs=placed,
        out_specs=(P(), P("batch", "proto"), P("batch", "proto")),
        check_vma=False,
    )
```

profile of v0, /device:TPU:1, one launch (start us, length us, event | category | flops | bytes accessed | tf_op | source)
XLA Modules:
  0.0 827.0 jit_solution(3423723717933420257)
XLA Ops:
  7.2 39.8 %all_gather.7 = bf16[1024,256]{0,1:T(8,128)(2,1)S(1)} all-gather(bf16[1024,8]{0,1:T(8,128)(2,1)} %param.5), channel_id=1, replica_groups=mesh['batch'=16,'proto'=32] {'proto'}, dimensions={1}, use_global_device_ids=true | all-gather | bytes 540672 | tf_op jit(solution)/shard_map/all_gather | solution.py:35
  48.6 2.6 multiply_exponential_fusion
  51.3 3.2 copy-done
  54.5 4.0 fusion.18
  58.5 41.7 %psum.71 = f32[2048]{0:T(1024)S(1)} all-reduce(f32[2048]{0:T(1024)S(1)} %bitcast.29), channel_id=1, replica_groups=mesh['batch'=16,'proto'=32] {'batch'}, use_global_device_ids=true, to_apply=%region_7.0 | all-reduce | flops 2048 | bytes 16384 | tf_op jit(solution)/shard_map/psum | solution.py:49
  100.2 9.4 %fusion.22 = f32[1,1024]{1,0:T(1,128)S(1)} fusion(f32[1024,2048]{1,0:T(8,128)} %copy-done, f32[2048,1]{0,1:T(1,128)S(1)} %bitcast.25), kind=kOutput, calls=%fused_computation.49 | convolution fusion | flops 25165824 | bytes 8400896 | tf_op jit(solution)/shard_map/dot_general | solution.py:53
  109.6 58.4 %psum.72 = f32[1024]{0:T(1024)S(1)} all-reduce(f32[1024]{0:T(1024)S(1)} %bitcast.30), channel_id=1, replica_groups=mesh['batch'=16,'proto'=32] {'proto'}, use_global_device_ids=true, to_apply=%region_8.0 | all-reduce | flops 1024 | bytes 8192 | tf_op jit(solution)/shard_map/psum | solution.py:54
  168.1 6.3 fusion.23
  174.4 37.6 %psum.73 = f32[2048]{0:T(1024)S(1)} all-reduce(f32[2048]{0:T(1024)S(1)} %bitcast.26), channel_id=1, replica_groups=mesh['batch'=16,'proto'=32] {'batch'}, use_global_device_ids=true, to_apply=%region_9.0 | all-reduce | flops 2048 | bytes 16384 | tf_op jit(solution)/shard_map/psum | solution.py:49
  212.0 9.4 %fusion.24 = f32[1,1024]{1,0:T(1,128)S(1)} fusion(f32[1024,2048]{1,0:T(8,128)} %copy-done, f32[2048,1]{0,1:T(1,128)S(1)} %bitcast.27), kind=kOutput, calls=%fused_computation.51 | convolution fusion | flops 25165824 | bytes 8400896 | tf_op jit(solution)/shard_map/dot_general | solution.py:53
  221.4 55.7 %psum.74 = f32[1024]{0:T(1024)S(1)} all-reduce(f32[1024]{0:T(1024)S(1)} %bitcast.32), channel_id=1, replica_groups=mesh['batch'=16,'proto'=32] {'proto'}, use_global_device_ids=true, to_apply=%region_10.0 | all-reduce | flops 1024 | bytes 8192 | tf_op jit(solution)/shard_map/psum | solution.py:54
  277.1 6.4 fusion.25
  283.6 38.0 %psum.75 = f32[2048]{0:T(1024)S(1)} all-reduce(f32[2048]{0:T(1024)S(1)} %bitcast.28), channel_id=1, replica_groups=mesh['batch'=16,'proto'=32] {'batch'}, use_global_device_ids=true, to_apply=%region_11.0 | all-reduce | flops 2048 | bytes 16384 | tf_op jit(solution)/shard_map/psum | solution.py:49
  321.6 9.4 %fusion.26 = f32[1,1024]{1,0:T(1,128)S(1)} fusion(f32[1024,2048]{1,0:T(8,128)} %copy-done, f32[2048,1]{0,1:T(1,128)S(1)} %bitcast.24), kind=kOutput, calls=%fused_computation.53 | convolution fusion | flops 25165824 | bytes 8400896 | tf_op jit(solution)/shard_map/dot_general | solution.py:53
  331.0 57.4 %psum.76 = f32[1024]{0:T(1024)S(1)} all-reduce(f32[1024]{0:T(1024)S(1)} %bitcast.34), channel_id=1, replica_groups=mesh['batch'=16,'proto'=32] {'proto'}, use_global_device_ids=true, to_apply=%region_12.0 | all-reduce | flops 1024 | bytes 8192 | tf_op jit(solution)/shard_map/psum | solution.py:54
  388.4 34.9 %all_gather.6 = bf16[1024,256]{0,1:T(8,128)(2,1)S(1)} all-gather(bf16[1024,8]{0,1:T(8,128)(2,1)S(1)} %copy-done.3), channel_id=1, replica_groups=mesh['batch'=16,'proto'=32] {'proto'}, dimensions={1}, use_global_device_ids=true | all-gather | bytes 540672 | tf_op jit(solution)/shard_map/all_gather | solution.py:34
  424.0 8.7 %multiply_reduce_fusion = (f32[]{:T(128)}, f32[1024]{0:T(1024)S(1)}, f32[1024,2048]{1,0:T(8,128)}) fusion(f32[1024,2048]{1,0:T(8,128)} %copy-done, f32[1024]{0:T(1024)S(1)} %multiply_divide_fusion.3, f32[2048]{0:T(1024)S(1)} %get-tuple-element.15, f32[2048]{0:T(1024)S(1)} %add_rsqrt_fusion.1, bf16[256,2048]{1,0:T(8,128)(2,1)S(1)} %copy-done.1, ...), kind=kOutput, calls=%fused_computation.1 | convolution fusion | flops 1088683008 | bytes 18378756 | tf_op jit(solution)/shard_map/dot_general | solution.py:44
  432.7 58.4 %psum.70 = f32[1024]{0:T(1024)S(1)} all-reduce(f32[1024]{0:T(1024)S(1)} %get-tuple-element.10), channel_id=1, replica_groups=mesh['batch'=16,'proto'=32] {'proto'}, use_global_device_ids=true, to_apply=%region_3.0 | all-reduce | flops 1024 | bytes 8192 | tf_op jit(solution)/shard_map/psum | solution.py:56
  491.6 7.1 multiply_convert_fusion
  500.7 2.3 fusion.9
  503.1 4.9 fusion.15
  509.3 132.9 %psum.77 = f32[]{:T(128)} all-reduce(f32[]{:T(128)S(6)} %sub.20), channel_id=1, replica_groups=mesh['batch'=16,'proto'=32] {'batch','proto'}, use_global_device_ids=true, to_apply=%region_14.15 | all-reduce | flops 1 | bytes 8 | tf_op jit(solution)/shard_map/psum | solution.py:61
  642.9 47.1 %all-reduce.3.cloned.1.call-done = f32[1024,256]{1,0:T(8,128)} async-done(((f32[1024,256]{1,0:T(8,128)}), f32[1024,256]{1,0:T(8,128)}) %all-reduce.3.cloned.1.call-update) | async-done | bytes 1048592 | tf_op jit(solution)/shard_map/psum | solution.py:71
  693.9 121.6 %all-reduce.5.cloned.1.call-done = f32[256,2048]{1,0:T(8,128)} async-done(((f32[256,2048]{1,0:T(8,128)}), f32[256,2048]{1,0:T(8,128)}) %all-reduce.5.cloned.1.call-update) | async-done | bytes 2097168 | tf_op jit(solution)/shard_map/psum | solution.py:77
  (32 shorter events, 12.4 us)
Async XLA Ops:
  7.2 682.8 %all-reduce.3.cloned.1.call-start = ((), (), s32[]{:S(2)}) async-start(), calls=%async_computation | async-start | bytes 2097152 | tf_op jit(solution)/shard_map/psum | solution.py:71
  51.3 3.2 copy-start
  277.1 111.3 %copy-start.3 = (bf16[1024,8]{0,1:T(8,128)(2,1)S(1)}, bf16[1024,8]{0,1:T(8,128)(2,1)}, u32[]{:S(2)}) copy-start(bf16[1024,8]{0,1:T(8,128)(2,1)} %param.4) | copy-start | bytes 49156
  277.1 146.6 %copy-start.1 = (bf16[256,2048]{1,0:T(8,128)(2,1)S(1)}, bf16[256,2048]{1,0:T(8,128)(2,1)}, u32[]{:S(2)}) copy-start(bf16[256,2048]{1,0:T(8,128)(2,1)} %param.6) | copy-start | bytes 3145732
  498.8 1.9 copy-start.2
  503.0 312.4 %all-reduce.5.cloned.1.call-start = ((), (), s32[]{:S(2)}) async-start(), calls=%async_computation.1 | async-start | bytes 4194304 | tf_op jit(solution)/shard_map/psum | solution.py:77
Sparse Core Ops, SparseCore 0:
  503.1 186.7 all-reduce.2
  692.3 123.0 all-reduce.4
where the time goes:
time: 828 us; the launch traced here: 827 us
  blocking collectives  555 us (67%)
  waiting for transfers between devices  169 us (20%)
  matrix products  63.5 us (8%)
  between operations  17.3 us (2%)
  other arithmetic  16.5 us (2%)
    psum x3, blocking collectives, per_device(): row_sum = lax.psum(row_local, 'proto')  172 us
    psum x1, blocking collectives, per_device(): loss_value = lax.psum(local_term, ('batch', 'proto')) / crop_total  133 us
    psum x1, waiting for transfers between devices, per_device(): grad_cols = lax.psum(cols_local, 'batch')  122 us
    psum x3, blocking collectives, per_device(): lax.psum(jnp.dot(row_scale, teacher_exp, precision=lax.Precision.HIGHEST)...  117 us
    psum x1, blocking collectives, per_device(): exp_total = lax.psum(exp_local, 'proto')  58.4 us
    psum x1, waiting for transfers between devices, per_device(): grad_feat = lax.psum(grad_local, 'proto')  47.1 us
    all_gather x1, blocking collectives, per_device(): lax.all_gather(teacher_feat, 'proto', axis=1, tiled=True)  39.8 us
    all_gather x1, blocking collectives, per_device(): lax.all_gather(student_feat, 'proto', axis=1, tiled=True)  34.9 us
  transfers between devices with their start and end apart: 2, of which 2 were waited for; matrix products, arithmetic and copies ran while one was open for 1% of the time, Pallas kernels for 0%

commit v1 on v0

v1 whole, which is shorter than its diff:
```python
import functools

import jax
import jax.numpy as jnp
from jax import lax
from jax.experimental import pallas as pl
from jax.experimental.pallas import tpu as pltpu
from jax.sharding import PartitionSpec as P

F32, BF16 = jnp.float32, jnp.bfloat16
SWEEPS = 3
LOG2E = 1.4426950408889634
STUDENT_SCALE = LOG2E / 0.1
TEACHER_SCALE = LOG2E / 0.07
D, ROWS, COLS = 256, 1024, 2048
LANES = 128
ROW_TILES, COL_TILES = ROWS // LANES, COLS // LANES
PROTO, BATCH = 32, 16
CROPS, PROTOS = ROWS * BATCH, COLS * PROTO
HALF = ROWS // 2
CHUNK = 512
VMEM_LIMIT = 30 * 1024 * 1024

VM = pl.BlockSpec(memory_space=pltpu.VMEM)
SM = pl.BlockSpec(memory_space=pltpu.SMEM)


def shape(dims, dtype=F32):
    return jax.ShapeDtypeStruct(dims, dtype)


def pinned(dims, dtype=F32):
    return pltpu.VMEM(dims, dtype)


def pin(array):
    return pltpu.with_memory_space_constraint(array, pltpu.VMEM)


def call(body, outs, args, scratch=(), scalars=0, name=None):
    return pl.pallas_call(
        body,
        out_shape=outs,
        in_specs=[SM] * scalars + [VM] * (len(args) - scalars),
        out_specs=[VM] * len(outs),
        scratch_shapes=list(scratch),
        compiler_params=pltpu.CompilerParams(vmem_limit_bytes=VMEM_LIMIT),
        name=name,
    )(*args)


def lane_major(tile):
    return jnp.sum(tile.T, axis=0, keepdims=True)


def sublane_major(row):
    return jnp.broadcast_to(row, (LANES, LANES)).T


def pack_kernel(feat_ref, out_ref):
    x = feat_ref[...].astype(F32)
    both = jnp.concatenate([x[:, :HALF], x[:, HALF:]], axis=0).astype(BF16)
    for peer in range(PROTO):
        out_ref[peer] = both


def unit_cols_kernel(raw_ref, round_ref, inv_ref):
    for lo in range(0, COLS, CHUNK):
        x = raw_ref[:, lo : lo + CHUNK].astype(F32)
        inv = lax.rsqrt(jnp.sum(x * x, axis=0, keepdims=True) + 1e-06)
        inv_ref[:, lo : lo + CHUNK] = inv
        round_ref[:, lo : lo + CHUNK] = (x * inv).astype(BF16)


def unit_rows(feat_ref, half):
    x = feat_ref[:, 8 * half : 8 * half + 8, :].astype(F32).reshape(D, HALF)
    inv = lax.rsqrt(jnp.sum(x * x, axis=0, keepdims=True) + 1e-06)
    return x, inv


def put_cols(out_ref, sums):
    for peer in range(BATCH):
        out_ref[peer] = sums


def put_rows(out_ref, rows, first=0):
    for peer in range(PROTO):
        out_ref[peer, first : first + ROW_TILES, :] = rows


def col_rows(acc_ref):
    total = jnp.sum(acc_ref[...], axis=0, keepdims=True)
    return jnp.concatenate([total[:, LANES * i : LANES * (i + 1)] for i in range(COL_TILES)], axis=0)


def teacher_kernel(feat_ref, cols_ref, exp_ref, out_ref, rows_ref, acc_ref):
    for half in range(2):
        x, inv = unit_rows(feat_ref, half)
        rows_ref[HALF * half : HALF * (half + 1), :] = (x * inv).T.astype(BF16)
    acc_ref[...] = jnp.zeros_like(acc_ref)

    def block(j, carry):
        at = pl.ds(pl.multiple_of(j * LANES, LANES), LANES)
        rows = rows_ref[at, :]
        for lo in range(0, COLS, CHUNK):
            z = jnp.dot(rows, cols_ref[:, lo : lo + CHUNK], preferred_element_type=F32)
            e = jnp.exp2(z * TEACHER_SCALE)
            exp_ref[at, lo : lo + CHUNK] = e
            acc_ref[:, lo : lo + CHUNK] += jnp.sum(e.reshape(LANES // 8, 8, CHUNK), axis=0)
        return carry

    lax.fori_loop(0, ROW_TILES, block, 0)
    put_cols(out_ref, col_rows(acc_ref))


def col_scale_of(got_ref):
    return 1.0 / (PROTOS * jnp.sum(got_ref[...], axis=0))


def row_pass_kernel(exp_ref, got_ref, out_ref, scale_ref, sum_ref):
    scale_ref[...] = col_scale_of(got_ref)

    def block(j, carry):
        at = pl.ds(pl.multiple_of(j * LANES, LANES), LANES)
        acc = jnp.zeros((LANES, LANES), F32)
        for i in range(COL_TILES):
            acc += exp_ref[at, LANES * i : LANES * (i + 1)] * scale_ref[i : i + 1, :]
        sum_ref[pl.ds(j, 1), :] = lane_major(acc)
        return carry

    lax.fori_loop(0, ROW_TILES, block, 0)
    put_rows(out_ref, sum_ref[...])


def col_pass_kernel(exp_ref, got_ref, out_ref, scale_ref, acc_ref):
    scale_ref[...] = 1.0 / (CROPS * jnp.sum(got_ref[...], axis=0))
    acc_ref[...] = jnp.zeros_like(acc_ref)

    def block(j, carry):
        at = pl.ds(pl.multiple_of(j * LANES, LANES), LANES)
        r = sublane_major(scale_ref[pl.ds(j, 1), :])
        for i in range(COL_TILES):
            lanes = slice(LANES * i, LANES * (i + 1))
            acc_ref[:, lanes] += jnp.sum((exp_ref[at, lanes] * r).reshape(LANES // 8, 8, LANES), axis=0)
        return carry

    lax.fori_loop(0, ROW_TILES, block, 0)
    put_cols(out_ref, col_rows(acc_ref))


def student_kernel(feat_ref, cols_ref, rows_ref, feat_out_ref, inv_ref, sum_ref):
    for half in range(2):
        x, inv = unit_rows(feat_ref, half)
        lanes = slice(HALF * half, HALF * (half + 1))
        unit = x * inv
        rows_ref[lanes, :] = unit.T.astype(BF16)
        feat_out_ref[:, lanes] = unit.astype(BF16)
        inv_ref[:, lanes] = inv

    def block(j, carry):
        at = pl.ds(pl.multiple_of(j * LANES, LANES), LANES)
        rows = rows_ref[at, :]
        acc = jnp.zeros((LANES, LANES), F32)
        for lo in range(0, COLS, CHUNK):
            z = jnp.dot(rows, cols_ref[:, lo : lo + CHUNK], preferred_element_type=F32)
            e = jnp.exp2(z * STUDENT_SCALE)
            for i in range(0, CHUNK, LANES):
                acc += e[:, i : i + LANES]
        sum_ref[pl.ds(j, 1), :] = lane_major(acc)
        return carry

    lax.fori_loop(0, ROW_TILES, block, 0)


def last_row_kernel(exp_ref, rows_ref, cols_ref, got_ref, total_ref, out_ref, scale_ref, sum_ref, cross_ref):
    scale_ref[...] = col_scale_of(got_ref)

    def block(j, carry):
        at = pl.ds(pl.multiple_of(j * LANES, LANES), LANES)
        rows = rows_ref[at, :]
        acc = jnp.zeros((LANES, LANES), F32)
        cross = jnp.zeros((LANES, LANES), F32)
        for lo in range(0, COLS, CHUNK):
            z = jnp.dot(rows, cols_ref[:, lo : lo + CHUNK], preferred_element_type=F32)
            for i in range(lo // LANES, (lo + CHUNK) // LANES):
                weighted = exp_ref[at, LANES * i : LANES * (i + 1)] * scale_ref[i : i + 1, :]
                acc += weighted
                cross += weighted * z[:, LANES * i - lo : LANES * (i + 1) - lo]
        sum_ref[pl.ds(j, 1), :] = lane_major(acc)
        cross_ref[pl.ds(j, 1), :] = lane_major(cross)
        return carry

    lax.fori_loop(0, ROW_TILES, block, 0)
    put_rows(out_ref, sum_ref[...])
    put_rows(out_ref, cross_ref[...] / 0.1, ROW_TILES)
    put_rows(out_ref, total_ref[...], 2 * ROW_TILES)


def grad_kernel(
    core_ref, exp_ref, rows_ref, feat_ref, cols_ref, got_ref, scale_ref, raw_feat_ref, feat_inv_ref, raw_cols_ref, cols_inv_ref,
    feat_out_ref, own_ref, other_ref, grad_ref, row_ref, total_ref, col_ref, part_ref,
):
    got = jnp.sum(got_ref[...], axis=0)
    sums, cross, totals = got[:ROW_TILES], got[ROW_TILES : 2 * ROW_TILES], got[2 * ROW_TILES :]
    local_loss = jnp.sum(jnp.log(totals) - cross / sums)
    row_ref[...] = PROTOS / sums
    total_ref[...] = PROTOS / totals
    col_ref[...] = scale_ref[...]

    def block(j, carry):
        at = pl.ds(pl.multiple_of(j * LANES, LANES), LANES)
        rows = rows_ref[at, :]
        target_rows = sublane_major(row_ref[pl.ds(j, 1), :])
        soft_rows = sublane_major(total_ref[pl.ds(j, 1), :])
        for lo in range(0, COLS, CHUNK):
            z = jnp.dot(rows, cols_ref[:, lo : lo + CHUNK], preferred_element_type=F32)
            e = jnp.exp2(z * STUDENT_SCALE)
            for i in range(lo // LANES, (lo + CHUNK) // LANES):
                lanes = slice(LANES * i, LANES * (i + 1))
                target = exp_ref[at, lanes] * col_ref[i : i + 1, :] * target_rows
                soft = e[:, LANES * i - lo : LANES * (i + 1) - lo] * soft_rows
                grad_ref[at, lanes] = (soft - target).astype(BF16)
        return carry

    lax.fori_loop(0, ROW_TILES, block, 0)

    for lo in range(0, COLS, CHUNK):
        lanes = slice(lo, lo + CHUNK)
        part = jnp.dot(feat_ref[...], grad_ref[:, lanes], preferred_element_type=F32)
        unit = raw_cols_ref[:, lanes].astype(F32) * cols_inv_ref[:, lanes]
        part = part - unit * jnp.sum(unit * part, axis=0, keepdims=True)
        part_ref[:, :, :, lanes] = part.reshape(BATCH // 2, 2, D // BATCH, CHUNK)
    core = core_ref[0]
    loss_row = jnp.full((D // BATCH, LANES), local_loss, F32)
    for peer in range(BATCH // 2):
        own_ref[peer, :, :COLS] = part_ref[peer, core]
        other_ref[peer, :, :COLS] = part_ref[peer, 1 - core]
        own_ref[peer, :, COLS:] = loss_row
        other_ref[peer, :, COLS:] = loss_row

    for half in range(2):
        lanes = slice(HALF * half, HALF * (half + 1))
        part = lax.dot_general(
            cols_ref[...], grad_ref[lanes, :], (((1,), (1,)), ((), ())), preferred_element_type=F32
        )
        unit = raw_feat_ref[:, 8 * half : 8 * half + 8, :].astype(F32).reshape(D, HALF) * feat_inv_ref[:, lanes]
        part = part - unit * jnp.sum(unit * part, axis=0, keepdims=True)
        part_ref_half = part.reshape(PROTO, 8, HALF)
        col_part = part_ref_half
        if half == 0:
            first = col_part
    feat_out_ref[...] = jnp.concatenate([first, col_part], axis=1).astype(BF16)


def join_kernel(own_ref, got_ref, out_ref, low_ref):
    total = own_ref[...] + got_ref[...]
    out_ref[:, :, :COLS] = total[:, :, :COLS].astype(BF16)
    tail = total[:, :, COLS:]
    lane = lax.broadcasted_iota(jnp.int32, tail.shape, 2)
    high = tail.astype(BF16).astype(F32)
    middle = (tail - high).astype(BF16).astype(F32)
    low = tail - high - middle
    out_ref[:, :, COLS:] = jnp.where(lane == 0, high, jnp.where(lane == 1, middle, low)).astype(BF16)


def proto_sum_kernel(got_ref, out_ref, loss_ref):
    total = jnp.sum(got_ref[...].astype(F32), axis=0)
    out_ref[...] = total[:, :COLS]
    tail = total[:, COLS:]
    loss_ref[...] = (tail[0:1, 0:1] + tail[0:1, 1:2] + tail[0:1, 2:3]) / CROPS


def feat_sum_kernel(got_ref, out_ref):
    total = jnp.sum(got_ref[...].astype(F32), axis=0)
    out_ref[:, :HALF] = total[:8]
    out_ref[:, HALF:] = total[8:]


def per_device(student_feat, teacher_feat, student_proto, teacher_proto):
    core = lax.rem(lax.axis_index("batch"), 2).astype(jnp.int32).reshape(1)
    swap = [(i, i ^ 1) for i in range(BATCH)]
    z_groups = [list(range(c, BATCH, 2)) for c in range(2)]

    def over_batch(array):
        return lax.all_to_all(array, "batch", 0, 0)

    def over_proto(array):
        return lax.all_to_all(array, "proto", 0, 0)

    packed = shape((PROTO, 16, HALF), BF16)
    row_shape, col_shape = shape((PROTO, ROW_TILES, LANES)), shape((BATCH, COL_TILES, LANES))
    (send_t,) = call(pack_kernel, [packed], [teacher_feat.T], name="pack_teacher")
    (send_s,) = call(pack_kernel, [packed], [student_feat.T], name="pack_student")
    teach = over_proto(send_t)
    stud = over_proto(send_s)
    unit_out = [shape((D, COLS), BF16), shape((1, COLS))]
    teacher_cols, _ = call(unit_cols_kernel, unit_out, [teacher_proto], name="unit_teacher_cols")
    proto_round, proto_inv = call(unit_cols_kernel, unit_out, [student_proto], name="unit_student_cols")

    teacher_exp, send = call(
        teacher_kernel,
        [pinned((ROWS, COLS)), col_shape],
        [teach, teacher_cols],
        [pltpu.VMEM((ROWS, D), BF16), pltpu.VMEM((8, COLS), F32)],
        name="teacher_exp",
    )
    rows_round, feat_round, feat_inv, exp_sum = call(
        student_kernel,
        [shape((ROWS, D), BF16), shape((D, ROWS), BF16), shape((1, ROWS)), shape((ROW_TILES, LANES))],
        [stud, proto_round],
        name="student_exp",
    )
    scale_shape = shape((COL_TILES, LANES))
    for sweep in range(SWEEPS - 1):
        got = over_batch(send)
        send, _ = call(
            row_pass_kernel,
            [row_shape, scale_shape],
            [pin(teacher_exp), got],
            [pltpu.VMEM((ROW_TILES, LANES), F32)],
            name="row_pass",
        )
        got = over_proto(send)
        (send,) = call(
            col_pass_kernel,
            [col_shape],
            [pin(teacher_exp), got],
            [pltpu.VMEM((ROW_TILES, LANES), F32), pltpu.VMEM((8, COLS), F32)],
            name="col_pass",
        )
    got = over_batch(send)
    send, col_scale = call(
        last_row_kernel,
        [shape((PROTO, 3 * ROW_TILES, LANES)), scale_shape],
        [pin(teacher_exp), rows_round, proto_round, got, exp_sum],
        [pltpu.VMEM((ROW_TILES, LANES), F32), pltpu.VMEM((ROW_TILES, LANES), F32)],
        name="last_row_pass",
    )
    got = over_proto(send)
    half_shape = shape((BATCH // 2, D // BATCH, COLS + LANES))
    feat_part, own, other = call(
        grad_kernel,
        [packed, half_shape, half_shape],
        [core, pin(teacher_exp), rows_round, feat_round, proto_round, got, col_scale, stud, feat_inv, student_proto, proto_inv],
        [
            pltpu.VMEM((ROWS, COLS), BF16),
            pltpu.VMEM((ROW_TILES, LANES), F32),
            pltpu.VMEM((ROW_TILES, LANES), F32),
            pltpu.VMEM((COL_TILES, LANES), F32),
            pltpu.VMEM((BATCH // 2, 2, D // BATCH, COLS), F32),
        ],
        scalars=1,
        name="grads",
    )
    arrived = lax.ppermute(other, "batch", swap)
    (joined,) = call(
        functools.partial(join_kernel, low_ref=None),
        [shape((BATCH // 2, D // BATCH, COLS + LANES), BF16)],
        [own, arrived],
        name="join_cores",
    )
    feat_got = over_proto(feat_part)
    proto_got = lax.all_to_all(joined, "batch", 0, 0, axis_index_groups=z_groups)
    (feat_out,) = call(feat_sum_kernel, [shape((8, ROWS))], [feat_got], name="feat_sum")
    proto_out, loss = call(
        proto_sum_kernel, [shape((D // BATCH, COLS)), shape((1, 1))], [proto_got], name="proto_sum"
    )
    return (loss.reshape(()), feat_out.T, proto_out)


def solution(mesh):
    placed = (P("batch", "proto"), P("batch", "proto"), P(None, "proto"), P(None, "proto"))
    return jax.shard_map(
        per_device,
        mesh=mesh,
        in_specs=placed,
        out_specs=(P(), P("batch", "proto"), P("batch", "proto")),
        check_vma=False,
    )
```

time: 828 us -> 223 us (0.27)
  the two profiles are of different devices: /device:TPU:1 before, /device:TPU:8 now
where the time goes in v1:
time: 223 us; the launch traced here: 222 us
  waiting for transfers between devices  91 us (41%)
  blocking collectives  45.6 us (20%)
  starting transfers between devices  37.6 us (17%)
  Pallas kernels  29.1 us (13%)
  local copies, waits for them, and re-layouts  17.9 us (8%)
    all_to_all x5, waiting for transfers between devices, over_proto(): return lax.all_to_all(array, 'proto', 0, 0)  71 us
    all_to_all x2, blocking collectives, over_batch(): return lax.all_to_all(array, 'batch', 0, 0)  30.3 us
    pallas_call x15, Pallas kernels, call(): pl.pallas_call(body, out_shape=outs, in_specs=[SM] * scalars + [VM] * (le...  29.1 us
    all_to_all x5, starting transfers between devices, over_proto(): return lax.all_to_all(array, 'proto', 0, 0)  28.6 us
    unnamed x32, local copies, waits for them, and re-layouts  17.9 us
    all_to_all x1, waiting for transfers between devices, per_device(): lax.all_to_all(joined, 'batch', 0, 0, axis_index_groups=z_groups)  16.6 us
    all_to_all x1, blocking collectives, over_proto(): return lax.all_to_all(array, 'proto', 0, 0)  15.4 us
  transfers between devices with their start and end apart: 8, of which 7 were waited for; matrix products, arithmetic and copies ran while one was open for 0% of the time, Pallas kernels for 4%

profile of v1, /device:TPU:8, one launch (start us, length us, event | category | flops | bytes accessed | tf_op | source)
XLA Modules:
  0.0 222.1 jit_solution(3587613353014023222)
XLA Ops:
  2.3 10.2 %all-to-all-start = ((bf16[32,16,512]{2,1,0:T(8,128)(2,1)}), bf16[32,16,512]{2,1,0:T(8,128)(2,1)S(1)}, u32[]{:S(2)}, u32[]{:S(2)}) async-start(bf16[32,16,512]{2,1,0:T(8,128)(2,1)} %pack_teacher.1), calls=%async_computation | async-start | bytes 1048576 | tf_op jit(solution)/shard_map/all_to_all | solution.py:288
  13.4 16.7 %all-to-all-done.feat_ref = bf16[32,16,512]{2,1,0:T(8,128)(2,1)S(1)} async-done(((bf16[32,16,512]{2,1,0:T(8,128)(2,1)}), bf16[32,16,512]{2,1,0:T(8,128)(2,1)S(1)}, u32[]{:S(2)}, u32[]{:S(2)}) %all-to-all-start) | async-done | bytes 524320 | tf_op jit(solution)/shard_map/all_to_all | solution.py:288
  30.1 2.9 %teacher_exp.1 = (f32[1024,2048]{1,0:T(8,128)S(1)}, f32[16,16,128]{2,1,0:T(8,128)S(1)}) custom-call(bf16[32,16,512]{2,1,0:T(8,128)(2,1)S(1)} %all-to-all-done.feat_ref, bf16[256,2048]{1,0:T(8,128)(2,1)S(1)} %get-tuple-element.21.cols_ref), custom_call_target="tpu_custom_call" | custom-call | tf_op jit(solution)/shard_map/teacher_exp/pallas_call | solution.py:41
  33.0 19.0 %all_to_all.50.got_ref = f32[16,16,128]{2,1,0:T(8,128)S(1)} all-to-all(f32[16,16,128]{2,1,0:T(8,128)S(1)} %get-tuple-element.26), channel_id=1, replica_groups=mesh['batch'=16,'proto'=32] {'batch'}, dimensions={0} | all-to-all | bytes 262144 | tf_op jit(solution)/shard_map/all_to_all | solution.py:285
  53.7 15.4 %all_to_all.51.got_ref = f32[32,8,128]{2,1,0:T(8,128)S(1)} all-to-all(f32[32,8,128]{2,1,0:T(8,128)S(1)} %get-tuple-element.27), channel_id=1, replica_groups=mesh['batch'=16,'proto'=32] {'proto'}, dimensions={0} | all-to-all | bytes 262144 | tf_op jit(solution)/shard_map/all_to_all | solution.py:288
  70.2 11.3 %all_to_all.52.got_ref = f32[16,16,128]{2,1,0:T(8,128)S(1)} all-to-all(f32[16,16,128]{2,1,0:T(8,128)S(1)} %col_pass.2), channel_id=1, replica_groups=mesh['batch'=16,'proto'=32] {'batch'}, dimensions={0} | all-to-all | bytes 262144 | tf_op jit(solution)/shard_map/all_to_all | solution.py:285
  83.5 4.3 %all-to-all-start.5 = ((f32[32,8,128]{2,1,0:T(8,128)}), f32[32,8,128]{2,1,0:T(8,128)S(1)}, u32[]{:S(2)}, u32[]{:S(2)}) async-start(f32[32,8,128]{2,1,0:T(8,128)} %get-tuple-element.28), calls=%async_computation.5 | async-start | bytes 262144 | tf_op jit(solution)/shard_map/all_to_all | solution.py:288
  88.7 9.9 %all-to-all-done.5.got_ref = f32[32,8,128]{2,1,0:T(8,128)S(1)} async-done(((f32[32,8,128]{2,1,0:T(8,128)}), f32[32,8,128]{2,1,0:T(8,128)S(1)}, u32[]{:S(2)}, u32[]{:S(2)}) %all-to-all-start.5) | async-done | bytes 131104 | tf_op jit(solution)/shard_map/all_to_all | solution.py:288
  98.7 4.4 %all-to-all-start.1 = ((bf16[32,16,512]{2,1,0:T(8,128)(2,1)}), bf16[32,16,512]{2,1,0:T(8,128)(2,1)S(1)}, u32[]{:S(2)}, u32[]{:S(2)}) async-start(bf16[32,16,512]{2,1,0:T(8,128)(2,1)} %pack_student.1), calls=%async_computation.1 | async-start | bytes 1048576 | tf_op jit(solution)/shard_map/all_to_all | solution.py:288
  103.0 3.4 %copy-done.1 = f32[1024,2048]{1,0:T(8,128)S(1)} copy-done((f32[1024,2048]{1,0:T(8,128)S(1)}, f32[1024,2048]{1,0:T(8,128)}, u32[]{:S(2)}) %copy-start.1) | copy-done | bytes 8388632
  108.3 12.5 %all-to-all-done.1.feat_ref.raw_feat_ref = bf16[32,16,512]{2,1,0:T(8,128)(2,1)S(1)} async-done(((bf16[32,16,512]{2,1,0:T(8,128)(2,1)}), bf16[32,16,512]{2,1,0:T(8,128)(2,1)S(1)}, u32[]{:S(2)}, u32[]{:S(2)}) %all-to-all-start.1) | async-done | bytes 524320 | tf_op jit(solution)/shard_map/all_to_all | solution.py:288
  120.8 3.5 %all-to-all-start.6 = ((f32[16,16,128]{2,1,0:T(8,128)}), f32[16,16,128]{2,1,0:T(8,128)S(1)}, u32[]{:S(2)}, u32[]{:S(2)}) async-start(f32[16,16,128]{2,1,0:T(8,128)} %col_pass.3), calls=%async_computation.6 | async-start | bytes 262144 | tf_op jit(solution)/shard_map/all_to_all | solution.py:285
  124.7 3.5 %student_exp.1 = (bf16[1024,256]{1,0:T(8,128)(2,1)S(1)}, bf16[256,1024]{1,0:T(8,128)(2,1)S(1)}, f32[1,1024]{1,0:T(1,128)S(1)}, f32[8,128]{1,0:T(8,128)S(1)}) custom-call(bf16[32,16,512]{2,1,0:T(8,128)(2,1)S(1)} %all-to-all-done.1.feat_ref.raw_feat_ref, bf16[256,2048]{1,0:T(8,128)(2,1)S(1)} %get-tuple-element.23.cols_ref), custom_call_target="tpu_custom_call" | custom-call | tf_op jit(solution)/shard_map/student_exp/pallas_call | solution.py:41
  129.6 3.4 %all-to-all-done.6.got_ref = f32[16,16,128]{2,1,0:T(8,128)S(1)} async-done(((f32[16,16,128]{2,1,0:T(8,128)}), f32[16,16,128]{2,1,0:T(8,128)S(1)}, u32[]{:S(2)}, u32[]{:S(2)}) %all-to-all-start.6) | async-done | bytes 131104 | tf_op jit(solution)/shard_map/all_to_all | solution.py:285
  133.0 3.4 %copy-done.2 = f32[1024,2048]{1,0:T(8,128)S(1)} copy-done((f32[1024,2048]{1,0:T(8,128)S(1)}, f32[1024,2048]{1,0:T(8,128)}, u32[]{:S(2)}) %copy-start.2) | copy-done | bytes 8388632
  136.4 3.3 %last_row_pass.1 = (f32[32,24,128]{2,1,0:T(8,128)S(1)}, f32[16,128]{1,0:T(8,128)S(1)}) custom-call(f32[1024,2048]{1,0:T(8,128)S(1)} %copy-done.2, bf16[1024,256]{1,0:T(8,128)(2,1)S(1)} %get-tuple-element.24.rows_ref, bf16[256,2048]{1,0:T(8,128)(2,1)S(1)} %get-tuple-element.23.cols_ref, f32[16,16,128]{2,1,0:T(8,128)S(1)} %all-to-all-done.6.got_ref, ...), custom_call_target="tpu_custom_call" | custom-call | tf_op jit(solution)/shard_map/last_row_pass/pallas_call | solution.py:41
  140.5 4.8 %all-to-all-start.7 = ((f32[32,24,128]{2,1,0:T(8,128)}), f32[32,24,128]{2,1,0:T(8,128)S(1)}, u32[]{:S(2)}, u32[]{:S(2)}) async-start(f32[32,24,128]{2,1,0:T(8,128)} %copy-done.11), calls=%async_computation.7 | async-start | bytes 786432 | tf_op jit(solution)/shard_map/all_to_all | solution.py:288
  145.4 15.7 %all-to-all-done.7.got_ref = f32[32,24,128]{2,1,0:T(8,128)S(1)} async-done(((f32[32,24,128]{2,1,0:T(8,128)}), f32[32,24,128]{2,1,0:T(8,128)S(1)}, u32[]{:S(2)}, u32[]{:S(2)}) %all-to-all-start.7) | async-done | bytes 393248 | tf_op jit(solution)/shard_map/all_to_all | solution.py:288
  161.1 3.4 %copy-done.3 = f32[1024,2048]{1,0:T(8,128)S(1)} copy-done((f32[1024,2048]{1,0:T(8,128)S(1)}, f32[1024,2048]{1,0:T(8,128)}, u32[]{:S(2)}) %copy-start.3) | copy-done | bytes 8388632
  166.2 7.3 %grads.1 = (bf16[32,16,512]{2,1,0:T(8,128)(2,1)S(1)}, f32[8,16,2176]{2,1,0:T(8,128)S(1)}, f32[8,16,2176]{2,1,0:T(8,128)}) custom-call(s32[1]{0:T(128)} %bitcast.core_ref, f32[1024,2048]{1,0:T(8,128)S(1)} %copy-done.3, bf16[1024,256]{1,0:T(8,128)(2,1)S(1)} %get-tuple-element.24.rows_ref, bf16[256,1024]{1,0:T(8,128)(2,1)S(1)} %copy-done.9, ...), custom_call_target="tpu_custom_call" | custom-call | tf_op jit(solution)/shard_map/grads/pallas_call | solution.py:41
  177.3 4.9 %all-to-all-start.9 = ((bf16[32,16,512]{2,1,0:T(8,128)(2,1)}), bf16[32,16,512]{2,1,0:T(8,128)(2,1)S(1)}, u32[]{:S(2)}, u32[]{:S(2)}) async-start(bf16[32,16,512]{2,1,0:T(8,128)(2,1)} %copy-done.10), calls=%async_computation.9 | async-start | bytes 1048576 | tf_op jit(solution)/shard_map/all_to_all | solution.py:288
  184.4 16.1 %all-to-all-done.9.got_ref = bf16[32,16,512]{2,1,0:T(8,128)(2,1)S(1)} async-done(((bf16[32,16,512]{2,1,0:T(8,128)(2,1)}), bf16[32,16,512]{2,1,0:T(8,128)(2,1)S(1)}, u32[]{:S(2)}, u32[]{:S(2)}) %all-to-all-start.9) | async-done | bytes 524320 | tf_op jit(solution)/shard_map/all_to_all | solution.py:288
  200.5 3.5 %all-to-all-start.8 = ((bf16[8,16,2176]{2,1,0:T(8,128)(2,1)}), bf16[8,16,2176]{2,1,0:T(8,128)(2,1)S(1)}, u32[]{:S(2)}, u32[]{:S(2)}) async-start(bf16[8,16,2176]{2,1,0:T(8,128)(2,1)} %join_cores.1), calls=%async_computation.8 | async-start | bytes 1114112 | tf_op jit(solution)/shard_map/all_to_all | solution.py:363
  204.8 16.6 %all-to-all-done.8.got_ref = bf16[8,16,2176]{2,1,0:T(8,128)(2,1)S(1)} async-done(((bf16[8,16,2176]{2,1,0:T(8,128)(2,1)}), bf16[8,16,2176]{2,1,0:T(8,128)(2,1)S(1)}, u32[]{:S(2)}, u32[]{:S(2)}) %all-to-all-start.8) | async-done | bytes 557088 | tf_op jit(solution)/shard_map/all_to_all | solution.py:363
  (42 shorter events, 21.8 us)
Async XLA Ops:
  0.6 11.8 %copy-start.7 = (bf16[256,2048]{1,0:T(8,128)(2,1)S(1)}, bf16[256,2048]{1,0:T(8,128)(2,1)}, u32[]{:S(2)}) copy-start(bf16[256,2048]{1,0:T(8,128)(2,1)} %raw_ref.2) | copy-start | bytes 3145732
  0.6 0.8 copy-start.12
  2.3 27.8 %all-to-all-start = ((bf16[32,16,512]{2,1,0:T(8,128)(2,1)}), bf16[32,16,512]{2,1,0:T(8,128)(2,1)S(1)}, u32[]{:S(2)}, u32[]{:S(2)}) async-start(bf16[32,16,512]{2,1,0:T(8,128)(2,1)} %pack_teacher.1), calls=%async_computation | async-start | bytes 1048576 | tf_op jit(solution)/shard_map/all_to_all | solution.py:288
  33.0 48.6 %copy-start = (f32[1024,2048]{1,0:T(8,128)}, f32[1024,2048]{1,0:T(8,128)S(1)}, u32[]{:S(2)}) copy-start(f32[1024,2048]{1,0:T(8,128)S(1)} %get-tuple-element.22.exp_ref) | copy-start | bytes 25165828
  81.6 6.3 %copy-start.13 = (bf16[1024,8]{0,1:T(8,128)(2,1)S(1)}, bf16[1024,8]{0,1:T(8,128)(2,1)}, u32[]{:S(2)}) copy-start(bf16[1024,8]{0,1:T(8,128)(2,1)} %param.4) | copy-start | bytes 49156
  83.5 15.2 %all-to-all-start.5 = ((f32[32,8,128]{2,1,0:T(8,128)}), f32[32,8,128]{2,1,0:T(8,128)S(1)}, u32[]{:S(2)}, u32[]{:S(2)}) async-start(f32[32,8,128]{2,1,0:T(8,128)} %get-tuple-element.28), calls=%async_computation.5 | async-start | bytes 262144 | tf_op jit(solution)/shard_map/all_to_all | solution.py:288
  98.7 22.1 %all-to-all-start.1 = ((bf16[32,16,512]{2,1,0:T(8,128)(2,1)}), bf16[32,16,512]{2,1,0:T(8,128)(2,1)S(1)}, u32[]{:S(2)}, u32[]{:S(2)}) async-start(bf16[32,16,512]{2,1,0:T(8,128)(2,1)} %pack_student.1), calls=%async_computation.1 | async-start | bytes 1048576 | tf_op jit(solution)/shard_map/all_to_all | solution.py:288
  103.0 3.4 %copy-start.1 = (f32[1024,2048]{1,0:T(8,128)S(1)}, f32[1024,2048]{1,0:T(8,128)}, u32[]{:S(2)}) copy-start(f32[1024,2048]{1,0:T(8,128)} %copy-done) | copy-start | bytes 25165828
  106.4 17.9 %copy-start.4 = (bf16[256,2048]{1,0:T(8,128)(2,1)S(1)}, bf16[256,2048]{1,0:T(8,128)(2,1)}, u32[]{:S(2)}) copy-start(bf16[256,2048]{1,0:T(8,128)(2,1)} %raw_cols_ref.1) | copy-start | bytes 3145732
  120.8 12.2 %all-to-all-start.6 = ((f32[16,16,128]{2,1,0:T(8,128)}), f32[16,16,128]{2,1,0:T(8,128)S(1)}, u32[]{:S(2)}, u32[]{:S(2)}) async-start(f32[16,16,128]{2,1,0:T(8,128)} %col_pass.3), calls=%async_computation.6 | async-start | bytes 262144 | tf_op jit(solution)/shard_map/all_to_all | solution.py:285
  128.2 0.8 copy-start.8
  129.0 0.6 copy-start.14
  133.0 3.4 %copy-start.2 = (f32[1024,2048]{1,0:T(8,128)S(1)}, f32[1024,2048]{1,0:T(8,128)}, u32[]{:S(2)}) copy-start(f32[1024,2048]{1,0:T(8,128)} %copy-done) | copy-start | bytes 25165828
  139.7 0.8 copy-start.11
  140.5 20.6 %all-to-all-start.7 = ((f32[32,24,128]{2,1,0:T(8,128)}), f32[32,24,128]{2,1,0:T(8,128)S(1)}, u32[]{:S(2)}, u32[]{:S(2)}) async-start(f32[32,24,128]{2,1,0:T(8,128)} %copy-done.11), calls=%async_computation.7 | async-start | bytes 786432 | tf_op jit(solution)/shard_map/all_to_all | solution.py:288
  161.1 3.4 %copy-start.3 = (f32[1024,2048]{1,0:T(8,128)S(1)}, f32[1024,2048]{1,0:T(8,128)}, u32[]{:S(2)}) copy-start(f32[1024,2048]{1,0:T(8,128)} %copy-done) | copy-start | bytes 25165828
  164.5 1.0 copy-start.9
  165.5 0.7 copy-start.15
  173.5 1.0 copy-start.5
  174.5 0.8 copy-start.10
  175.3 6.9 %collective-permute-start = (f32[8,16,2176]{2,1,0:T(8,128)}, f32[8,16,2176]{2,1,0:T(8,128)S(1)}, u32[]{:S(2)}, u32[]{:S(2)}) collective-permute-start(f32[8,16,2176]{2,1,0:T(8,128)} %get-tuple-element.35), channel_id=1, source_target_pairs={{0,32},{32,0},{64,96},{96,64},{128,160},{160,128},{192,224},{224,1... | collective-permute-start | bytes 3342344 | tf_op jit(solution)/shard_map/ppermute | solution.py:355
  177.3 23.2 %all-to-all-start.9 = ((bf16[32,16,512]{2,1,0:T(8,128)(2,1)}), bf16[32,16,512]{2,1,0:T(8,128)(2,1)S(1)}, u32[]{:S(2)}, u32[]{:S(2)}) async-start(bf16[32,16,512]{2,1,0:T(8,128)(2,1)} %copy-done.10), calls=%async_computation.9 | async-start | bytes 1048576 | tf_op jit(solution)/shard_map/all_to_all | solution.py:288
  182.2 1.2 copy-start.6
  200.5 20.8 %all-to-all-start.8 = ((bf16[8,16,2176]{2,1,0:T(8,128)(2,1)}), bf16[8,16,2176]{2,1,0:T(8,128)(2,1)S(1)}, u32[]{:S(2)}, u32[]{:S(2)}) async-start(bf16[8,16,2176]{2,1,0:T(8,128)(2,1)} %join_cores.1), calls=%async_computation.8 | async-start | bytes 1114112 | tf_op jit(solution)/shard_map/all_to_all | solution.py:363

commit v2 on v1

v2 whole, which is shorter than its diff:
```python
import jax
import jax.numpy as jnp
from jax import lax
from jax.experimental import pallas as pl
from jax.experimental.pallas import tpu as pltpu
from jax.sharding import PartitionSpec as P

F32, BF16 = jnp.float32, jnp.bfloat16
SWEEPS = 3
LOG2E = 1.4426950408889634
STUDENT_SCALE = LOG2E / 0.1
TEACHER_SCALE = LOG2E / 0.07
D, ROWS, COLS = 256, 1024, 2048
LANES = 128
ROW_TILES, COL_TILES = ROWS // LANES, COLS // LANES
PROTO, BATCH = 32, 16
PAIRS = BATCH // 4
CROPS, PROTOS = ROWS * BATCH, COLS * PROTO
HALF = ROWS // 2
CHUNK = 512
MIB = 1024 * 1024

VM = pl.BlockSpec(memory_space=pltpu.VMEM)
SM = pl.BlockSpec(memory_space=pltpu.SMEM)
ANY = pl.BlockSpec(memory_space=pl.ANY)


def shape(dims, dtype=F32):
    return jax.ShapeDtypeStruct(dims, dtype)


def pinned(dims, dtype=F32):
    return pltpu.VMEM(dims, dtype)


def pin(array):
    return pltpu.with_memory_space_constraint(array, pltpu.VMEM)


def stay(array):
    return pltpu.with_memory_space_constraint(array, pltpu.HBM)


def call(body, outs, args, scratch=(), specs=None, name=None, vmem=12, aliases=None):
    return pl.pallas_call(
        body,
        out_shape=outs,
        in_specs=specs or [VM] * len(args),
        out_specs=[VM] * len(outs),
        scratch_shapes=list(scratch),
        compiler_params=pltpu.CompilerParams(vmem_limit_bytes=vmem * MIB),
        input_output_aliases=aliases or {},
        name=name,
    )(*args)


def lane_major(partial_ref, out_ref):
    for j in range(ROW_TILES):
        tile = partial_ref[LANES * j : LANES * (j + 1), :]
        out_ref[j : j + 1, :] = jnp.sum(tile.T, axis=0, keepdims=True)


def sublane_major(values, out_ref):
    for j in range(ROW_TILES):
        out_ref[LANES * j : LANES * (j + 1), :] = jnp.broadcast_to(values[j : j + 1, :], (LANES, LANES)).T


def halves(x):
    return jnp.concatenate([x[:, :HALF], x[:, HALF:]], axis=0)


def col_fetches(source_ref, raw_ref, sems):
    lanes = [pl.ds(lo, CHUNK) for lo in range(0, COLS, CHUNK)]
    return [
        pltpu.make_async_copy(source_ref.at[:, here], raw_ref.at[:, here], sems.at[i]) for i, here in enumerate(lanes)
    ]


def unit_cols(fetches, raw_ref, round_ref, inv_ref=None):
    for fetch, lo in zip(fetches, range(0, COLS, CHUNK)):
        fetch.wait()
        x = raw_ref[:, lo : lo + CHUNK].astype(F32)
        inv = lax.rsqrt(jnp.sum(x * x, axis=0, keepdims=True) + 1e-06)
        if inv_ref is not None:
            inv_ref[:, lo : lo + CHUNK] = inv
        round_ref[:, lo : lo + CHUNK] = (x * inv).astype(BF16)


def unit_rows(x):
    return x * lax.rsqrt(jnp.sum(x * x, axis=0, keepdims=True) + 1e-06)


def prepare_kernel(place_ref, teach_ref, stud_ref, teach_out, stud_out, place_out):
    both = halves(teach_ref[...].astype(F32)).astype(BF16)
    for peer in range(PROTO):
        teach_out[peer] = both
    stud_out[...] = stud_ref[...].astype(F32)
    place_out[0] = place_ref[0]


def put(out_ref, value, rows=slice(None), lanes=slice(None)):
    for peer in range(out_ref.shape[0]):
        out_ref[peer, rows, lanes] = value


def col_rows(acc_ref):
    total = jnp.sum(acc_ref[...], axis=0, keepdims=True)
    return jnp.concatenate([total[:, LANES * i : LANES * (i + 1)] for i in range(COL_TILES)], axis=0)


def row_block(j):
    return pl.ds(pl.multiple_of(j * LANES, LANES), LANES)


def teacher_kernel(feat_ref, source_ref, exp_ref, out_ref, rows_ref, raw_cols_ref, cols_ref, acc_ref, sems):
    fetches = col_fetches(source_ref, raw_cols_ref, sems)
    for fetch in fetches:
        fetch.start()
    for half in range(2):
        x = feat_ref[:, 8 * half : 8 * half + 8, :].astype(F32).reshape(D, HALF)
        rows_ref[HALF * half : HALF * (half + 1), :] = unit_rows(x).T.astype(BF16)
    unit_cols(fetches, raw_cols_ref, cols_ref)
    acc_ref[...] = jnp.zeros_like(acc_ref)

    def block(j, carry):
        at = row_block(j)
        rows = rows_ref[at, :]
        for lo in range(0, COLS, CHUNK):
            z = jnp.dot(rows, cols_ref[:, lo : lo + CHUNK], preferred_element_type=F32)
            e = jnp.exp2(z * TEACHER_SCALE)
            exp_ref[at, lo : lo + CHUNK] = e
            acc_ref[:, lo : lo + CHUNK] += jnp.sum(e.reshape(LANES // 8, 8, CHUNK), axis=0)
        return carry

    lax.fori_loop(0, ROW_TILES, block, 0)
    put(out_ref, col_rows(acc_ref).astype(out_ref.dtype))


def col_scale_of(got_ref):
    return 1.0 / (PROTOS * jnp.sum(got_ref[...].astype(F32), axis=0))


def row_sums(exp_ref, scale_ref, part_ref, sum_ref):
    def block(j, carry):
        at = row_block(j)
        acc = jnp.zeros((LANES, LANES), F32)
        for i in range(COL_TILES):
            acc += exp_ref[at, LANES * i : LANES * (i + 1)] * scale_ref[i : i + 1, :]
        part_ref[at, :] = acc
        return carry

    lax.fori_loop(0, ROW_TILES, block, 0)
    lane_major(part_ref, sum_ref)


def row_kernel(exp_ref, got_ref, out_ref, scale_ref, part_ref, sum_ref):
    scale_ref[...] = col_scale_of(got_ref)
    row_sums(exp_ref, scale_ref, part_ref, sum_ref)
    put(out_ref, sum_ref[...])


def col_kernel(exp_ref, got_ref, out_ref, rows_ref, acc_ref):
    sublane_major(1.0 / (CROPS * jnp.sum(got_ref[...], axis=0)), rows_ref)
    acc_ref[...] = jnp.zeros_like(acc_ref)

    def block(j, carry):
        at = row_block(j)
        r = rows_ref[at, :]
        for i in range(COL_TILES):
            lanes = slice(LANES * i, LANES * (i + 1))
            acc_ref[:, lanes] += jnp.sum((exp_ref[at, lanes] * r).reshape(LANES // 8, 8, LANES), axis=0)
        return carry

    lax.fori_loop(0, ROW_TILES, block, 0)
    put(out_ref, col_rows(acc_ref).astype(out_ref.dtype))


def student_kernel(
    gathered_ref, source_ref, send_ref, exp_ref, rows_ref, raw_feat_ref, feat_out_ref, feat_inv_ref, raw_cols_ref, cols_ref,
    cols_inv_ref, sum_ref, out_ref, part_ref, feat_ref, sems, sem,
):
    fetches = col_fetches(source_ref, raw_cols_ref, sems)
    for fetch in fetches:
        fetch.start()
    fetch = pltpu.make_async_copy(gathered_ref, feat_ref, sem)
    fetch.start()
    out_ref[...] = send_ref[...]
    unit_cols(fetches, raw_cols_ref, cols_ref, cols_inv_ref)
    fetch.wait()
    for half in range(2):
        lanes = slice(HALF * half, HALF * (half + 1))
        x = feat_ref[:, lanes]
        raw_feat_ref[:, lanes] = x.astype(BF16)
        inv = lax.rsqrt(jnp.sum(x * x, axis=0, keepdims=True) + 1e-06)
        unit = x * inv
        rows_ref[lanes, :] = unit.T.astype(BF16)
        feat_out_ref[:, lanes] = unit.astype(BF16)
        feat_inv_ref[:, lanes] = inv

    def block(j, carry):
        at = row_block(j)
        rows = rows_ref[at, :]
        acc = jnp.zeros((LANES, LANES), F32)
        for lo in range(0, COLS, CHUNK):
            z = jnp.dot(rows, cols_ref[:, lo : lo + CHUNK], preferred_element_type=F32)
            e = jnp.exp2(z * STUDENT_SCALE)
            exp_ref[at, lo : lo + CHUNK] = e
            for i in range(0, CHUNK, LANES):
                acc += e[:, i : i + LANES]
        part_ref[at, :] = acc
        return carry

    lax.fori_loop(0, ROW_TILES, block, 0)
    lane_major(part_ref, sum_ref)


def last_row_kernel(
    source_ref, rows_ref, cols_ref, got_ref, total_ref, out_ref, weighted_ref, scale_ref, part_ref, cross_ref, sum_ref, sems
):
    def fetch(j):
        at = row_block(j)
        return pltpu.make_async_copy(source_ref.at[at, :], weighted_ref.at[at, :], sems.at[j])

    for j in range(ROW_TILES):
        fetch(j).start()
    scale_ref[...] = col_scale_of(got_ref)

    def block(j, carry):
        at = row_block(j)
        rows = rows_ref[at, :]
        acc = jnp.zeros((LANES, LANES), F32)
        cross = jnp.zeros((LANES, LANES), F32)
        fetch(j).wait()
        for lo in range(0, COLS, CHUNK):
            z = jnp.dot(rows, cols_ref[:, lo : lo + CHUNK], preferred_element_type=F32)
            for i in range(lo // LANES, (lo + CHUNK) // LANES):
                lanes = slice(LANES * i, LANES * (i + 1))
                weighted = weighted_ref[at, lanes] * scale_ref[i : i + 1, :]
                weighted_ref[at, lanes] = weighted
                acc += weighted
                cross += weighted * z[:, LANES * i - lo : LANES * (i + 1) - lo]
        part_ref[at, :] = acc
        cross_ref[at, :] = cross
        return carry

    lax.fori_loop(0, ROW_TILES, block, 0)
    lane_major(part_ref, sum_ref)
    put(out_ref, sum_ref[...], rows=slice(0, ROW_TILES))
    lane_major(cross_ref, sum_ref)
    put(out_ref, sum_ref[...] / 0.1, rows=slice(ROW_TILES, 2 * ROW_TILES))
    put(out_ref, total_ref[...], rows=slice(2 * ROW_TILES, 3 * ROW_TILES))


def grad_kernel(
    place_ref, weighted_ref, exp_ref, feat_ref, got_ref, raw_cols_ref, cols_inv_ref,
    grad_ref, own_ref, other_ref, target_ref, soft_ref, part_ref,
):
    got = jnp.sum(got_ref[...], axis=0)
    sums, cross, totals = got[:ROW_TILES], got[ROW_TILES : 2 * ROW_TILES], got[2 * ROW_TILES :]
    local_loss = jnp.sum(jnp.log(totals) - cross / sums)
    sublane_major(PROTOS / sums, target_ref)
    sublane_major(PROTOS / totals, soft_ref)

    def block(j, carry):
        at = row_block(j)
        target_rows, soft_rows = target_ref[at, :], soft_ref[at, :]
        for i in range(COL_TILES):
            lanes = slice(LANES * i, LANES * (i + 1))
            grad_ref[at, lanes] = (exp_ref[at, lanes] * soft_rows - weighted_ref[at, lanes] * target_rows).astype(BF16)
        return carry

    lax.fori_loop(0, ROW_TILES, block, 0)

    for lo in range(0, COLS, CHUNK):
        lanes = slice(lo, lo + CHUNK)
        part = jnp.dot(feat_ref[...], grad_ref[:, lanes], preferred_element_type=F32)
        unit = raw_cols_ref[:, lanes].astype(F32) * cols_inv_ref[:, lanes]
        part = part - unit * jnp.sum(unit * part, axis=0, keepdims=True)
        part_ref[:, :, :, :, lanes] = part.reshape(PAIRS, 2, 2, D // BATCH, CHUNK)
    core, odd = lax.rem(place_ref[0], 2), lax.rem(lax.div(place_ref[0], 2), 2)
    loss_row = jnp.full((D // BATCH, LANES), local_loss, F32)
    for away in range(2):
        parity = odd if away == 0 else 1 - odd
        for pair in range(PAIRS):
            own_ref[away, pair, :, :COLS] = part_ref[pair, parity, core]
            other_ref[away, pair, :, :COLS] = part_ref[pair, parity, 1 - core]
            own_ref[away, pair, :, COLS:] = loss_row
            other_ref[away, pair, :, COLS:] = loss_row


def feat_grad_kernel(grad_ref, cols_ref, raw_feat_ref, feat_inv_ref, out_ref):
    parts = []
    for half in range(2):
        lanes = slice(HALF * half, HALF * (half + 1))
        part = lax.dot_general(
            cols_ref[...], grad_ref[lanes, :], (((1,), (1,)), ((), ())), preferred_element_type=F32
        )
        unit = raw_feat_ref[:, lanes].astype(F32) * feat_inv_ref[:, lanes]
        part = part - unit * jnp.sum(unit * part, axis=0, keepdims=True)
        parts.append(part.reshape(PROTO, 8, HALF))
    out_ref[...] = jnp.concatenate(parts, axis=1).astype(BF16)


def join_cores_kernel(own_ref, got_ref, feat_ref, keep_ref, send_ref, feat_out_ref):
    keep_ref[...] = own_ref[0] + got_ref[0]
    send_ref[...] = own_ref[1] + got_ref[1]


def join_pairs_kernel(own_ref, got_ref, after_ref, out_ref):
    total = own_ref[...] + got_ref[...]
    out_ref[:, :, :COLS] = total[:, :, :COLS].astype(BF16)
    tail = total[:, :, COLS:]
    lane = lax.broadcasted_iota(jnp.int32, tail.shape, 2)
    high = tail.astype(BF16).astype(F32)
    middle = (tail - high).astype(BF16).astype(F32)
    low = tail - high - middle
    out_ref[:, :, COLS:] = jnp.where(lane == 0, high, jnp.where(lane == 1, middle, low)).astype(BF16)


def final_kernel(feat_ref, proto_ref, feat_out_ref, proto_out_ref, loss_ref):
    total = jnp.sum(proto_ref[...].astype(F32), axis=0)
    proto_out_ref[...] = total[:, :COLS]
    tail = total[:, COLS:]
    loss_ref[...] = (tail[0:1, 0:1] + tail[0:1, 1:2] + tail[0:1, 2:3]) / CROPS
    feat = jnp.sum(feat_ref[...].astype(F32), axis=0)
    feat_out_ref[:, :HALF] = feat[:8]
    feat_out_ref[:, HALF:] = feat[8:]


def per_device(student_feat, teacher_feat, student_proto, teacher_proto):
    place = lax.axis_index("batch").astype(jnp.int32).reshape(1)
    swap_cores = [(i, i ^ 1) for i in range(BATCH)]
    swap_pairs = [(i, i ^ 2) for i in range(BATCH)]
    quads = [list(range(first, BATCH, 4)) for first in range(4)]

    def over_batch(array):
        return lax.all_to_all(array, "batch", 0, 0)

    def over_proto(array):
        return lax.all_to_all(array, "proto", 0, 0)

    packed = shape((PROTO, 16, HALF), BF16)
    rounded = shape((D, COLS), BF16)
    rounded_rows = shape((ROWS, D), BF16)
    row_shape = shape((PROTO, ROW_TILES, LANES))
    last_shape = shape((PROTO, 3 * ROW_TILES, LANES))
    col_shape, last_col_shape = shape((BATCH, COL_TILES, LANES), BF16), shape((BATCH, COL_TILES, LANES))
    row_tile, row_part = pltpu.VMEM((ROW_TILES, LANES), F32), pltpu.VMEM((ROWS, LANES), F32)
    col_tile, col_part = pltpu.VMEM((COL_TILES, LANES), F32), pltpu.VMEM((8, COLS), F32)

    send, stud_send, place = pl.pallas_call(
        prepare_kernel,
        out_shape=[packed, shape((8, ROWS)), shape((1,), jnp.int32)],
        in_specs=[SM, VM, VM],
        out_specs=[VM, VM, SM],
        name="prepare",
    )(place, teacher_feat.T, student_feat.T)
    stud = lax.all_gather(stud_send, "proto", axis=0, tiled=True)
    teach = over_proto(send)
    teacher_exp, send = call(
        teacher_kernel,
        [pinned((ROWS, COLS)), col_shape],
        [teach, stay(teacher_proto)],
        [
            pltpu.VMEM((ROWS, D), BF16),
            pltpu.VMEM((D, COLS), BF16),
            pltpu.VMEM((D, COLS), BF16),
            col_part,
            pltpu.SemaphoreType.DMA((COLS // CHUNK,)),
        ],
        specs=[VM, ANY],
        name="teacher_exp",
    )
    for sweep in range(SWEEPS - 1):
        got = over_batch(send)
        (send,) = call(
            row_kernel, [row_shape], [pin(teacher_exp), got], [col_tile, row_part, row_tile], name="row_pass"
        )
        got = over_proto(send)
        (send,) = call(
            col_kernel,
            [col_shape if sweep + 2 < SWEEPS else last_col_shape],
            [pin(teacher_exp), got],
            [row_part, col_part],
            name="col_pass",
        )
    student_exp, rows_round, raw_feat, feat_round, feat_inv, raw_proto, proto_round, proto_inv, exp_sum, send = call(
        student_kernel,
        [
            pinned((ROWS, COLS)),
            rounded_rows,
            shape((D, ROWS), BF16),
            shape((D, ROWS), BF16),
            shape((1, ROWS)),
            rounded,
            rounded,
            shape((1, COLS)),
            shape((ROW_TILES, LANES)),
            last_col_shape,
        ],
        [stay(stud), stay(student_proto), send],
        [
            row_part,
            pltpu.VMEM((D, ROWS), F32),
            pltpu.SemaphoreType.DMA((COLS // CHUNK,)),
            pltpu.SemaphoreType.DMA,
        ],
        specs=[ANY, ANY, VM],
        name="student_exp",
    )
    got = over_batch(send)
    send, weighted = call(
        last_row_kernel,
        [last_shape, pinned((ROWS, COLS))],
        [stay(teacher_exp), rows_round, proto_round, got, exp_sum],
        [col_tile, row_part, row_part, row_tile, pltpu.SemaphoreType.DMA((ROW_TILES,))],
        specs=[ANY] + [VM] * 4,
        name="last_row_pass",
    )
    got = over_proto(send)
    half_shape = shape((2, PAIRS, D // BATCH, COLS + LANES))
    grad_logit, own, other = call(
        grad_kernel,
        [pinned((ROWS, COLS), BF16), half_shape, half_shape],
        [place, pin(weighted), pin(student_exp), feat_round, got, raw_proto, proto_inv],
        [row_part, row_part, pltpu.VMEM((PAIRS, 2, 2, D // BATCH, COLS), F32)],
        specs=[SM] + [VM] * 6,
        vmem=16,
        name="proto_grad",
    )
    arrived = lax.ppermute(other, "batch", swap_cores)
    (feat_part,) = call(
        feat_grad_kernel, [packed], [pin(grad_logit), proto_round, raw_feat, feat_inv], name="feat_grad"
    )
    pair_shape = (PAIRS, D // BATCH, COLS + LANES)
    keep, send, feat_part = pl.pallas_call(
        join_cores_kernel,
        out_shape=[shape(pair_shape), shape(pair_shape), packed],
        in_specs=[VM, VM, ANY],
        out_specs=[VM, VM, ANY],
        input_output_aliases={2: 2},
        compiler_params=pltpu.CompilerParams(vmem_limit_bytes=12 * MIB),
        name="join_cores",
    )(own, arrived, feat_part)
    feat_got = over_proto(feat_part)
    arrived = lax.ppermute(send, "batch", swap_pairs)
    (joined,) = call(join_pairs_kernel, [shape(pair_shape, BF16)], [keep, arrived, feat_got], specs=[VM, VM, ANY], name="join_pairs")
    proto_got = lax.all_to_all(joined, "batch", 0, 0, axis_index_groups=quads)
    feat_out, proto_out, loss = call(
        final_kernel,
        [shape((8, ROWS)), shape((D // BATCH, COLS)), shape((1, 1))],
        [feat_got, proto_got],
        name="final_sums",
    )
    return (loss.reshape(()), feat_out.T, proto_out)


def solution(mesh):
    placed = (P("batch", "proto"), P("batch", "proto"), P(None, "proto"), P(None, "proto"))
    return jax.shard_map(
        per_device,
        mesh=mesh,
        in_specs=placed,
        out_specs=(P(), P("batch", "proto"), P("batch", "proto")),
        check_vma=False,
    )
```

time: 223 us -> 199 us (0.89)
  blocking collectives: 45.6 us -> 132 us
  waiting for transfers between devices: 91 us -> 16.2 us
  starting transfers between devices: 37.6 us -> 9.19 us
  local copies, waits for them, and re-layouts: 17.9 us -> 0.01 us
  between operations: 0.84 us -> 14.1 us
  Pallas kernels: 29.1 us -> 26.4 us
    all_to_all x5 -> x1, waiting for transfers between devices: 71 us -> 1.93 us  [over_proto(): return lax.all_to_all(array, 'proto', 0, 0)]
    all_to_all x1 -> x4, blocking collectives: 15.4 us -> 79.7 us  [over_proto(): return lax.all_to_all(array, 'proto', 0, 0)]
    all_to_all x5 -> x1, starting transfers between devices: 28.6 us -> 4.95 us  [over_proto(): return lax.all_to_all(array, 'proto', 0, 0)]
    all_to_all x2 -> x0, waiting for transfers between devices: 20 us -> none  [the longest x1 16.6 us: per_device(): lax.all_to_all(joined, 'batch', 0, 0, axis_index_groups=z_groups)]
    unnamed x32 -> x2, local copies, waits for them, and re-layouts: 17.9 us -> 0.01 us
    ppermute x1 -> x2, waiting for transfers between devices: 0.01 us -> 14.2 us  [the longest x1 13.7 us: per_device(): arrived = lax.ppermute(send, 'batch', swap_pairs)]
    all_to_all x0 -> x1, blocking collectives: none -> 12 us  [per_device(): proto_got = lax.all_to_all(joined, 'batch', 0, 0, axis_index_groups=quads)]
    all_to_all x2 -> x3, blocking collectives: 30.3 us -> 40 us  [over_batch(): return lax.all_to_all(array, 'batch', 0, 0)]
  transfers between devices with their start and end apart: 8 -> 4, of which waited for: 7 -> 3; matrix products, arithmetic and copies ran while one was open for 0% -> 0% of each run, Pallas kernels for 4% -> 5%
where the time goes in v2:
time: 199 us; the launch traced here: 198 us
  blocking collectives  132 us (66%)
  Pallas kernels  26.4 us (13%)
  waiting for transfers between devices  16.2 us (8%)
  between operations  14.1 us (7%)
  starting transfers between devices  9.19 us (5%)
    all_to_all x4, blocking collectives, over_proto(): return lax.all_to_all(array, 'proto', 0, 0)  79.7 us
    all_to_all x3, blocking collectives, over_batch(): return lax.all_to_all(array, 'batch', 0, 0)  40 us
    pallas_call x11, Pallas kernels, call(): pl.pallas_call(body, out_shape=outs, in_specs=specs or [VM] * len(args),...  24.7 us
    ppermute x1, waiting for transfers between devices, per_device(): arrived = lax.ppermute(send, 'batch', swap_pairs)  13.7 us
    all_to_all x1, blocking collectives, per_device(): proto_got = lax.all_to_all(joined, 'batch', 0, 0, axis_index_groups=quads)  12 us
    all_to_all x1, starting transfers between devices, over_proto(): return lax.all_to_all(array, 'proto', 0, 0)  4.95 us
  transfers between devices with their start and end apart: 4, of which 3 were waited for; matrix products, arithmetic and copies ran while one was open for 0% of the time, Pallas kernels for 5%

profile of v2, /device:TPU:8, one launch (start us, length us, event | category | flops | bytes accessed | tf_op | source)
XLA Modules:
  0.0 197.6 jit_solution(8212351107414688938)
XLA Ops:
  7.2 1.6 prepare.1
  8.8 27.8 %all_to_all.45.feat_ref = bf16[32,16,512]{2,1,0:T(8,128)(2,1)S(1)} all-to-all(bf16[32,16,512]{2,1,0:T(8,128)(2,1)} %get-tuple-element.30), channel_id=1, replica_groups=mesh['batch'=16,'proto'=32] {'proto'}, dimensions={0} | all-to-all | bytes 1048576 | tf_op jit(solution)/shard_map/all_to_all | solution.py:340
  36.6 4.1 %teacher_exp.1 = (f32[1024,2048]{1,0:T(8,128)S(1)}, bf16[16,16,128]{2,1,0:T(8,128)(2,1)S(1)}) custom-call(bf16[32,16,512]{2,1,0:T(8,128)(2,1)S(1)} %all_to_all.45.feat_ref, bf16[256,2048]{1,0:T(8,128)(2,1)} %source_ref.2), custom_call_target="tpu_custom_call" | custom-call | tf_op jit(solution)/shard_map/teacher_exp/pallas_call | solution.py:45
  40.8 18.3 %all_to_all.46.got_ref = bf16[16,16,128]{2,1,0:T(8,128)(2,1)S(1)} all-to-all(bf16[16,16,128]{2,1,0:T(8,128)(2,1)S(1)} %get-tuple-element.33), channel_id=1, replica_groups=mesh['batch'=16,'proto'=32] {'batch'}, dimensions={0} | all-to-all | bytes 131072 | tf_op jit(solution)/shard_map/all_to_all | solution.py:337
  59.1 0.9 row_pass.2
  60.0 14.9 %all_to_all.47.got_ref = f32[32,8,128]{2,1,0:T(8,128)S(1)} all-to-all(f32[32,8,128]{2,1,0:T(8,128)S(1)} %row_pass.2), channel_id=1, replica_groups=mesh['batch'=16,'proto'=32] {'proto'}, dimensions={0} | all-to-all | bytes 262144 | tf_op jit(solution)/shard_map/all_to_all | solution.py:340
  74.8 0.9 col_pass.2
  75.7 10.4 %all_to_all.48.got_ref = bf16[16,16,128]{2,1,0:T(8,128)(2,1)S(1)} all-to-all(bf16[16,16,128]{2,1,0:T(8,128)(2,1)S(1)} %col_pass.2), channel_id=1, replica_groups=mesh['batch'=16,'proto'=32] {'batch'}, dimensions={0} | all-to-all | bytes 131072 | tf_op jit(solution)/shard_map/all_to_all | solution.py:337
  86.1 0.9 row_pass.3
  87.0 14.6 %all_to_all.49.got_ref = f32[32,8,128]{2,1,0:T(8,128)S(1)} all-to-all(f32[32,8,128]{2,1,0:T(8,128)S(1)} %row_pass.3), channel_id=1, replica_groups=mesh['batch'=16,'proto'=32] {'proto'}, dimensions={0} | all-to-all | bytes 262144 | tf_op jit(solution)/shard_map/all_to_all | solution.py:340
  101.6 0.9 col_pass.3.send_ref
  102.5 4.9 %student_exp.1 = (f32[1024,2048]{1,0:T(8,128)S(1)}, bf16[1024,256]{1,0:T(8,128)(2,1)S(1)}, bf16[256,1024]{1,0:T(8,128)(2,1)S(1)}, bf16[256,1024]{1,0:T(8,128)(2,...) custom-call(f32[256,1024]{1,0:T(8,128)} %all-gather.2.cloned.1.call-, ...), custom_call_target="tpu_custom_call" | custom-call | tf_op jit(solution)/shard_map/student_exp/pallas_call | solution.py:45
  107.4 11.3 %all_to_all.50.got_ref = f32[16,16,128]{2,1,0:T(8,128)S(1)} all-to-all(f32[16,16,128]{2,1,0:T(8,128)S(1)} %get-tuple-element.36), channel_id=1, replica_groups=mesh['batch'=16,'proto'=32] {'batch'}, dimensions={0} | all-to-all | bytes 262144 | tf_op jit(solution)/shard_map/all_to_all | solution.py:337
  118.7 4.4 %last_row_pass.1 = (f32[32,24,128]{2,1,0:T(8,128)S(1)}, f32[1024,2048]{1,0:T(8,128)S(1)}) custom-call(f32[1024,2048]{1,0:T(8,128)} %copy-done, bf16[1024,256]{1,0:T(8,128)(2,1)S(1)} %get-tuple-element.34.rows_ref, bf16[256,2048]{1,0:T(8,128)(2,1)S(1)} %get-tuple-element.35.cols_ref, f32[16,16,128]{2,1,0:T(8,128)S(1)} %all_to_all.50.got_ref, ...), custom_call_target="tpu_custom_call" | custom-call | tf_op jit(solution)/shard_map/last_row_pass/pallas_call | solution.py:45
  123.1 22.5 %all_to_all.51.got_ref = f32[32,24,128]{2,1,0:T(8,128)S(1)} all-to-all(f32[32,24,128]{2,1,0:T(8,128)S(1)} %get-tuple-element.41), channel_id=1, replica_groups=mesh['batch'=16,'proto'=32] {'proto'}, dimensions={0} | all-to-all | bytes 786432 | tf_op jit(solution)/shard_map/all_to_all | solution.py:340
  145.6 4.6 %proto_grad.1 = (bf16[1024,2048]{1,0:T(8,128)(2,1)S(1)}, f32[2,4,16,2176]{3,2,1,0:T(8,128)S(1)}, f32[2,4,16,2176]{3,2,1,0:T(8,128)S(1)}) custom-call(s32[1]{0:T(128)} %get-tuple-element.29.place_ref, f32[1024,2048]{1,0:T(8,128)S(1)} %get-tuple-element.38.weighted_ref, f32[1024,2048]{1,0:T(8,128)S(1)} %get-tuple-element.39.exp_ref, ...), custom_call_target="tpu_custom_call" | custom-call | tf_op jit(solution)/shard_map/proto_grad/pallas_call | solution.py:45
  150.3 1.9 collective-permute-start
  152.2 2.2 %feat_grad.1.feat_ref = bf16[32,16,512]{2,1,0:T(8,128)(2,1)} custom-call(bf16[1024,2048]{1,0:T(8,128)(2,1)S(1)} %get-tuple-element.46.grad_ref, bf16[256,2048]{1,0:T(8,128)(2,1)S(1)} %get-tuple-element.35.cols_ref, bf16[256,1024]{1,0:T(8,128)(2,1)S(1)} %get-tuple-element.47.raw_feat_ref, f32[1,1024]{1,0:T(1,128)S(1)} %get-tuple-element.48.feat_inv_ref), custom_call_target="tpu_custom_call" | custom-call | tf_op jit(solution)/shard_map/feat_grad/pallas_call | solution.py:45
  155.1 5.0 %all-to-all-start.7 = ((bf16[32,16,512]{2,1,0:T(8,128)(2,1)}), bf16[32,16,512]{2,1,0:T(8,128)(2,1)S(1)}, u32[]{:S(2)}, u32[]{:S(2)}) async-start(bf16[32,16,512]{2,1,0:T(8,128)(2,1)} %get-tuple-element.49), calls=%async_computation.7 | async-start | bytes 1048576 | tf_op jit(solution)/shard_map/all_to_all | solution.py:340
  160.0 2.3 %collective-permute-start.1 = (f32[4,16,2176]{2,1,0:T(8,128)S(1)}, f32[4,16,2176]{2,1,0:T(8,128)S(1)}, u32[]{:S(2)}, u32[]{:S(2)}) collective-permute-start(f32[4,16,2176]{2,1,0:T(8,128)S(1)} %get-tuple-element.51), channel_id=1, source_target_pairs={{0,64},{32,96},{64,0},{96,32},{128,192},{160,224},{192,128},{224,1... | collective-permute-start | bytes 1671176 | tf_op jit(solution)/shard_map/ppermute | solution.py:446
  162.3 13.7 %collective-permute-done.1.got_ref = f32[4,16,2176]{2,1,0:T(8,128)S(1)} collective-permute-done((f32[4,16,2176]{2,1,0:T(8,128)S(1)}, f32[4,16,2176]{2,1,0:T(8,128)S(1)}, u32[]{:S(2)}, u32[]{:S(2)}) %collective-permute-start.1) | collective-permute-done | bytes 557088 | tf_op jit(solution)/shard_map/ppermute | solution.py:446
  176.0 1.9 all-to-all-done.7.after_ref.feat_ref
  178.0 12.0 %all_to_all.52.proto_ref = bf16[4,16,2176]{2,1,0:T(8,128)(2,1)S(1)} all-to-all(bf16[4,16,2176]{2,1,0:T(8,128)(2,1)S(1)} %join_pairs.1), channel_id=1, replica_groups={{0,128,256,384},{32,160,288,416},{64,192,320,448},{96,224,352,480},{1,1..., dimensions={0} | all-to-all | bytes 557056 | tf_op jit(solution)/shard_map/all_to_all | solution.py:448
  190.0 0.8 final_sums.1
  (8 shorter events, 0.8 us)
Async XLA Ops:
  7.2 95.3 %all-gather.2.cloned.1.call-start = ((), (), s32[]{:S(2)}) async-start(), calls=%async_computation.9 | async-start | bytes 1081344 | tf_op jit(solution)/shard_map/all_gather | solution.py:358
  40.8 60.8 %copy-start = (f32[1024,2048]{1,0:T(8,128)}, f32[1024,2048]{1,0:T(8,128)S(1)}, u32[]{:S(2)}) copy-start(f32[1024,2048]{1,0:T(8,128)S(1)} %get-tuple-element.31.exp_ref.source_ref) | copy-start | bytes 25165828
  150.3 4.6 %collective-permute-start = (f32[2,4,16,2176]{3,2,1,0:T(8,128)S(1)}, f32[2,4,16,2176]{3,2,1,0:T(8,128)S(1)}, u32[]{:S(2)}, u32[]{:S(2)}) collective-permute-start(f32[2,4,16,2176]{3,2,1,0:T(8,128)S(1)} %get-tuple-element.45), channel_id=1, source_target_pairs={{0,32},{32,0},{64,96},{96,64},{128,160},{160,128},{192,224},{224,1... | collective-permute-start | bytes 3342344 | tf_op jit(solution)/shard_map/ppermute | solution.py:431
  155.1 22.9 %all-to-all-start.7 = ((bf16[32,16,512]{2,1,0:T(8,128)(2,1)}), bf16[32,16,512]{2,1,0:T(8,128)(2,1)S(1)}, u32[]{:S(2)}, u32[]{:S(2)}) async-start(bf16[32,16,512]{2,1,0:T(8,128)(2,1)} %get-tuple-element.49), calls=%async_computation.7 | async-start | bytes 1048576 | tf_op jit(solution)/shard_map/all_to_all | solution.py:340
  160.0 16.0 %collective-permute-start.1 = (f32[4,16,2176]{2,1,0:T(8,128)S(1)}, f32[4,16,2176]{2,1,0:T(8,128)S(1)}, u32[]{:S(2)}, u32[]{:S(2)}) collective-permute-start(f32[4,16,2176]{2,1,0:T(8,128)S(1)} %get-tuple-element.51), channel_id=1, source_target_pairs={{0,64},{32,96},{64,0},{96,32},{128,192},{160,224},{192,128},{224,1... | collective-permute-start | bytes 1671176 | tf_op jit(solution)/shard_map/ppermute | solution.py:446
Sparse Core Ops, SparseCore 0:
  11.7 85.1 all-gather.1

commit v3 on v2

--- a/solution.py
+++ b/solution.py
@@ -65,37 +65,24 @@
         out_ref[LANES * j : LANES * (j + 1), :] = jnp.broadcast_to(values[j : j + 1, :], (LANES, LANES)).T
 
 
-def halves(x):
-    return jnp.concatenate([x[:, :HALF], x[:, HALF:]], axis=0)
-
-
-def col_fetches(source_ref, raw_ref, sems):
-    lanes = [pl.ds(lo, CHUNK) for lo in range(0, COLS, CHUNK)]
-    return [
-        pltpu.make_async_copy(source_ref.at[:, here], raw_ref.at[:, here], sems.at[i]) for i, here in enumerate(lanes)
-    ]
-
-
-def unit_cols(fetches, raw_ref, round_ref, inv_ref=None):
-    for fetch, lo in zip(fetches, range(0, COLS, CHUNK)):
-        fetch.wait()
-        x = raw_ref[:, lo : lo + CHUNK].astype(F32)
+def prepare_kernel(place_ref, teach_ref, stud_ref, teach_out, stud_out, place_out):
+    place_out[0] = place_ref[0]
+    stud_out[...] = stud_ref[...].astype(F32)
+    put(teach_out, teach_ref[...])
+
+
+def unit_cols_kernel(teacher_ref, student_ref, teacher_out, student_out, inv_ref):
+    for lo in range(0, COLS, CHUNK):
+        lanes = slice(lo, lo + CHUNK)
+        teacher_out[:, lanes] = unit_rows(teacher_ref[:, lanes].astype(F32)).astype(BF16)
+        x = student_ref[:, lanes].astype(F32)
         inv = lax.rsqrt(jnp.sum(x * x, axis=0, keepdims=True) + 1e-06)
-        if inv_ref is not None:
-            inv_ref[:, lo : lo + CHUNK] = inv
-        round_ref[:, lo : lo + CHUNK] = (x * inv).astype(BF16)
+        inv_ref[:, lanes] = inv
+        student_out[:, lanes] = (x * inv).astype(BF16)
 
 
 def unit_rows(x):
     return x * lax.rsqrt(jnp.sum(x * x, axis=0, keepdims=True) + 1e-06)
-
-
-def prepare_kernel(place_ref, teach_ref, stud_ref, teach_out, stud_out, place_out):
-    both = halves(teach_ref[...].astype(F32)).astype(BF16)
-    for peer in range(PROTO):
-        teach_out[peer] = both
-    stud_out[...] = stud_ref[...].astype(F32)
-    place_out[0] = place_ref[0]
 
 
 def put(out_ref, value, rows=slice(None), lanes=slice(None)):
@@ -112,14 +99,11 @@
     return pl.ds(pl.multiple_of(j * LANES, LANES), LANES)
 
 
-def teacher_kernel(feat_ref, source_ref, exp_ref, out_ref, rows_ref, raw_cols_ref, cols_ref, acc_ref, sems):
-    fetches = col_fetches(source_ref, raw_cols_ref, sems)
-    for fetch in fetches:
-        fetch.start()
+def teacher_kernel(feat_ref, cols_ref, exp_ref, out_ref, rows_ref, acc_ref):
     for half in range(2):
-        x = feat_ref[:, 8 * half : 8 * half + 8, :].astype(F32).reshape(D, HALF)
-        rows_ref[HALF * half : HALF * (half + 1), :] = unit_rows(x).T.astype(BF16)
-    unit_cols(fetches, raw_cols_ref, cols_ref)
+        lanes = slice(HALF * half, HALF * (half + 1))
+        x = feat_ref[:, :, lanes].astype(F32).reshape(D, HALF)
+        rows_ref[lanes, :] = unit_rows(x).T.astype(BF16)
     acc_ref[...] = jnp.zeros_like(acc_ref)
 
     def block(j, carry):
@@ -156,11 +140,11 @@
 def row_kernel(exp_ref, got_ref, out_ref, scale_ref, part_ref, sum_ref):
     scale_ref[...] = col_scale_of(got_ref)
     row_sums(exp_ref, scale_ref, part_ref, sum_ref)
-    put(out_ref, sum_ref[...])
+    put(out_ref, sum_ref[...].astype(out_ref.dtype))
 
 
 def col_kernel(exp_ref, got_ref, out_ref, rows_ref, acc_ref):
-    sublane_major(1.0 / (CROPS * jnp.sum(got_ref[...], axis=0)), rows_ref)
+    sublane_major(1.0 / (CROPS * jnp.sum(got_ref[...].astype(F32), axis=0)), rows_ref)
     acc_ref[...] = jnp.zeros_like(acc_ref)
 
     def block(j, carry):
@@ -176,20 +160,26 @@
 
 
 def student_kernel(
-    gathered_ref, source_ref, send_ref, exp_ref, rows_ref, raw_feat_ref, feat_out_ref, feat_inv_ref, raw_cols_ref, cols_ref,
-    cols_inv_ref, sum_ref, out_ref, part_ref, feat_ref, sems, sem,
+    gathered_ref, source_ref, cols_ref, got_ref, exp_ref, weighted_ref, raw_feat_ref, feat_out_ref, feat_inv_ref, out_ref,
+    feat_ref, teacher_ref, rows_ref, scale_ref, part_ref, cross_ref, total_ref, sum_ref, feat_sems, sems,
 ):
-    fetches = col_fetches(source_ref, raw_cols_ref, sems)
-    for fetch in fetches:
-        fetch.start()
-    fetch = pltpu.make_async_copy(gathered_ref, feat_ref, sem)
-    fetch.start()
-    out_ref[...] = send_ref[...]
-    unit_cols(fetches, raw_cols_ref, cols_ref, cols_inv_ref)
-    fetch.wait()
+    def feat_fetch(half):
+        lanes = pl.ds(HALF * half, HALF)
+        return pltpu.make_async_copy(gathered_ref.at[:, lanes], feat_ref.at[half], feat_sems.at[half])
+
+    def fetch(j):
+        at = row_block(j)
+        return pltpu.make_async_copy(source_ref.at[at, :], teacher_ref.at[at, :], sems.at[j])
+
+    for half in range(2):
+        feat_fetch(half).start()
+    for j in range(ROW_TILES):
+        fetch(j).start()
+    scale_ref[...] = col_scale_of(got_ref)
     for half in range(2):
         lanes = slice(HALF * half, HALF * (half + 1))
-        x = feat_ref[:, lanes]
+        feat_fetch(half).wait()
+        x = feat_ref[half]
         raw_feat_ref[:, lanes] = x.astype(BF16)
         inv = lax.rsqrt(jnp.sum(x * x, axis=0, keepdims=True) + 1e-06)
         unit = x * inv
@@ -201,62 +191,54 @@
         at = row_block(j)
         rows = rows_ref[at, :]
         acc = jnp.zeros((LANES, LANES), F32)
+        cross = jnp.zeros((LANES, LANES), F32)
+        total = jnp.zeros((LANES, LANES), F32)
+        fetch(j).wait()
         for lo in range(0, COLS, CHUNK):
             z = jnp.dot(rows, cols_ref[:, lo : lo + CHUNK], preferred_element_type=F32)
             e = jnp.exp2(z * STUDENT_SCALE)
             exp_ref[at, lo : lo + CHUNK] = e
-            for i in range(0, CHUNK, LANES):
-                acc += e[:, i : i + LANES]
-        part_ref[at, :] = acc
-        return carry
-
-    lax.fori_loop(0, ROW_TILES, block, 0)
-    lane_major(part_ref, sum_ref)
-
-
-def last_row_kernel(
-    source_ref, rows_ref, cols_ref, got_ref, total_ref, out_ref, weighted_ref, scale_ref, part_ref, cross_ref, sum_ref, sems
-):
-    def fetch(j):
-        at = row_block(j)
-        return pltpu.make_async_copy(source_ref.at[at, :], weighted_ref.at[at, :], sems.at[j])
-
-    for j in range(ROW_TILES):
-        fetch(j).start()
-    scale_ref[...] = col_scale_of(got_ref)
-
-    def block(j, carry):
-        at = row_block(j)
-        rows = rows_ref[at, :]
-        acc = jnp.zeros((LANES, LANES), F32)
-        cross = jnp.zeros((LANES, LANES), F32)
-        fetch(j).wait()
-        for lo in range(0, COLS, CHUNK):
-            z = jnp.dot(rows, cols_ref[:, lo : lo + CHUNK], preferred_element_type=F32)
             for i in range(lo // LANES, (lo + CHUNK) // LANES):
                 lanes = slice(LANES * i, LANES * (i + 1))
-                weighted = weighted_ref[at, lanes] * scale_ref[i : i + 1, :]
+                here = slice(LANES * i - lo, LANES * (i + 1) - lo)
+                weighted = teacher_ref[at, lanes] * scale_ref[i : i + 1, :]
                 weighted_ref[at, lanes] = weighted
                 acc += weighted
-                cross += weighted * z[:, LANES * i - lo : LANES * (i + 1) - lo]
+                cross += weighted * z[:, here]
+                total += e[:, here]
         part_ref[at, :] = acc
         cross_ref[at, :] = cross
+        total_ref[at, :] = total
         return carry
 
     lax.fori_loop(0, ROW_TILES, block, 0)
-    lane_major(part_ref, sum_ref)
-    put(out_ref, sum_ref[...], rows=slice(0, ROW_TILES))
-    lane_major(cross_ref, sum_ref)
-    put(out_ref, sum_ref[...] / 0.1, rows=slice(ROW_TILES, 2 * ROW_TILES))
-    put(out_ref, total_ref[...], rows=slice(2 * ROW_TILES, 3 * ROW_TILES))
+    sends = []
+    for ref in (part_ref, total_ref, cross_ref):
+        lane_major(ref, sum_ref)
+        high = sum_ref[...].astype(BF16).astype(F32)
+        sends += [high, sum_ref[...] - high]
+    put(out_ref, jnp.concatenate(sends[:5], axis=0).astype(BF16))
 
 
 def grad_kernel(
-    place_ref, weighted_ref, exp_ref, feat_ref, got_ref, raw_cols_ref, cols_inv_ref,
-    grad_ref, own_ref, other_ref, target_ref, soft_ref, part_ref,
+    place_ref, weighted_ref, exp_ref, feat_ref, got_ref, source_ref, cols_inv_ref,
+    grad_ref, own_ref, other_ref, target_ref, soft_ref, order_ref, raw_cols_ref, sems,
 ):
-    got = jnp.sum(got_ref[...], axis=0)
-    sums, cross, totals = got[:ROW_TILES], got[ROW_TILES : 2 * ROW_TILES], got[2 * ROW_TILES :]
+    core, odd = lax.rem(place_ref[0], 2), lax.rem(lax.div(place_ref[0], 2), 2)
+    fetches = []
+    for away in range(2):
+        parity = odd if away == 0 else 1 - odd
+        for side in range(2):
+            other = core if side == 0 else 1 - core
+            fetches.append(
+                pltpu.make_async_copy(source_ref.at[:, parity, other], raw_cols_ref.at[side, away], sems.at[len(fetches)])
+            )
+            for pair in range(PAIRS):
+                order_ref[side, away, pair] = feat_ref[pair, parity, other]
+    for fetch in fetches:
+        fetch.start()
+    got = jnp.sum(got_ref[...].astype(F32), axis=0).reshape(5, ROW_TILES, LANES)
+    sums, totals, cross = got[0] + got[1], got[2] + got[3], got[4] / 0.1
     local_loss = jnp.sum(jnp.log(totals) - cross / sums)
     sublane_major(PROTOS / sums, target_ref)
     sublane_major(PROTOS / totals, soft_ref)
@@ -271,25 +253,23 @@
 
     lax.fori_loop(0, ROW_TILES, block, 0)
 
+    for fetch in fetches:
+        fetch.wait()
+    half_block = (2, PAIRS, D // BATCH, CHUNK)
     for lo in range(0, COLS, CHUNK):
         lanes = slice(lo, lo + CHUNK)
-        part = jnp.dot(feat_ref[...], grad_ref[:, lanes], preferred_element_type=F32)
-        unit = raw_cols_ref[:, lanes].astype(F32) * cols_inv_ref[:, lanes]
+        rows = order_ref[...].reshape(D, ROWS)
+        part = jnp.dot(rows, grad_ref[:, lanes], preferred_element_type=F32)
+        unit = raw_cols_ref[:, :, :, :, lanes].astype(F32).reshape(D, CHUNK) * cols_inv_ref[:, lanes]
         part = part - unit * jnp.sum(unit * part, axis=0, keepdims=True)
-        part_ref[:, :, :, :, lanes] = part.reshape(PAIRS, 2, 2, D // BATCH, CHUNK)
-    core, odd = lax.rem(place_ref[0], 2), lax.rem(lax.div(place_ref[0], 2), 2)
-    loss_row = jnp.full((D // BATCH, LANES), local_loss, F32)
-    for away in range(2):
-        parity = odd if away == 0 else 1 - odd
-        for pair in range(PAIRS):
-            own_ref[away, pair, :, :COLS] = part_ref[pair, parity, core]
-            other_ref[away, pair, :, :COLS] = part_ref[pair, parity, 1 - core]
-            own_ref[away, pair, :, COLS:] = loss_row
-            other_ref[away, pair, :, COLS:] = loss_row
+        own_ref[:, :, :, lanes] = part[: D // 2].reshape(half_block)
+        other_ref[:, :, :, lanes] = part[D // 2 :].reshape(half_block)
+    loss_row = jnp.full((2, PAIRS, D // BATCH, LANES), local_loss, F32)
+    own_ref[:, :, :, COLS:] = loss_row
+    other_ref[:, :, :, COLS:] = loss_row
 
 
 def feat_grad_kernel(grad_ref, cols_ref, raw_feat_ref, feat_inv_ref, out_ref):
-    parts = []
     for half in range(2):
         lanes = slice(HALF * half, HALF * (half + 1))
         part = lax.dot_general(
@@ -297,8 +277,7 @@
         )
         unit = raw_feat_ref[:, lanes].astype(F32) * feat_inv_ref[:, lanes]
         part = part - unit * jnp.sum(unit * part, axis=0, keepdims=True)
-        parts.append(part.reshape(PROTO, 8, HALF))
-    out_ref[...] = jnp.concatenate(parts, axis=1).astype(BF16)
+        out_ref[:, :, lanes] = part.reshape(PROTO, 8, HALF).astype(BF16)
 
 
 def join_cores_kernel(own_ref, got_ref, feat_ref, keep_ref, send_ref, feat_out_ref):
@@ -322,9 +301,7 @@
     proto_out_ref[...] = total[:, :COLS]
     tail = total[:, COLS:]
     loss_ref[...] = (tail[0:1, 0:1] + tail[0:1, 1:2] + tail[0:1, 2:3]) / CROPS
-    feat = jnp.sum(feat_ref[...].astype(F32), axis=0)
-    feat_out_ref[:, :HALF] = feat[:8]
-    feat_out_ref[:, HALF:] = feat[8:]
+    feat_out_ref[...] = jnp.sum(feat_ref[...].astype(F32), axis=0)
 
 
 def per_device(student_feat, teacher_feat, student_proto, teacher_proto):
@@ -339,11 +316,10 @@
     def over_proto(array):
         return lax.all_to_all(array, "proto", 0, 0)
 
-    packed = shape((PROTO, 16, HALF), BF16)
+    packed = shape((PROTO, 8, ROWS), BF16)
     rounded = shape((D, COLS), BF16)
-    rounded_rows = shape((ROWS, D), BF16)
-    row_shape = shape((PROTO, ROW_TILES, LANES))
-    last_shape = shape((PROTO, 3 * ROW_TILES, LANES))
+    row_shape = shape((PROTO, ROW_TILES, LANES), BF16)
+    last_shape = shape((PROTO, 5 * ROW_TILES, LANES), BF16)
     col_shape, last_col_shape = shape((BATCH, COL_TILES, LANES), BF16), shape((BATCH, COL_TILES, LANES))
     row_tile, row_part = pltpu.VMEM((ROW_TILES, LANES), F32), pltpu.VMEM((ROWS, LANES), F32)
     col_tile, col_part = pltpu.VMEM((COL_TILES, LANES), F32), pltpu.VMEM((8, COLS), F32)
@@ -357,18 +333,14 @@
     )(place, teacher_feat.T, student_feat.T)
     stud = lax.all_gather(stud_send, "proto", axis=0, tiled=True)
     teach = over_proto(send)
+    teacher_cols, proto_round, proto_inv = call(
+        unit_cols_kernel, [rounded, rounded, shape((1, COLS))], [teacher_proto, student_proto], name="unit_cols"
+    )
     teacher_exp, send = call(
         teacher_kernel,
         [pinned((ROWS, COLS)), col_shape],
-        [teach, stay(teacher_proto)],
-        [
-            pltpu.VMEM((ROWS, D), BF16),
-            pltpu.VMEM((D, COLS), BF16),
-            pltpu.VMEM((D, COLS), BF16),
-            col_part,
-            pltpu.SemaphoreType.DMA((COLS // CHUNK,)),
-        ],
-        specs=[VM, ANY],
+        [teach, teacher_cols],
+        [pltpu.VMEM((ROWS, D), BF16), col_part],
         name="teacher_exp",
     )
     for sweep in range(SWEEPS - 1):
@@ -384,47 +356,58 @@
             [row_part, col_part],
             name="col_pass",
         )
-    student_exp, rows_round, raw_feat, feat_round, feat_inv, raw_proto, proto_round, proto_inv, exp_sum, send = call(
+    got = over_batch(send)
+    student_exp, weighted, raw_feat, feat_round, feat_inv, send = call(
         student_kernel,
         [
             pinned((ROWS, COLS)),
-            rounded_rows,
+            pinned((ROWS, COLS)),
             shape((D, ROWS), BF16),
             shape((D, ROWS), BF16),
             shape((1, ROWS)),
-            rounded,
-            rounded,
-            shape((1, COLS)),
-            shape((ROW_TILES, LANES)),
-            last_col_shape,
+            last_shape,
         ],
-        [stay(stud), stay(student_proto), send],
+        [stay(stud), stay(teacher_exp), proto_round, got],
         [
+            pltpu.VMEM((2, D, HALF), F32),
+            pltpu.VMEM((ROWS, COLS), F32),
+            pltpu.VMEM((ROWS, D), BF16),
+            col_tile,
             row_part,
-            pltpu.VMEM((D, ROWS), F32),
-            pltpu.SemaphoreType.DMA((COLS // CHUNK,)),
-            pltpu.SemaphoreType.DMA,
+            row_part,
+            row_part,
+            row_tile,
+            pltpu.SemaphoreType.DMA((2,)),
+            pltpu.SemaphoreType.DMA((ROW_TILES,)),
         ],
-        specs=[ANY, ANY, VM],
-        name="student_exp",
-    )
-    got = over_batch(send)
-    send, weighted = call(
-        last_row_kernel,
-        [last_shape, pinned((ROWS, COLS))],
-        [stay(teacher_exp), rows_round, proto_round, got, exp_sum],
-        [col_tile, row_part, row_part, row_tile, pltpu.SemaphoreType.DMA((ROW_TILES,))],
-        specs=[ANY] + [VM] * 4,
-        name="last_row_pass",
+        specs=[ANY, ANY, VM, VM],
+        vmem=20,
+        name="student_and_last_row",
     )
     got = over_proto(send)
     half_shape = shape((2, PAIRS, D // BATCH, COLS + LANES))
+    split = (PAIRS, 2, 2, D // BATCH)
+    order = (2, 2, PAIRS, D // BATCH)
     grad_logit, own, other = call(
         grad_kernel,
         [pinned((ROWS, COLS), BF16), half_shape, half_shape],
-        [place, pin(weighted), pin(student_exp), feat_round, got, raw_proto, proto_inv],
-        [row_part, row_part, pltpu.VMEM((PAIRS, 2, 2, D // BATCH, COLS), F32)],
-        specs=[SM] + [VM] * 6,
+        [
+            place,
+            pin(weighted),
+            pin(student_exp),
+            feat_round.reshape(split + (ROWS,)),
+            got,
+            stay(student_proto.reshape(split + (COLS,))),
+            proto_inv,
+        ],
+        [
+            row_part,
+            row_part,
+            pltpu.VMEM(order + (ROWS,), BF16),
+            pltpu.VMEM(order + (COLS,), BF16),
+            pltpu.SemaphoreType.DMA((4,)),
+        ],
+        specs=[SM] + [VM] * 4 + [ANY, VM],
         vmem=16,
         name="proto_grad",
     )

time: 199 us -> 189 us (0.950)
  blocking collectives: 132 us -> 98.5 us
  waiting for transfers between devices: 16.2 us -> 30.7 us
  starting transfers between devices: 9.19 us -> 19.1 us
  Pallas kernels: 26.4 us -> 23.6 us
  local copies, waits for them, and re-layouts: 0.01 us -> 2.45 us
    all_to_all x4 -> x3, blocking collectives: 79.7 us -> 45.8 us  [over_proto(): return lax.all_to_all(array, 'proto', 0, 0)]
    all_to_all x1 -> x2, waiting for transfers between devices: 1.93 us -> 16.4 us  [over_proto(): return lax.all_to_all(array, 'proto', 0, 0)]
    all_to_all x1 -> x2, starting transfers between devices: 4.95 us -> 15 us  [over_proto(): return lax.all_to_all(array, 'proto', 0, 0)]
    pallas_call x11, Pallas kernels: 24.7 us -> 21.9 us  [call(): pl.pallas_call(body, out_shape=outs, in_specs=specs or [VM] * len(args),...]
    unnamed x2 -> x6, local copies, waits for them, and re-layouts: 0.01 us -> 2.45 us
  transfers between devices with their start and end apart: 4 -> 5, of which waited for: 3 -> 4; matrix products, arithmetic and copies ran while one was open for 0% -> 0% of each run, Pallas kernels for 5% -> 5%
where the time goes in v3:
time: 189 us
  blocking collectives  98.5 us (52%)
  waiting for transfers between devices  30.7 us (16%)
  Pallas kernels  23.6 us (12%)
  starting transfers between devices  19.1 us (10%)
  between operations  14.1 us (7%)
  local copies, waits for them, and re-layouts  2.45 us (1%)
    all_to_all x3, blocking collectives, over_proto(): return lax.all_to_all(array, 'proto', 0, 0)  45.8 us
    all_to_all x3, blocking collectives, over_batch(): return lax.all_to_all(array, 'batch', 0, 0)  40 us
    pallas_call x11, Pallas kernels, call(): pl.pallas_call(body, out_shape=outs, in_specs=specs or [VM] * len(args),...  21.9 us
    all_to_all x2, waiting for transfers between devices, over_proto(): return lax.all_to_all(array, 'proto', 0, 0)  16.4 us
    all_to_all x2, starting transfers between devices, over_proto(): return lax.all_to_all(array, 'proto', 0, 0)  15 us
    ppermute x1, waiting for transfers between devices, per_device(): arrived = lax.ppermute(send, 'batch', swap_pairs)  13.8 us
    all_to_all x1, blocking collectives, per_device(): proto_got = lax.all_to_all(joined, 'batch', 0, 0, axis_index_groups=quads)  12.8 us
  transfers between devices with their start and end apart: 5, of which 4 were waited for; matrix products, arithmetic and copies ran while one was open for 0% of the time, Pallas kernels for 5%

profile of v3, /device:TPU:8, one launch (start us, length us, event | category | flops | bytes accessed | tf_op | source)
XLA Modules:
  0.0 188.6 jit_solution(15225567849945042587)
XLA Ops:
  7.2 1.6 prepare.1
  8.9 10.2 %all-to-all-start = ((bf16[32,8,1024]{2,1,0:T(8,128)(2,1)}), bf16[32,8,1024]{2,1,0:T(8,128)(2,1)S(1)}, u32[]{:S(2)}, u32[]{:S(2)}) async-start(bf16[32,8,1024]{2,1,0:T(8,128)(2,1)} %get-tuple-element.28), calls=%async_computation | async-start | bytes 1048576 | tf_op jit(solution)/shard_map/all_to_all | solution.py:317
  19.1 1.2 copy-done.1
  20.3 1.2 copy-done.2
  22.2 14.5 %all-to-all-done.feat_ref = bf16[32,8,1024]{2,1,0:T(8,128)(2,1)S(1)} async-done(((bf16[32,8,1024]{2,1,0:T(8,128)(2,1)}), bf16[32,8,1024]{2,1,0:T(8,128)(2,1)S(1)}, u32[]{:S(2)}, u32[]{:S(2)}) %all-to-all-start) | async-done | bytes 524320 | tf_op jit(solution)/shard_map/all_to_all | solution.py:317
  36.7 2.9 %teacher_exp.1 = (f32[1024,2048]{1,0:T(8,128)S(1)}, bf16[16,16,128]{2,1,0:T(8,128)(2,1)S(1)}) custom-call(bf16[32,8,1024]{2,1,0:T(8,128)(2,1)S(1)} %all-to-all-done.feat_ref, bf16[256,2048]{1,0:T(8,128)(2,1)S(1)} %get-tuple-element.29.cols_ref), custom_call_target="tpu_custom_call" | custom-call | tf_op jit(solution)/shard_map/teacher_exp/pallas_call | solution.py:45
  39.6 18.3 %all_to_all.45.got_ref = bf16[16,16,128]{2,1,0:T(8,128)(2,1)S(1)} all-to-all(bf16[16,16,128]{2,1,0:T(8,128)(2,1)S(1)} %get-tuple-element.32), channel_id=1, replica_groups=mesh['batch'=16,'proto'=32] {'batch'}, dimensions={0} | all-to-all | bytes 131072 | tf_op jit(solution)/shard_map/all_to_all | solution.py:314
  57.9 0.9 row_pass.2
  58.7 13.9 %all_to_all.46.got_ref = bf16[32,8,128]{2,1,0:T(8,128)(2,1)S(1)} all-to-all(bf16[32,8,128]{2,1,0:T(8,128)(2,1)S(1)} %row_pass.2), channel_id=1, replica_groups=mesh['batch'=16,'proto'=32] {'proto'}, dimensions={0} | all-to-all | bytes 131072 | tf_op jit(solution)/shard_map/all_to_all | solution.py:317
  72.6 0.9 col_pass.2
  73.5 10.4 %all_to_all.47.got_ref = bf16[16,16,128]{2,1,0:T(8,128)(2,1)S(1)} all-to-all(bf16[16,16,128]{2,1,0:T(8,128)(2,1)S(1)} %col_pass.2), channel_id=1, replica_groups=mesh['batch'=16,'proto'=32] {'batch'}, dimensions={0} | all-to-all | bytes 131072 | tf_op jit(solution)/shard_map/all_to_all | solution.py:314
  84.8 13.2 %all_to_all.48.got_ref = bf16[32,8,128]{2,1,0:T(8,128)(2,1)S(1)} all-to-all(bf16[32,8,128]{2,1,0:T(8,128)(2,1)S(1)} %row_pass.3), channel_id=1, replica_groups=mesh['batch'=16,'proto'=32] {'proto'}, dimensions={0} | all-to-all | bytes 131072 | tf_op jit(solution)/shard_map/all_to_all | solution.py:317
  98.0 0.9 col_pass.3
  98.9 11.3 %all_to_all.49.got_ref = f32[16,16,128]{2,1,0:T(8,128)S(1)} all-to-all(f32[16,16,128]{2,1,0:T(8,128)S(1)} %col_pass.3), channel_id=1, replica_groups=mesh['batch'=16,'proto'=32] {'batch'}, dimensions={0} | all-to-all | bytes 262144 | tf_op jit(solution)/shard_map/all_to_all | solution.py:314
  110.2 7.4 %student_and_last_row.1 = (f32[1024,2048]{1,0:T(8,128)S(1)}, f32[1024,2048]{1,0:T(8,128)S(1)}, bf16[256,1024]{1,0:T(8,128)(2,1)S(1)}, bf16[256,1024]{1,0:T(8,128...) custom-call(f32[256,1024]{1,0:T(8,128)} %all-gather.2.cloned.1.call-done.gathered_ref, ...), custom_call_target="tpu_custom_call" | custom-call | tf_op jit(solution)/shard_map/student_and_last_row/pallas_call | solution.py:45
  117.7 18.7 %all_to_all.50.got_ref = bf16[32,40,128]{2,1,0:T(8,128)(2,1)S(1)} all-to-all(bf16[32,40,128]{2,1,0:T(8,128)(2,1)S(1)} %get-tuple-element.36), channel_id=1, replica_groups=mesh['batch'=16,'proto'=32] {'proto'}, dimensions={0} | all-to-all | bytes 655360 | tf_op jit(solution)/shard_map/all_to_all | solution.py:317
  136.3 4.3 %proto_grad.1 = (bf16[1024,2048]{1,0:T(8,128)(2,1)S(1)}, f32[2,4,16,2176]{3,2,1,0:T(8,128)S(1)}, f32[2,4,16,2176]{3,2,1,0:T(8,128)S(1)}) custom-call(s32[1]{0:T(128)} %get-tuple-element.26.place_ref, f32[1024,2048]{1,0:T(8,128)S(1)} %get-tuple-element.33.weighted_ref, f32[1024,2048]{1,0:T(8,128)S(1)} %get-tuple-element.34.exp_ref, ...), custom_call_target="tpu_custom_call" | custom-call | tf_op jit(solution)/shard_map/proto_grad/pallas_call | solution.py:45
  140.6 1.9 %collective-permute-start = (f32[2,4,16,2176]{3,2,1,0:T(8,128)S(1)}, f32[2,4,16,2176]{3,2,1,0:T(8,128)S(1)}, u32[]{:S(2)}, u32[]{:S(2)}) collective-permute-start(f32[2,4,16,2176]{3,2,1,0:T(8,128)S(1)} %get-tuple-element.39), channel_id=1, source_target_pairs={{0,32},{32,0},{64,96},{96,64},{128,160},{160,128},{192,224},{224,1... | collective-permute-start | bytes 3342344 | tf_op jit(solution)/shard_map/ppermute | solution.py:414
  142.5 2.3 %feat_grad.1.feat_ref = bf16[32,8,1024]{2,1,0:T(8,128)(2,1)} custom-call(bf16[1024,2048]{1,0:T(8,128)(2,1)S(1)} %get-tuple-element.40.grad_ref, bf16[256,2048]{1,0:T(8,128)(2,1)S(1)} %get-tuple-element.31.cols_ref, bf16[256,1024]{1,0:T(8,128)(2,1)S(1)} %get-tuple-element.41.raw_feat_ref, f32[1,1024]{1,0:T(1,128)S(1)} %get-tuple-element.42.feat_inv_ref), custom_call_target="tpu_custom_call" | custom-call | tf_op jit(solution)/shard_map/feat_grad/pallas_call | solution.py:45
  145.4 4.8 %all-to-all-start.7 = ((bf16[32,8,1024]{2,1,0:T(8,128)(2,1)}), bf16[32,8,1024]{2,1,0:T(8,128)(2,1)S(1)}, u32[]{:S(2)}, u32[]{:S(2)}) async-start(bf16[32,8,1024]{2,1,0:T(8,128)(2,1)} %get-tuple-element.43), calls=%async_computation.7 | async-start | bytes 1048576 | tf_op jit(solution)/shard_map/all_to_all | solution.py:317
  150.2 2.2 %collective-permute-start.1 = (f32[4,16,2176]{2,1,0:T(8,128)S(1)}, f32[4,16,2176]{2,1,0:T(8,128)S(1)}, u32[]{:S(2)}, u32[]{:S(2)}) collective-permute-start(f32[4,16,2176]{2,1,0:T(8,128)S(1)} %get-tuple-element.45), channel_id=1, source_target_pairs={{0,64},{32,96},{64,0},{96,32},{128,192},{160,224},{192,128},{224,1... | collective-permute-start | bytes 1671176 | tf_op jit(solution)/shard_map/ppermute | solution.py:429
  152.4 13.8 %collective-permute-done.1.got_ref = f32[4,16,2176]{2,1,0:T(8,128)S(1)} collective-permute-done((f32[4,16,2176]{2,1,0:T(8,128)S(1)}, f32[4,16,2176]{2,1,0:T(8,128)S(1)}, u32[]{:S(2)}, u32[]{:S(2)}) %collective-permute-start.1) | collective-permute-done | bytes 557088 | tf_op jit(solution)/shard_map/ppermute | solution.py:429
  166.2 1.9 %all-to-all-done.7.after_ref.feat_ref = bf16[32,8,1024]{2,1,0:T(8,128)(2,1)S(1)} async-done(((bf16[32,8,1024]{2,1,0:T(8,128)(2,1)}), bf16[32,8,1024]{2,1,0:T(8,128)(2,1)S(1)}, u32[]{:S(2)}, u32[]{:S(2)}) %all-to-all-start.7) | async-done | bytes 524320 | tf_op jit(solution)/shard_map/all_to_all | solution.py:317
  168.2 12.8 %all_to_all.51.proto_ref = bf16[4,16,2176]{2,1,0:T(8,128)(2,1)S(1)} all-to-all(bf16[4,16,2176]{2,1,0:T(8,128)(2,1)S(1)} %join_pairs.1), channel_id=1, replica_groups={{0,128,256,384},{32,160,288,416},{64,192,320,448},{96,224,352,480},{1,1..., dimensions={0} | all-to-all | bytes 557056 | tf_op jit(solution)/shard_map/all_to_all | solution.py:431
  (13 shorter events, 3.0 us)
Async XLA Ops:
  7.2 103.1 %all-gather.2.cloned.1.call-start = ((), (), s32[]{:S(2)}) async-start(), calls=%async_computation.9 | async-start | bytes 1081344 | tf_op jit(solution)/shard_map/all_gather | solution.py:334
  8.9 27.8 %all-to-all-start = ((bf16[32,8,1024]{2,1,0:T(8,128)(2,1)}), bf16[32,8,1024]{2,1,0:T(8,128)(2,1)S(1)}, u32[]{:S(2)}, u32[]{:S(2)}) async-start(bf16[32,8,1024]{2,1,0:T(8,128)(2,1)} %get-tuple-element.28), calls=%async_computation | async-start | bytes 1048576 | tf_op jit(solution)/shard_map/all_to_all | solution.py:317
  19.0 1.2 copy-start.1
  20.3 1.2 copy-start.2
  39.6 58.4 %copy-start = (f32[1024,2048]{1,0:T(8,128)}, f32[1024,2048]{1,0:T(8,128)S(1)}, u32[]{:S(2)}) copy-start(f32[1024,2048]{1,0:T(8,128)S(1)} %get-tuple-element.30.exp_ref.source_ref) | copy-start | bytes 25165828
  140.6 4.6 %collective-permute-start = (f32[2,4,16,2176]{3,2,1,0:T(8,128)S(1)}, f32[2,4,16,2176]{3,2,1,0:T(8,128)S(1)}, u32[]{:S(2)}, u32[]{:S(2)}) collective-permute-start(f32[2,4,16,2176]{3,2,1,0:T(8,128)S(1)} %get-tuple-element.39), channel_id=1, source_target_pairs={{0,32},{32,0},{64,96},{96,64},{128,160},{160,128},{192,224},{224,1... | collective-permute-start | bytes 3342344 | tf_op jit(solution)/shard_map/ppermute | solution.py:414
  145.4 22.8 %all-to-all-start.7 = ((bf16[32,8,1024]{2,1,0:T(8,128)(2,1)}), bf16[32,8,1024]{2,1,0:T(8,128)(2,1)S(1)}, u32[]{:S(2)}, u32[]{:S(2)}) async-start(bf16[32,8,1024]{2,1,0:T(8,128)(2,1)} %get-tuple-element.43), calls=%async_computation.7 | async-start | bytes 1048576 | tf_op jit(solution)/shard_map/all_to_all | solution.py:317
  150.2 16.0 %collective-permute-start.1 = (f32[4,16,2176]{2,1,0:T(8,128)S(1)}, f32[4,16,2176]{2,1,0:T(8,128)S(1)}, u32[]{:S(2)}, u32[]{:S(2)}) collective-permute-start(f32[4,16,2176]{2,1,0:T(8,128)S(1)} %get-tuple-element.45), channel_id=1, source_target_pairs={{0,64},{32,96},{64,0},{96,32},{128,192},{160,224},{192,128},{224,1... | collective-permute-start | bytes 1671176 | tf_op jit(solution)/shard_map/ppermute | solution.py:429
Sparse Core Ops, SparseCore 0:
  11.7 85.1 all-gather.1

commit v4 on v3

--- a/solution.py
+++ b/solution.py
@@ -15,9 +15,11 @@
 ROW_TILES, COL_TILES = ROWS // LANES, COLS // LANES
 PROTO, BATCH = 32, 16
 PAIRS = BATCH // 4
+SIDE = 8
 CROPS, PROTOS = ROWS * BATCH, COLS * PROTO
 HALF = ROWS // 2
 CHUNK = 512
+BAND = 32
 MIB = 1024 * 1024
 
 VM = pl.BlockSpec(memory_space=pltpu.VMEM)
@@ -65,9 +67,8 @@
         out_ref[LANES * j : LANES * (j + 1), :] = jnp.broadcast_to(values[j : j + 1, :], (LANES, LANES)).T
 
 
-def prepare_kernel(place_ref, teach_ref, stud_ref, teach_out, stud_out, place_out):
+def prepare_kernel(place_ref, teach_ref, teach_out, place_out):
     place_out[0] = place_ref[0]
-    stud_out[...] = stud_ref[...].astype(F32)
     put(teach_out, teach_ref[...])
 
 
@@ -104,19 +105,12 @@
         lanes = slice(HALF * half, HALF * (half + 1))
         x = feat_ref[:, :, lanes].astype(F32).reshape(D, HALF)
         rows_ref[lanes, :] = unit_rows(x).T.astype(BF16)
-    acc_ref[...] = jnp.zeros_like(acc_ref)
-
-    def block(j, carry):
-        at = row_block(j)
-        rows = rows_ref[at, :]
-        for lo in range(0, COLS, CHUNK):
-            z = jnp.dot(rows, cols_ref[:, lo : lo + CHUNK], preferred_element_type=F32)
-            e = jnp.exp2(z * TEACHER_SCALE)
-            exp_ref[at, lo : lo + CHUNK] = e
-            acc_ref[:, lo : lo + CHUNK] += jnp.sum(e.reshape(LANES // 8, 8, CHUNK), axis=0)
-        return carry
-
-    lax.fori_loop(0, ROW_TILES, block, 0)
+    for lo in range(0, COLS, CHUNK):
+        lanes = slice(lo, lo + CHUNK)
+        z = jnp.dot(rows_ref[...], cols_ref[:, lanes], preferred_element_type=F32)
+        e = jnp.exp2(z * TEACHER_SCALE)
+        exp_ref[:, lanes] = e
+        acc_ref[:, lanes] = jnp.sum(e.reshape(ROWS // 8, 8, CHUNK), axis=0)
     put(out_ref, col_rows(acc_ref).astype(out_ref.dtype))
 
 
@@ -125,26 +119,37 @@
 
 
 def row_sums(exp_ref, scale_ref, part_ref, sum_ref):
-    def block(j, carry):
-        at = row_block(j)
-        acc = jnp.zeros((LANES, LANES), F32)
-        for i in range(COL_TILES):
-            acc += exp_ref[at, LANES * i : LANES * (i + 1)] * scale_ref[i : i + 1, :]
-        part_ref[at, :] = acc
+    def block(pair, carry):
+        for j in (2 * pair, 2 * pair + 1):
+            at = row_block(j)
+            acc = jnp.zeros((LANES, LANES), F32)
+            for i in range(COL_TILES):
+                acc += exp_ref[at, LANES * i : LANES * (i + 1)] * scale_ref[i : i + 1, :]
+            part_ref[at, :] = acc
         return carry
 
-    lax.fori_loop(0, ROW_TILES, block, 0)
+    lax.fori_loop(0, ROW_TILES // 2, block, 0)
     lane_major(part_ref, sum_ref)
 
 
-def row_kernel(exp_ref, got_ref, out_ref, scale_ref, part_ref, sum_ref):
+def first_row_kernel(exp_ref, got_ref, stud_ref, out_ref, scale_ref, part_ref, sum_ref):
     scale_ref[...] = col_scale_of(got_ref)
     row_sums(exp_ref, scale_ref, part_ref, sum_ref)
-    put(out_ref, sum_ref[...].astype(out_ref.dtype))
+    sums = sum_ref[...].astype(BF16)
+    for peer in range(PROTO):
+        half = peer // SIDE % 2
+        out_ref[peer, :, :HALF] = stud_ref[:, HALF * half : HALF * (half + 1)]
+        out_ref[peer, :, HALF:] = sums
+
+
+def row_kernel(exp_ref, got_ref, after_ref, out_ref, scale_ref, part_ref, sum_ref):
+    scale_ref[...] = col_scale_of(got_ref)
+    row_sums(exp_ref, scale_ref, part_ref, sum_ref)
+    put(out_ref, sum_ref[...].astype(BF16))
 
 
 def col_kernel(exp_ref, got_ref, out_ref, rows_ref, acc_ref):
-    sublane_major(1.0 / (CROPS * jnp.sum(got_ref[...].astype(F32), axis=0)), rows_ref)
+    sublane_major(1.0 / (CROPS * jnp.sum(got_ref[:, :, -LANES:].astype(F32), axis=0)), rows_ref)
     acc_ref[...] = jnp.zeros_like(acc_ref)
 
     def block(j, carry):
@@ -160,26 +165,15 @@
 
 
 def student_kernel(
-    gathered_ref, source_ref, cols_ref, got_ref, exp_ref, weighted_ref, raw_feat_ref, feat_out_ref, feat_inv_ref, out_ref,
-    feat_ref, teacher_ref, rows_ref, scale_ref, part_ref, cross_ref, total_ref, sum_ref, feat_sems, sems,
+    place_ref, own_ref, other_ref, teacher_ref, cols_ref, got_ref, exp_ref, weighted_ref, raw_feat_ref, feat_out_ref, feat_inv_ref,
+    out_ref, rows_ref, scale_ref, part_ref, cross_ref, total_ref, sum_ref,
 ):
-    def feat_fetch(half):
-        lanes = pl.ds(HALF * half, HALF)
-        return pltpu.make_async_copy(gathered_ref.at[:, lanes], feat_ref.at[half], feat_sems.at[half])
-
-    def fetch(j):
-        at = row_block(j)
-        return pltpu.make_async_copy(source_ref.at[at, :], teacher_ref.at[at, :], sems.at[j])
-
-    for half in range(2):
-        feat_fetch(half).start()
-    for j in range(ROW_TILES):
-        fetch(j).start()
     scale_ref[...] = col_scale_of(got_ref)
+    side = lax.rem(lax.div(place_ref[0], SIDE), 2)
     for half in range(2):
         lanes = slice(HALF * half, HALF * (half + 1))
-        feat_fetch(half).wait()
-        x = feat_ref[half]
+        own, other = own_ref[:, :, :HALF].astype(F32), other_ref[:, :, :HALF].astype(F32)
+        x = jnp.where(side == half, own, other).reshape(D, HALF)
         raw_feat_ref[:, lanes] = x.astype(BF16)
         inv = lax.rsqrt(jnp.sum(x * x, axis=0, keepdims=True) + 1e-06)
         unit = x * inv
@@ -187,31 +181,25 @@
         feat_out_ref[:, lanes] = unit.astype(BF16)
         feat_inv_ref[:, lanes] = inv
 
-    def block(j, carry):
-        at = row_block(j)
-        rows = rows_ref[at, :]
-        acc = jnp.zeros((LANES, LANES), F32)
-        cross = jnp.zeros((LANES, LANES), F32)
-        total = jnp.zeros((LANES, LANES), F32)
-        fetch(j).wait()
-        for lo in range(0, COLS, CHUNK):
-            z = jnp.dot(rows, cols_ref[:, lo : lo + CHUNK], preferred_element_type=F32)
-            e = jnp.exp2(z * STUDENT_SCALE)
-            exp_ref[at, lo : lo + CHUNK] = e
+    for lo in range(0, COLS, CHUNK):
+        z = jnp.dot(rows_ref[...], cols_ref[:, lo : lo + CHUNK], preferred_element_type=F32)
+        for top in range(0, ROWS, BAND):
+            band = slice(top, top + BAND)
+            if lo == 0:
+                acc = cross = total = jnp.zeros((BAND, LANES), F32)
+            else:
+                acc, cross, total = part_ref[band, :], cross_ref[band, :], total_ref[band, :]
             for i in range(lo // LANES, (lo + CHUNK) // LANES):
                 lanes = slice(LANES * i, LANES * (i + 1))
-                here = slice(LANES * i - lo, LANES * (i + 1) - lo)
-                weighted = teacher_ref[at, lanes] * scale_ref[i : i + 1, :]
-                weighted_ref[at, lanes] = weighted
+                logit = z[band, LANES * i - lo : LANES * (i + 1) - lo]
+                e = jnp.exp2(logit * STUDENT_SCALE)
+                exp_ref[band, lanes] = e
+                weighted = teacher_ref[band, lanes] * scale_ref[i : i + 1, :]
+                weighted_ref[band, lanes] = weighted
                 acc += weighted
-                cross += weighted * z[:, here]
-                total += e[:, here]
-        part_ref[at, :] = acc
-        cross_ref[at, :] = cross
-        total_ref[at, :] = total
-        return carry
-
-    lax.fori_loop(0, ROW_TILES, block, 0)
+                cross += weighted * logit
+                total += e
+            part_ref[band, :], cross_ref[band, :], total_ref[band, :] = acc, cross, total
     sends = []
     for ref in (part_ref, total_ref, cross_ref):
         lane_major(ref, sum_ref)
@@ -224,7 +212,8 @@
     place_ref, weighted_ref, exp_ref, feat_ref, got_ref, source_ref, cols_inv_ref,
     grad_ref, own_ref, other_ref, target_ref, soft_ref, order_ref, raw_cols_ref, sems,
 ):
-    core, odd = lax.rem(place_ref[0], 2), lax.rem(lax.div(place_ref[0], 2), 2)
+    batch = lax.div(place_ref[0], PROTO)
+    core, odd = lax.rem(batch, 2), lax.rem(lax.div(batch, 2), 2)
     fetches = []
     for away in range(2):
         parity = odd if away == 0 else 1 - odd
@@ -244,14 +233,14 @@
     sublane_major(PROTOS / totals, soft_ref)
 
     def block(j, carry):
-        at = row_block(j)
+        at = pl.ds(pl.multiple_of(j * 64, 64), 64)
         target_rows, soft_rows = target_ref[at, :], soft_ref[at, :]
         for i in range(COL_TILES):
             lanes = slice(LANES * i, LANES * (i + 1))
             grad_ref[at, lanes] = (exp_ref[at, lanes] * soft_rows - weighted_ref[at, lanes] * target_rows).astype(BF16)
         return carry
 
-    lax.fori_loop(0, ROW_TILES, block, 0)
+    lax.fori_loop(0, ROWS // 64, block, 0)
 
     for fetch in fetches:
         fetch.wait()
@@ -280,34 +269,42 @@
         out_ref[:, :, lanes] = part.reshape(PROTO, 8, HALF).astype(BF16)
 
 
-def join_cores_kernel(own_ref, got_ref, feat_ref, keep_ref, send_ref, feat_out_ref):
-    keep_ref[...] = own_ref[0] + got_ref[0]
-    send_ref[...] = own_ref[1] + got_ref[1]
-
-
-def join_pairs_kernel(own_ref, got_ref, after_ref, out_ref):
-    total = own_ref[...] + got_ref[...]
-    out_ref[:, :, :COLS] = total[:, :, :COLS].astype(BF16)
-    tail = total[:, :, COLS:]
+def spread(tail):
     lane = lax.broadcasted_iota(jnp.int32, tail.shape, 2)
     high = tail.astype(BF16).astype(F32)
     middle = (tail - high).astype(BF16).astype(F32)
-    low = tail - high - middle
-    out_ref[:, :, COLS:] = jnp.where(lane == 0, high, jnp.where(lane == 1, middle, low)).astype(BF16)
+    return jnp.where(lane == 0, high, jnp.where(lane == 1, middle, tail - high - middle)).astype(BF16)
+
+
+def gather_parts(tail):
+    return tail[..., 0:1] + tail[..., 1:2] + tail[..., 2:3]
+
+
+def join_cores_kernel(own_ref, got_ref, feat_ref, keep_ref, send_ref, feat_out_ref):
+    keep_ref[...] = own_ref[0] + got_ref[0]
+    away = own_ref[1] + got_ref[1]
+    send_ref[:, :, :COLS] = away[:, :, :COLS].astype(BF16)
+    send_ref[:, :, COLS:] = spread(away[:, :, COLS:])
+
+
+def join_pairs_kernel(own_ref, got_ref, after_ref, out_ref):
+    got = got_ref[...].astype(F32)
+    out_ref[:, :, :COLS] = (own_ref[:, :, :COLS] + got[:, :, :COLS]).astype(BF16)
+    out_ref[:, :, COLS:] = spread(own_ref[:, :, COLS:] + gather_parts(got[:, :, COLS:]))
 
 
 def final_kernel(feat_ref, proto_ref, feat_out_ref, proto_out_ref, loss_ref):
     total = jnp.sum(proto_ref[...].astype(F32), axis=0)
     proto_out_ref[...] = total[:, :COLS]
-    tail = total[:, COLS:]
-    loss_ref[...] = (tail[0:1, 0:1] + tail[0:1, 1:2] + tail[0:1, 2:3]) / CROPS
+    loss_ref[...] = gather_parts(total[0:1, COLS:]) / CROPS
     feat_out_ref[...] = jnp.sum(feat_ref[...].astype(F32), axis=0)
 
 
 def per_device(student_feat, teacher_feat, student_proto, teacher_proto):
-    place = lax.axis_index("batch").astype(jnp.int32).reshape(1)
+    place = (lax.axis_index("batch") * PROTO + lax.axis_index("proto")).astype(jnp.int32).reshape(1)
     swap_cores = [(i, i ^ 1) for i in range(BATCH)]
     swap_pairs = [(i, i ^ 2) for i in range(BATCH)]
+    swap_sides = [(i, i ^ SIDE) for i in range(PROTO)]
     quads = [list(range(first, BATCH, 4)) for first in range(4)]
 
     def over_batch(array):
@@ -319,19 +316,19 @@
     packed = shape((PROTO, 8, ROWS), BF16)
     rounded = shape((D, COLS), BF16)
     row_shape = shape((PROTO, ROW_TILES, LANES), BF16)
+    first_row_shape = shape((PROTO, ROW_TILES, HALF + LANES), BF16)
     last_shape = shape((PROTO, 5 * ROW_TILES, LANES), BF16)
     col_shape, last_col_shape = shape((BATCH, COL_TILES, LANES), BF16), shape((BATCH, COL_TILES, LANES))
     row_tile, row_part = pltpu.VMEM((ROW_TILES, LANES), F32), pltpu.VMEM((ROWS, LANES), F32)
     col_tile, col_part = pltpu.VMEM((COL_TILES, LANES), F32), pltpu.VMEM((8, COLS), F32)
 
-    send, stud_send, place = pl.pallas_call(
+    send, place = pl.pallas_call(
         prepare_kernel,
-        out_shape=[packed, shape((8, ROWS)), shape((1,), jnp.int32)],
-        in_specs=[SM, VM, VM],
-        out_specs=[VM, VM, SM],
+        out_shape=[packed, shape((1,), jnp.int32)],
+        in_specs=[SM, VM],
+        out_specs=[VM, SM],
         name="prepare",
-    )(place, teacher_feat.T, student_feat.T)
-    stud = lax.all_gather(stud_send, "proto", axis=0, tiled=True)
+    )(place, teacher_feat.T)
     teach = over_proto(send)
     teacher_cols, proto_round, proto_inv = call(
         unit_cols_kernel, [rounded, rounded, shape((1, COLS))], [teacher_proto, student_proto], name="unit_cols"
@@ -343,19 +340,30 @@
         [pltpu.VMEM((ROWS, D), BF16), col_part],
         name="teacher_exp",
     )
-    for sweep in range(SWEEPS - 1):
-        got = over_batch(send)
-        (send,) = call(
-            row_kernel, [row_shape], [pin(teacher_exp), got], [col_tile, row_part, row_tile], name="row_pass"
-        )
-        got = over_proto(send)
-        (send,) = call(
-            col_kernel,
-            [col_shape if sweep + 2 < SWEEPS else last_col_shape],
-            [pin(teacher_exp), got],
-            [row_part, col_part],
-            name="col_pass",
-        )
+    got = over_batch(send)
+    (send,) = call(
+        first_row_kernel,
+        [first_row_shape],
+        [pin(teacher_exp), got, student_feat.T],
+        [col_tile, row_part, row_tile],
+        name="row_pass_1",
+    )
+    own_half = over_proto(send)
+    other_half = lax.ppermute(own_half, "proto", swap_sides)
+    (send,) = call(
+        col_kernel, [col_shape], [pin(teacher_exp), own_half], [row_part, col_part], name="col_pass_2"
+    )
+    got = over_batch(send)
+    (send,) = call(
+        row_kernel,
+        [row_shape],
+        [pin(teacher_exp), got, other_half],
+        [col_tile, row_part, row_tile],
+        specs=[VM, VM, ANY],
+        name="row_pass_2",
+    )
+    got = over_proto(send)
+    (send,) = call(col_kernel, [last_col_shape], [pin(teacher_exp), got], [row_part, col_part], name="col_pass_3")
     got = over_batch(send)
     student_exp, weighted, raw_feat, feat_round, feat_inv, send = call(
         student_kernel,
@@ -367,21 +375,9 @@
             shape((1, ROWS)),
             last_shape,
         ],
-        [stay(stud), stay(teacher_exp), proto_round, got],
-        [
-            pltpu.VMEM((2, D, HALF), F32),
-            pltpu.VMEM((ROWS, COLS), F32),
-            pltpu.VMEM((ROWS, D), BF16),
-            col_tile,
-            row_part,
-            row_part,
-            row_part,
-            row_tile,
-            pltpu.SemaphoreType.DMA((2,)),
-            pltpu.SemaphoreType.DMA((ROW_TILES,)),
-        ],
-        specs=[ANY, ANY, VM, VM],
-        vmem=20,
+        [place, own_half, other_half, pin(teacher_exp), proto_round, got],
+        [pltpu.VMEM((ROWS, D), BF16), col_tile, row_part, row_part, row_part, row_tile],
+        specs=[SM] + [VM] * 5,
         name="student_and_last_row",
     )
     got = over_proto(send)
@@ -418,7 +414,7 @@
     pair_shape = (PAIRS, D // BATCH, COLS + LANES)
     keep, send, feat_part = pl.pallas_call(
         join_cores_kernel,
-        out_shape=[shape(pair_shape), shape(pair_shape), packed],
+        out_shape=[shape(pair_shape), shape(pair_shape, BF16), packed],
         in_specs=[VM, VM, ANY],
         out_specs=[VM, VM, ANY],
         input_output_aliases={2: 2},

time: 189 us -> 179 us (0.947)
  between operations: 14.1 us -> 0.75 us
  blocking collectives: 98.5 us -> 104 us
  Pallas kernels: 23.6 us -> 18.2 us
  starting transfers between devices: 19.1 us -> 21.6 us
    ppermute x1, waiting for transfers between devices: 13.8 us -> 7.87 us  [per_device(): arrived = lax.ppermute(send, 'batch', swap_pairs)]
    all_to_all x2, waiting for transfers between devices: 16.4 us -> 22.3 us  [over_proto(): return lax.all_to_all(array, 'proto', 0, 0)]
    all_to_all x3, blocking collectives: 45.8 us -> 51.6 us  [over_proto(): return lax.all_to_all(array, 'proto', 0, 0)]
    pallas_call x11, Pallas kernels: 21.9 us -> 16.5 us  [call(): pl.pallas_call(body, out_shape=outs, in_specs=specs or [VM] * len(args),...]
    ppermute x0 -> x1, starting transfers between devices: none -> 2.52 us  [per_device(): other_half = lax.ppermute(own_half, 'proto', swap_sides)]
  transfers between devices with their start and end apart: 5 -> 5, of which waited for: 4 -> 4; matrix products, arithmetic and copies ran while one was open for 0% -> 0% of each run, Pallas kernels for 5% -> 2%
where the time goes in v4:
time: 179 us; the launch traced here: 178 us
  blocking collectives  104 us (58%)
  waiting for transfers between devices  30.7 us (17%)
  starting transfers between devices  21.6 us (12%)
  Pallas kernels  18.2 us (10%)
  local copies, waits for them, and re-layouts  2.45 us (1%)
    all_to_all x3, blocking collectives, over_proto(): return lax.all_to_all(array, 'proto', 0, 0)  51.6 us
    all_to_all x3, blocking collectives, over_batch(): return lax.all_to_all(array, 'batch', 0, 0)  39.8 us
    all_to_all x2, waiting for transfers between devices, over_proto(): return lax.all_to_all(array, 'proto', 0, 0)  22.3 us
    pallas_call x11, Pallas kernels, call(): pl.pallas_call(body, out_shape=outs, in_specs=specs or [VM] * len(args),...  16.5 us
    all_to_all x2, starting transfers between devices, over_proto(): return lax.all_to_all(array, 'proto', 0, 0)  15 us
    all_to_all x1, blocking collectives, per_device(): proto_got = lax.all_to_all(joined, 'batch', 0, 0, axis_index_groups=quads)  12.8 us
    ppermute x1, waiting for transfers between devices, per_device(): arrived = lax.ppermute(send, 'batch', swap_pairs)  7.87 us
  transfers between devices with their start and end apart: 5, of which 4 were waited for; matrix products, arithmetic and copies ran while one was open for 0% of the time, Pallas kernels for 2%

profile of v4, /device:TPU:8, one launch (start us, length us, event | category | flops | bytes accessed | tf_op | source)
XLA Modules:
  0.0 177.8 jit_solution(13518992033515810767)
XLA Ops:
  0.6 1.6 prepare.1
  2.2 10.2 %all-to-all-start = ((bf16[32,8,1024]{2,1,0:T(8,128)(2,1)}), bf16[32,8,1024]{2,1,0:T(8,128)(2,1)S(1)}, u32[]{:S(2)}, u32[]{:S(2)}) async-start(bf16[32,8,1024]{2,1,0:T(8,128)(2,1)} %get-tuple-element.26), calls=%async_computation | async-start | bytes 1048576 | tf_op jit(solution)/shard_map/all_to_all | solution.py:314
  12.4 1.2 copy-done
  13.6 1.2 copy-done.1
  15.6 14.4 %all-to-all-done.feat_ref = bf16[32,8,1024]{2,1,0:T(8,128)(2,1)S(1)} async-done(((bf16[32,8,1024]{2,1,0:T(8,128)(2,1)}), bf16[32,8,1024]{2,1,0:T(8,128)(2,1)S(1)}, u32[]{:S(2)}, u32[]{:S(2)}) %all-to-all-start) | async-done | bytes 524320 | tf_op jit(solution)/shard_map/all_to_all | solution.py:314
  30.0 1.4 teacher_exp.1
  31.4 18.1 %all_to_all.45.got_ref = bf16[16,16,128]{2,1,0:T(8,128)(2,1)S(1)} all-to-all(bf16[16,16,128]{2,1,0:T(8,128)(2,1)S(1)} %get-tuple-element.29), channel_id=1, replica_groups=mesh['batch'=16,'proto'=32] {'batch'}, dimensions={0} | all-to-all | bytes 131072 | tf_op jit(solution)/shard_map/all_to_all | solution.py:311
  50.4 18.8 %all_to_all.46.got_ref.own_ref = bf16[32,8,640]{2,1,0:T(8,128)(2,1)S(1)} all-to-all(bf16[32,8,640]{2,1,0:T(8,128)(2,1)S(1)} %row_pass_1.1), channel_id=1, replica_groups=mesh['batch'=16,'proto'=32] {'proto'}, dimensions={0} | all-to-all | bytes 655360 | tf_op jit(solution)/shard_map/all_to_all | solution.py:314
  69.1 2.5 %collective-permute-start = (bf16[32,8,640]{2,1,0:T(8,128)(2,1)S(1)}, bf16[32,8,640]{2,1,0:T(8,128)(2,1)S(1)}, u32[]{:S(2)}, u32[]{:S(2)}) collective-permute-start(bf16[32,8,640]{2,1,0:T(8,128)(2,1)S(1)} %all_to_all.46.got_ref.own_ref), channel_id=1, source_target_pairs={{0,8},{1,9},{2,10},{3,11},{4,12},{5,13},{6,14},{7,15},{8,0},{9,1},... | collective-permute-start | bytes 983048 | tf_op jit(solution)/shard_map/ppermute | solution.py:352
  71.6 0.9 col_pass_2.1
  72.5 10.4 %all_to_all.47.got_ref = bf16[16,16,128]{2,1,0:T(8,128)(2,1)S(1)} all-to-all(bf16[16,16,128]{2,1,0:T(8,128)(2,1)S(1)} %col_pass_2.1), channel_id=1, replica_groups=mesh['batch'=16,'proto'=32] {'batch'}, dimensions={0} | all-to-all | bytes 131072 | tf_op jit(solution)/shard_map/all_to_all | solution.py:311
  83.7 14.3 %all_to_all.48.got_ref = bf16[32,8,128]{2,1,0:T(8,128)(2,1)S(1)} all-to-all(bf16[32,8,128]{2,1,0:T(8,128)(2,1)S(1)} %row_pass_2.1), channel_id=1, replica_groups=mesh['batch'=16,'proto'=32] {'proto'}, dimensions={0} | all-to-all | bytes 131072 | tf_op jit(solution)/shard_map/all_to_all | solution.py:314
  98.1 0.9 col_pass_3.1
  99.0 11.3 %all_to_all.49.got_ref = f32[16,16,128]{2,1,0:T(8,128)S(1)} all-to-all(f32[16,16,128]{2,1,0:T(8,128)S(1)} %col_pass_3.1), channel_id=1, replica_groups=mesh['batch'=16,'proto'=32] {'batch'}, dimensions={0} | all-to-all | bytes 262144 | tf_op jit(solution)/shard_map/all_to_all | solution.py:311
  110.3 3.9 %student_and_last_row.1 = (f32[1024,2048]{1,0:T(8,128)S(1)}, f32[1024,2048]{1,0:T(8,128)S(1)}, bf16[256,1024]{1,0:T(8,128)(2,1)S(1)}, bf16[256,1024]{1,0:T(8,128...) custom-call(s32[1]{0:T(128)} %get-tuple-element.25.place_ref, ...), custom_call_target="tpu_custom_call" | custom-call | tf_op jit(solution)/shard_map/student_and_last_row/pallas_call | solution.py:47
  114.2 18.5 %all_to_all.50.got_ref = bf16[32,40,128]{2,1,0:T(8,128)(2,1)S(1)} all-to-all(bf16[32,40,128]{2,1,0:T(8,128)(2,1)S(1)} %get-tuple-element.34), channel_id=1, replica_groups=mesh['batch'=16,'proto'=32] {'proto'}, dimensions={0} | all-to-all | bytes 655360 | tf_op jit(solution)/shard_map/all_to_all | solution.py:314
  132.7 3.9 %proto_grad.1 = (bf16[1024,2048]{1,0:T(8,128)(2,1)S(1)}, f32[2,4,16,2176]{3,2,1,0:T(8,128)S(1)}, f32[2,4,16,2176]{3,2,1,0:T(8,128)S(1)}) custom-call(s32[1]{0:T(128)} %get-tuple-element.25.place_ref, f32[1024,2048]{1,0:T(8,128)S(1)} %get-tuple-element.31.weighted_ref, f32[1024,2048]{1,0:T(8,128)S(1)} %get-tuple-element.32.exp_ref, ...), custom_call_target="tpu_custom_call" | custom-call | tf_op jit(solution)/shard_map/proto_grad/pallas_call | solution.py:47
  136.6 1.9 %collective-permute-start.1 = (f32[2,4,16,2176]{3,2,1,0:T(8,128)S(1)}, f32[2,4,16,2176]{3,2,1,0:T(8,128)S(1)}, u32[]{:S(2)}, u32[]{:S(2)}) collective-permute-start(f32[2,4,16,2176]{3,2,1,0:T(8,128)S(1)} %get-tuple-element.37), channel_id=1, source_target_pairs={{0,32},{32,0},{64,96},{96,64},{128,160},{160,128},{192,224},{224,1... | collective-permute-start | bytes 3342344 | tf_op jit(solution)/shard_map/ppermute | solution.py:410
  138.5 2.2 %feat_grad.1.feat_ref = bf16[32,8,1024]{2,1,0:T(8,128)(2,1)} custom-call(bf16[1024,2048]{1,0:T(8,128)(2,1)S(1)} %get-tuple-element.38.grad_ref, bf16[256,2048]{1,0:T(8,128)(2,1)S(1)} %get-tuple-element.30.cols_ref, bf16[256,1024]{1,0:T(8,128)(2,1)S(1)} %get-tuple-element.39.raw_feat_ref, f32[1,1024]{1,0:T(1,128)S(1)} %get-tuple-element.40.feat_inv_ref), custom_call_target="tpu_custom_call" | custom-call | tf_op jit(solution)/shard_map/feat_grad/pallas_call | solution.py:47
  141.4 4.8 %all-to-all-start.7 = ((bf16[32,8,1024]{2,1,0:T(8,128)(2,1)}), bf16[32,8,1024]{2,1,0:T(8,128)(2,1)S(1)}, u32[]{:S(2)}, u32[]{:S(2)}) async-start(bf16[32,8,1024]{2,1,0:T(8,128)(2,1)} %get-tuple-element.41), calls=%async_computation.7 | async-start | bytes 1048576 | tf_op jit(solution)/shard_map/all_to_all | solution.py:314
  146.2 2.2 %collective-permute-start.2 = (bf16[4,16,2176]{2,1,0:T(8,128)(2,1)S(1)}, bf16[4,16,2176]{2,1,0:T(8,128)(2,1)S(1)}, u32[]{:S(2)}, u32[]{:S(2)}) collective-permute-start(bf16[4,16,2176]{2,1,0:T(8,128)(2,1)S(1)} %get-tuple-element.43), channel_id=1, source_target_pairs={{0,64},{32,96},{64,0},{96,32},{128,192},{160,224},{192,128},{224,1... | collective-permute-start | bytes 835592 | tf_op jit(solution)/shard_map/ppermute | solution.py:425
  148.3 7.9 %collective-permute-done.2.got_ref = bf16[4,16,2176]{2,1,0:T(8,128)(2,1)S(1)} collective-permute-done((bf16[4,16,2176]{2,1,0:T(8,128)(2,1)S(1)}, bf16[4,16,2176]{2,1,0:T(8,128)(2,1)S(1)}, u32[]{:S(2)}, u32[]{:S(2)}) %collective-permute-start.2) | collective-permute-done | bytes 278560 | tf_op jit(solution)/shard_map/ppermute | solution.py:425
  156.2 7.9 %all-to-all-done.7.after_ref.feat_ref = bf16[32,8,1024]{2,1,0:T(8,128)(2,1)S(1)} async-done(((bf16[32,8,1024]{2,1,0:T(8,128)(2,1)}), bf16[32,8,1024]{2,1,0:T(8,128)(2,1)S(1)}, u32[]{:S(2)}, u32[]{:S(2)}) %all-to-all-start.7) | async-done | bytes 524320 | tf_op jit(solution)/shard_map/all_to_all | solution.py:314
  164.3 12.8 %all_to_all.51.proto_ref = bf16[4,16,2176]{2,1,0:T(8,128)(2,1)S(1)} all-to-all(bf16[4,16,2176]{2,1,0:T(8,128)(2,1)S(1)} %join_pairs.1), channel_id=1, replica_groups={{0,128,256,384},{32,160,288,416},{64,192,320,448},{96,224,352,480},{1,1..., dimensions={0} | all-to-all | bytes 557056 | tf_op jit(solution)/shard_map/all_to_all | solution.py:427
  (12 shorter events, 3.9 us)
Async XLA Ops:
  0.6 48.9 %copy-start.2 = (bf16[1024,8]{0,1:T(8,128)(2,1)S(1)}, bf16[1024,8]{0,1:T(8,128)(2,1)}, u32[]{:S(2)}) copy-start(bf16[1024,8]{0,1:T(8,128)(2,1)} %param.4) | copy-start | bytes 49156
  2.2 27.8 %all-to-all-start = ((bf16[32,8,1024]{2,1,0:T(8,128)(2,1)}), bf16[32,8,1024]{2,1,0:T(8,128)(2,1)S(1)}, u32[]{:S(2)}, u32[]{:S(2)}) async-start(bf16[32,8,1024]{2,1,0:T(8,128)(2,1)} %get-tuple-element.26), calls=%async_computation | async-start | bytes 1048576 | tf_op jit(solution)/shard_map/all_to_all | solution.py:314
  12.4 1.2 copy-start
  13.6 1.2 copy-start.1
  69.1 13.8 %collective-permute-start = (bf16[32,8,640]{2,1,0:T(8,128)(2,1)S(1)}, bf16[32,8,640]{2,1,0:T(8,128)(2,1)S(1)}, u32[]{:S(2)}, u32[]{:S(2)}) collective-permute-start(bf16[32,8,640]{2,1,0:T(8,128)(2,1)S(1)} %all_to_all.46.got_ref.own_ref), channel_id=1, source_target_pairs={{0,8},{1,9},{2,10},{3,11},{4,12},{5,13},{6,14},{7,15},{8,0},{9,1},... | collective-permute-start | bytes 983048 | tf_op jit(solution)/shard_map/ppermute | solution.py:352
  136.6 4.6 %collective-permute-start.1 = (f32[2,4,16,2176]{3,2,1,0:T(8,128)S(1)}, f32[2,4,16,2176]{3,2,1,0:T(8,128)S(1)}, u32[]{:S(2)}, u32[]{:S(2)}) collective-permute-start(f32[2,4,16,2176]{3,2,1,0:T(8,128)S(1)} %get-tuple-element.37), channel_id=1, source_target_pairs={{0,32},{32,0},{64,96},{96,64},{128,160},{160,128},{192,224},{224,1... | collective-permute-start | bytes 3342344 | tf_op jit(solution)/shard_map/ppermute | solution.py:410
  141.4 22.7 %all-to-all-start.7 = ((bf16[32,8,1024]{2,1,0:T(8,128)(2,1)}), bf16[32,8,1024]{2,1,0:T(8,128)(2,1)S(1)}, u32[]{:S(2)}, u32[]{:S(2)}) async-start(bf16[32,8,1024]{2,1,0:T(8,128)(2,1)} %get-tuple-element.41), calls=%async_computation.7 | async-start | bytes 1048576 | tf_op jit(solution)/shard_map/all_to_all | solution.py:314
  146.2 10.0 %collective-permute-start.2 = (bf16[4,16,2176]{2,1,0:T(8,128)(2,1)S(1)}, bf16[4,16,2176]{2,1,0:T(8,128)(2,1)S(1)}, u32[]{:S(2)}, u32[]{:S(2)}) collective-permute-start(bf16[4,16,2176]{2,1,0:T(8,128)(2,1)S(1)} %get-tuple-element.43), channel_id=1, source_target_pairs={{0,64},{32,96},{64,0},{96,32},{128,192},{160,224},{192,128},{224,1... | collective-permute-start | bytes 835592 | tf_op jit(solution)/shard_map/ppermute | solution.py:425

commit v5 on v4

--- a/solution.py
+++ b/solution.py
@@ -18,9 +18,11 @@
 SIDE = 8
 CROPS, PROTOS = ROWS * BATCH, COLS * PROTO
 HALF = ROWS // 2
+QUARTER = ROWS // 4
 CHUNK = 512
 BAND = 32
 MIB = 1024 * 1024
+LONG = 200_000_000_000
 
 VM = pl.BlockSpec(memory_space=pltpu.VMEM)
 SM = pl.BlockSpec(memory_space=pltpu.SMEM)
@@ -43,7 +45,7 @@
     return pltpu.with_memory_space_constraint(array, pltpu.HBM)
 
 
-def call(body, outs, args, scratch=(), specs=None, name=None, vmem=12, aliases=None):
+def call(body, outs, args, scratch=(), specs=None, name=None, vmem=12, aliases=None, flops=None):
     return pl.pallas_call(
         body,
         out_shape=outs,
@@ -52,6 +54,7 @@
         scratch_shapes=list(scratch),
         compiler_params=pltpu.CompilerParams(vmem_limit_bytes=vmem * MIB),
         input_output_aliases=aliases or {},
+        cost_estimate=flops and pl.CostEstimate(flops=flops, bytes_accessed=0, transcendentals=0),
         name=name,
     )(*args)
 
@@ -258,19 +261,25 @@
     other_ref[:, :, :, COLS:] = loss_row
 
 
-def feat_grad_kernel(grad_ref, cols_ref, raw_feat_ref, feat_inv_ref, out_ref):
-    for half in range(2):
-        lanes = slice(HALF * half, HALF * (half + 1))
+def feat_grad_kernel(grad_ref, cols_ref, raw_feat_ref, feat_inv_ref, out_ref, stage_ref, sems):
+    copies = []
+    for quarter in range(4):
+        lanes = slice(QUARTER * quarter, QUARTER * (quarter + 1))
         part = lax.dot_general(
             cols_ref[...], grad_ref[lanes, :], (((1,), (1,)), ((), ())), preferred_element_type=F32
         )
         unit = raw_feat_ref[:, lanes].astype(F32) * feat_inv_ref[:, lanes]
         part = part - unit * jnp.sum(unit * part, axis=0, keepdims=True)
-        out_ref[:, :, lanes] = part.reshape(PROTO, 8, HALF).astype(BF16)
+        stage_ref[quarter] = part.reshape(PROTO, 8, QUARTER).astype(BF16)
+        there = out_ref.at[:, :, pl.ds(QUARTER * quarter, QUARTER)]
+        copies.append(pltpu.make_async_copy(stage_ref.at[quarter], there, sems.at[quarter]))
+        copies[-1].start()
+    for copy in copies:
+        copy.wait()
 
 
 def spread(tail):
-    lane = lax.broadcasted_iota(jnp.int32, tail.shape, 2)
+    lane = lax.broadcasted_iota(jnp.int32, tail.shape, tail.ndim - 1)
     high = tail.astype(BF16).astype(F32)
     middle = (tail - high).astype(BF16).astype(F32)
     return jnp.where(lane == 0, high, jnp.where(lane == 1, middle, tail - high - middle)).astype(BF16)
@@ -287,17 +296,34 @@
     send_ref[:, :, COLS:] = spread(away[:, :, COLS:])
 
 
-def join_pairs_kernel(own_ref, got_ref, after_ref, out_ref):
-    got = got_ref[...].astype(F32)
-    out_ref[:, :, :COLS] = (own_ref[:, :, :COLS] + got[:, :, :COLS]).astype(BF16)
-    out_ref[:, :, COLS:] = spread(own_ref[:, :, COLS:] + gather_parts(got[:, :, COLS:]))
-
-
-def final_kernel(feat_ref, proto_ref, feat_out_ref, proto_out_ref, loss_ref):
-    total = jnp.sum(proto_ref[...].astype(F32), axis=0)
-    proto_out_ref[...] = total[:, :COLS]
-    loss_ref[...] = gather_parts(total[0:1, COLS:]) / CROPS
+def join_pairs_kernel(place_ref, own_ref, got_ref, keep_ref, *send_refs):
+    pair = lax.div(lax.div(place_ref[0], PROTO), 4)
+    for away in range(PAIRS):
+        there = lax.rem(pair + away, PAIRS)
+        got = got_ref[there].astype(F32)
+        total = own_ref[there, :, :COLS] + got[:, :COLS]
+        tail = own_ref[there, :, COLS:] + gather_parts(got[:, COLS:])
+        if away == 0:
+            keep_ref[:, :COLS] = total
+            keep_ref[:, COLS:] = tail
+        else:
+            send_refs[away - 1][:, :COLS] = total.astype(BF16)
+            send_refs[away - 1][:, COLS:] = spread(tail)
+
+
+def feat_sum_kernel(feat_ref, feat_out_ref):
     feat_out_ref[...] = jnp.sum(feat_ref[...].astype(F32), axis=0)
+
+
+def proto_sum_kernel(keep_ref, first_ref, second_ref, third_ref, after_ref, proto_out_ref, loss_ref):
+    total = keep_ref[:, :COLS]
+    loss = keep_ref[0:1, COLS : COLS + 1]
+    for ref in (first_ref, second_ref, third_ref):
+        got = ref[...].astype(F32)
+        total += got[:, :COLS]
+        loss += gather_parts(got[0:1, COLS:])
+    proto_out_ref[...] = total
+    loss_ref[...] = loss / CROPS
 
 
 def per_device(student_feat, teacher_feat, student_proto, teacher_proto):
@@ -305,7 +331,6 @@
     swap_cores = [(i, i ^ 1) for i in range(BATCH)]
     swap_pairs = [(i, i ^ 2) for i in range(BATCH)]
     swap_sides = [(i, i ^ SIDE) for i in range(PROTO)]
-    quads = [list(range(first, BATCH, 4)) for first in range(4)]
 
     def over_batch(array):
         return lax.all_to_all(array, "batch", 0, 0)
@@ -408,9 +433,15 @@
         name="proto_grad",
     )
     arrived = lax.ppermute(other, "batch", swap_cores)
-    (feat_part,) = call(
-        feat_grad_kernel, [packed], [pin(grad_logit), proto_round, raw_feat, feat_inv], name="feat_grad"
-    )
+    feat_part = pl.pallas_call(
+        feat_grad_kernel,
+        out_shape=packed,
+        in_specs=[VM] * 4,
+        out_specs=ANY,
+        scratch_shapes=[pltpu.VMEM((4, PROTO, 8, QUARTER), BF16), pltpu.SemaphoreType.DMA((4,))],
+        compiler_params=pltpu.CompilerParams(vmem_limit_bytes=12 * MIB),
+        name="feat_grad",
+    )(pin(grad_logit), proto_round, raw_feat, feat_inv)
     pair_shape = (PAIRS, D // BATCH, COLS + LANES)
     keep, send, feat_part = pl.pallas_call(
         join_cores_kernel,
@@ -423,13 +454,26 @@
     )(own, arrived, feat_part)
     feat_got = over_proto(feat_part)
     arrived = lax.ppermute(send, "batch", swap_pairs)
-    (joined,) = call(join_pairs_kernel, [shape(pair_shape, BF16)], [keep, arrived, feat_got], specs=[VM, VM, ANY], name="join_pairs")
-    proto_got = lax.all_to_all(joined, "batch", 0, 0, axis_index_groups=quads)
-    feat_out, proto_out, loss = call(
-        final_kernel,
-        [shape((8, ROWS)), shape((D // BATCH, COLS)), shape((1, 1))],
-        [feat_got, proto_got],
-        name="final_sums",
+    block = pair_shape[1:]
+    keep, *sends = call(
+        join_pairs_kernel,
+        [shape(block)] + [shape(block, BF16)] * (PAIRS - 1),
+        [place, keep, arrived],
+        specs=[SM, VM, VM],
+        flops=LONG,
+        name="join_pairs",
+    )
+    quads = [
+        lax.ppermute(send, "batch", [(i, (i + 4 * away) % BATCH) for i in range(BATCH)])
+        for away, send in enumerate(sends, 1)
+    ]
+    (feat_out,) = call(feat_sum_kernel, [shape((8, ROWS))], [feat_got], name="feat_sum")
+    proto_out, loss = call(
+        proto_sum_kernel,
+        [shape((D // BATCH, COLS)), shape((1, 1))],
+        [keep, *quads, feat_out],
+        specs=[VM] * 4 + [ANY],
+        name="proto_sum",
     )
     return (loss.reshape(()), feat_out.T, proto_out)
 

time: 179 us -> 172 us (0.961)
  the two profiles are of different devices: /device:TPU:8 before, /device:TPU:1 now
where the time goes in v5:
time: 172 us; the launch traced here: 171 us
  blocking collectives  93.3 us (54%)
  starting transfers between devices  33.8 us (20%)
  Pallas kernels  20.5 us (12%)
  waiting for transfers between devices  19.1 us (11%)
  local copies, waits for them, and re-layouts  3.21 us (2%)
    all_to_all x3, blocking collectives, over_batch(): return lax.all_to_all(array, 'batch', 0, 0)  48.1 us
    all_to_all x3, blocking collectives, over_proto(): return lax.all_to_all(array, 'proto', 0, 0)  45.2 us
    pallas_call x11, Pallas kernels, call(): pl.pallas_call(body, out_shape=outs, in_specs=specs or [VM] * len(args),...  16.6 us
    all_to_all x2, starting transfers between devices, over_proto(): return lax.all_to_all(array, 'proto', 0, 0)  15.5 us
    all_to_all x2, waiting for transfers between devices, over_proto(): return lax.all_to_all(array, 'proto', 0, 0)  11.9 us
    ppermute x3, starting transfers between devices, per_device(): lax.ppermute(send, 'batch', [(i, (i + 4 * away) % BATCH) for i in range(B...  9.96 us
    ppermute x3, waiting for transfers between devices, per_device(): lax.ppermute(send, 'batch', [(i, (i + 4 * away) % BATCH) for i in range(B...  4.25 us
    ppermute x1, starting transfers between devices, per_device(): arrived = lax.ppermute(other, 'batch', swap_cores)  3.85 us
  transfers between devices with their start and end apart: 8, of which 5 were waited for; matrix products, arithmetic and copies ran while one was open for 0% of the time, Pallas kernels for 4%

profile of v5, /device:TPU:1, one launch (start us, length us, event | category | flops | bytes accessed | tf_op | source)
XLA Modules:
  0.0 170.7 jit_solution(16497494883222970812)
XLA Ops:
  0.6 1.6 prepare.1
  2.2 10.5 %all-to-all-start = ((bf16[32,8,1024]{2,1,0:T(8,128)(2,1)}), bf16[32,8,1024]{2,1,0:T(8,128)(2,1)S(1)}, u32[]{:S(2)}, u32[]{:S(2)}) async-start(bf16[32,8,1024]{2,1,0:T(8,128)(2,1)} %get-tuple-element.29), calls=%async_computation | async-start | bytes 1048576 | tf_op jit(solution)/shard_map/all_to_all | solution.py:339
  14.0 1.2 copy-done.1
  16.0 11.1 %all-to-all-done.feat_ref = bf16[32,8,1024]{2,1,0:T(8,128)(2,1)S(1)} async-done(((bf16[32,8,1024]{2,1,0:T(8,128)(2,1)}), bf16[32,8,1024]{2,1,0:T(8,128)(2,1)S(1)}, u32[]{:S(2)}, u32[]{:S(2)}) %all-to-all-start) | async-done | bytes 524320 | tf_op jit(solution)/shard_map/all_to_all | solution.py:339
  27.1 1.4 teacher_exp.1
  28.5 21.4 %all_to_all.40.got_ref = bf16[16,16,128]{2,1,0:T(8,128)(2,1)S(1)} all-to-all(bf16[16,16,128]{2,1,0:T(8,128)(2,1)S(1)} %get-tuple-element.32), channel_id=1, replica_groups=mesh['batch'=16,'proto'=32] {'batch'}, dimensions={0} | all-to-all | bytes 131072 | tf_op jit(solution)/shard_map/all_to_all | solution.py:336
  50.7 15.9 %all_to_all.41.got_ref.own_ref = bf16[32,8,640]{2,1,0:T(8,128)(2,1)S(1)} all-to-all(bf16[32,8,640]{2,1,0:T(8,128)(2,1)S(1)} %row_pass_1.1), channel_id=1, replica_groups=mesh['batch'=16,'proto'=32] {'proto'}, dimensions={0} | all-to-all | bytes 655360 | tf_op jit(solution)/shard_map/all_to_all | solution.py:339
  66.6 2.6 %collective-permute-start = (bf16[32,8,640]{2,1,0:T(8,128)(2,1)S(1)}, bf16[32,8,640]{2,1,0:T(8,128)(2,1)S(1)}, u32[]{:S(2)}, u32[]{:S(2)}) collective-permute-start(bf16[32,8,640]{2,1,0:T(8,128)(2,1)S(1)} %all_to_all.41.got_ref.own_ref), channel_id=1, source_target_pairs={{0,8},{1,9},{2,10},{3,11},{4,12},{5,13},{6,14},{7,15},{8,0},{9,1},... | collective-permute-start | bytes 983048 | tf_op jit(solution)/shard_map/ppermute | solution.py:377
  70.1 13.4 %all_to_all.42.got_ref = bf16[16,16,128]{2,1,0:T(8,128)(2,1)S(1)} all-to-all(bf16[16,16,128]{2,1,0:T(8,128)(2,1)S(1)} %col_pass_2.1), channel_id=1, replica_groups=mesh['batch'=16,'proto'=32] {'batch'}, dimensions={0} | all-to-all | bytes 131072 | tf_op jit(solution)/shard_map/all_to_all | solution.py:336
  84.4 14.2 %all_to_all.43.got_ref = bf16[32,8,128]{2,1,0:T(8,128)(2,1)S(1)} all-to-all(bf16[32,8,128]{2,1,0:T(8,128)(2,1)S(1)} %row_pass_2.1), channel_id=1, replica_groups=mesh['batch'=16,'proto'=32] {'proto'}, dimensions={0} | all-to-all | bytes 131072 | tf_op jit(solution)/shard_map/all_to_all | solution.py:339
  99.5 13.2 %all_to_all.44.got_ref = f32[16,16,128]{2,1,0:T(8,128)S(1)} all-to-all(f32[16,16,128]{2,1,0:T(8,128)S(1)} %col_pass_3.1), channel_id=1, replica_groups=mesh['batch'=16,'proto'=32] {'batch'}, dimensions={0} | all-to-all | bytes 262144 | tf_op jit(solution)/shard_map/all_to_all | solution.py:336
  112.7 3.9 %student_and_last_row.1 = (f32[1024,2048]{1,0:T(8,128)S(1)}, f32[1024,2048]{1,0:T(8,128)S(1)}, bf16[256,1024]{1,0:T(8,128)(2,1)S(1)}, bf16[256,1024]{1,0:T(8,128...) custom-call(s32[1]{0:T(128)} %get-tuple-element.28.place_ref, ...), custom_call_target="tpu_custom_call" | custom-call | tf_op jit(solution)/shard_map/student_and_last_row/pallas_call | solution.py:49
  116.6 15.1 %all_to_all.45.got_ref = bf16[32,40,128]{2,1,0:T(8,128)(2,1)S(1)} all-to-all(bf16[32,40,128]{2,1,0:T(8,128)(2,1)S(1)} %get-tuple-element.37), channel_id=1, replica_groups=mesh['batch'=16,'proto'=32] {'proto'}, dimensions={0} | all-to-all | bytes 655360 | tf_op jit(solution)/shard_map/all_to_all | solution.py:339
  131.7 3.9 %proto_grad.1 = (bf16[1024,2048]{1,0:T(8,128)(2,1)S(1)}, f32[2,4,16,2176]{3,2,1,0:T(8,128)S(1)}, f32[2,4,16,2176]{3,2,1,0:T(8,128)S(1)}) custom-call(s32[1]{0:T(128)} %get-tuple-element.28.place_ref, f32[1024,2048]{1,0:T(8,128)S(1)} %get-tuple-element.34.weighted_ref, f32[1024,2048]{1,0:T(8,128)S(1)} %get-tuple-element.35.exp_ref, ...), custom_call_target="tpu_custom_call" | custom-call | tf_op jit(solution)/shard_map/proto_grad/pallas_call | solution.py:49
  135.6 3.8 %collective-permute-start.1 = (f32[2,4,16,2176]{3,2,1,0:T(8,128)S(1)}, f32[2,4,16,2176]{3,2,1,0:T(8,128)S(1)}, u32[]{:S(2)}, u32[]{:S(2)}) collective-permute-start(f32[2,4,16,2176]{3,2,1,0:T(8,128)S(1)} %get-tuple-element.40), channel_id=1, source_target_pairs={{0,32},{32,0},{64,96},{96,64},{128,160},{160,128},{192,224},{224,1... | collective-permute-start | bytes 3342344 | tf_op jit(solution)/shard_map/ppermute | solution.py:435
  139.5 2.2 %feat_grad.1.feat_ref = bf16[32,8,1024]{2,1,0:T(8,128)(2,1)} custom-call(bf16[1024,2048]{1,0:T(8,128)(2,1)S(1)} %get-tuple-element.41.grad_ref, bf16[256,2048]{1,0:T(8,128)(2,1)S(1)} %get-tuple-element.33.cols_ref, bf16[256,1024]{1,0:T(8,128)(2,1)S(1)} %get-tuple-element.42.raw_feat_ref, f32[1,1024]{1,0:T(1,128)S(1)} %get-tuple-element.43.feat_inv_ref), custom_call_target="tpu_custom_call" | custom-call | tf_op jit(solution)/shard_map/feat_grad/pallas_call | solution.py:436
  141.9 1.9 %collective-permute-start.2 = (bf16[4,16,2176]{2,1,0:T(8,128)(2,1)S(1)}, bf16[4,16,2176]{2,1,0:T(8,128)(2,1)S(1)}, u32[]{:S(2)}, u32[]{:S(2)}) collective-permute-start(bf16[4,16,2176]{2,1,0:T(8,128)(2,1)S(1)} %get-tuple-element.45), channel_id=1, source_target_pairs={{0,64},{32,96},{64,0},{96,32},{128,192},{160,224},{192,128},{224,1... | collective-permute-start | bytes 835592 | tf_op jit(solution)/shard_map/ppermute | solution.py:456
  143.9 5.0 %all-to-all-start.7 = ((bf16[32,8,1024]{2,1,0:T(8,128)(2,1)}), bf16[32,8,1024]{2,1,0:T(8,128)(2,1)}, u32[]{:S(2)}, u32[]{:S(2)}) async-start(bf16[32,8,1024]{2,1,0:T(8,128)(2,1)} %get-tuple-element.50), calls=%async_computation.7 | async-start | bytes 1048576 | tf_op jit(solution)/shard_map/all_to_all | solution.py:339
  148.9 2.8 %collective-permute-done.2.got_ref = bf16[4,16,2176]{2,1,0:T(8,128)(2,1)S(1)} collective-permute-done((bf16[4,16,2176]{2,1,0:T(8,128)(2,1)S(1)}, bf16[4,16,2176]{2,1,0:T(8,128)(2,1)S(1)}, u32[]{:S(2)}, u32[]{:S(2)}) %collective-permute-start.2) | collective-permute-done | bytes 278560 | tf_op jit(solution)/shard_map/ppermute | solution.py:456
  152.5 1.9 %collective-permute-start.3 = (bf16[16,2176]{1,0:T(8,128)(2,1)S(1)}, bf16[16,2176]{1,0:T(8,128)(2,1)S(1)}, u32[]{:S(2)}, u32[]{:S(2)}) collective-permute-start(bf16[16,2176]{1,0:T(8,128)(2,1)S(1)} %get-tuple-element.47), channel_id=1, source_target_pairs={{0,128},{32,160},{64,192},{96,224},{128,256},{160,288},{192,320},{... | collective-permute-start | bytes 208904 | tf_op jit(solution)/shard_map/ppermute | solution.py:467
  154.5 4.1 %collective-permute-start.4 = (bf16[16,2176]{1,0:T(8,128)(2,1)S(1)}, bf16[16,2176]{1,0:T(8,128)(2,1)S(1)}, u32[]{:S(2)}, u32[]{:S(2)}) collective-permute-start(bf16[16,2176]{1,0:T(8,128)(2,1)S(1)} %get-tuple-element.48), channel_id=1, source_target_pairs={{0,256},{32,288},{64,320},{96,352},{128,384},{160,416},{192,448},{... | collective-permute-start | bytes 208904 | tf_op jit(solution)/shard_map/ppermute | solution.py:467
  158.6 3.9 %collective-permute-start.5 = (bf16[16,2176]{1,0:T(8,128)(2,1)S(1)}, bf16[16,2176]{1,0:T(8,128)(2,1)S(1)}, u32[]{:S(2)}, u32[]{:S(2)}) collective-permute-start(bf16[16,2176]{1,0:T(8,128)(2,1)S(1)} %get-tuple-element.49), channel_id=1, source_target_pairs={{0,384},{32,416},{64,448},{96,480},{128,0},{160,32},{192,64},{224,... | collective-permute-start | bytes 208904 | tf_op jit(solution)/shard_map/ppermute | solution.py:467
  163.3 1.7 %feat_sum.1.after_ref = f32[8,1024]{1,0:T(8,128)} custom-call(bf16[32,8,1024]{2,1,0:T(8,128)(2,1)} %all-to-all-done.7.feat_ref), custom_call_target="tpu_custom_call" | custom-call | tf_op jit(solution)/shard_map/feat_sum/pallas_call | solution.py:49
  165.0 4.2 %collective-permute-done.5.third_ref = bf16[16,2176]{1,0:T(8,128)(2,1)S(1)} collective-permute-done((bf16[16,2176]{1,0:T(8,128)(2,1)S(1)}, bf16[16,2176]{1,0:T(8,128)(2,1)S(1)}, u32[]{:S(2)}, u32[]{:S(2)}) %collective-permute-start.5) | collective-permute-done | bytes 69664 | tf_op jit(solution)/shard_map/ppermute | solution.py:467
  (20 shorter events, 8.7 us)
Async XLA Ops:
  0.6 49.3 %copy-start.3 = (bf16[1024,8]{0,1:T(8,128)(2,1)S(1)}, bf16[1024,8]{0,1:T(8,128)(2,1)}, u32[]{:S(2)}) copy-start(bf16[1024,8]{0,1:T(8,128)(2,1)} %param.4) | copy-start | bytes 49156
  2.2 24.8 %all-to-all-start = ((bf16[32,8,1024]{2,1,0:T(8,128)(2,1)}), bf16[32,8,1024]{2,1,0:T(8,128)(2,1)S(1)}, u32[]{:S(2)}, u32[]{:S(2)}) async-start(bf16[32,8,1024]{2,1,0:T(8,128)(2,1)} %get-tuple-element.29), calls=%async_computation | async-start | bytes 1048576 | tf_op jit(solution)/shard_map/all_to_all | solution.py:339
  12.8 1.2 copy-start
  14.0 1.2 copy-start.1
  66.6 16.9 %collective-permute-start = (bf16[32,8,640]{2,1,0:T(8,128)(2,1)S(1)}, bf16[32,8,640]{2,1,0:T(8,128)(2,1)S(1)}, u32[]{:S(2)}, u32[]{:S(2)}) collective-permute-start(bf16[32,8,640]{2,1,0:T(8,128)(2,1)S(1)} %all_to_all.41.got_ref.own_ref), channel_id=1, source_target_pairs={{0,8},{1,9},{2,10},{3,11},{4,12},{5,13},{6,14},{7,15},{8,0},{9,1},... | collective-permute-start | bytes 983048 | tf_op jit(solution)/shard_map/ppermute | solution.py:377
  135.6 6.2 %collective-permute-start.1 = (f32[2,4,16,2176]{3,2,1,0:T(8,128)S(1)}, f32[2,4,16,2176]{3,2,1,0:T(8,128)S(1)}, u32[]{:S(2)}, u32[]{:S(2)}) collective-permute-start(f32[2,4,16,2176]{3,2,1,0:T(8,128)S(1)} %get-tuple-element.40), channel_id=1, source_target_pairs={{0,32},{32,0},{64,96},{96,64},{128,160},{160,128},{192,224},{224,1... | collective-permute-start | bytes 3342344 | tf_op jit(solution)/shard_map/ppermute | solution.py:435
  141.9 9.8 %collective-permute-start.2 = (bf16[4,16,2176]{2,1,0:T(8,128)(2,1)S(1)}, bf16[4,16,2176]{2,1,0:T(8,128)(2,1)S(1)}, u32[]{:S(2)}, u32[]{:S(2)}) collective-permute-start(bf16[4,16,2176]{2,1,0:T(8,128)(2,1)S(1)} %get-tuple-element.45), channel_id=1, source_target_pairs={{0,64},{32,96},{64,0},{96,32},{128,192},{160,224},{192,128},{224,1... | collective-permute-start | bytes 835592 | tf_op jit(solution)/shard_map/ppermute | solution.py:456
  143.9 19.4 %all-to-all-start.7 = ((bf16[32,8,1024]{2,1,0:T(8,128)(2,1)}), bf16[32,8,1024]{2,1,0:T(8,128)(2,1)}, u32[]{:S(2)}, u32[]{:S(2)}) async-start(bf16[32,8,1024]{2,1,0:T(8,128)(2,1)} %get-tuple-element.50), calls=%async_computation.7 | async-start | bytes 1048576 | tf_op jit(solution)/shard_map/all_to_all | solution.py:339
  152.5 12.5 %collective-permute-start.3 = (bf16[16,2176]{1,0:T(8,128)(2,1)S(1)}, bf16[16,2176]{1,0:T(8,128)(2,1)S(1)}, u32[]{:S(2)}, u32[]{:S(2)}) collective-permute-start(bf16[16,2176]{1,0:T(8,128)(2,1)S(1)} %get-tuple-element.47), channel_id=1, source_target_pairs={{0,128},{32,160},{64,192},{96,224},{128,256},{160,288},{192,320},{... | collective-permute-start | bytes 208904 | tf_op jit(solution)/shard_map/ppermute | solution.py:467
  154.5 10.6 %collective-permute-start.4 = (bf16[16,2176]{1,0:T(8,128)(2,1)S(1)}, bf16[16,2176]{1,0:T(8,128)(2,1)S(1)}, u32[]{:S(2)}, u32[]{:S(2)}) collective-permute-start(bf16[16,2176]{1,0:T(8,128)(2,1)S(1)} %get-tuple-element.48), channel_id=1, source_target_pairs={{0,256},{32,288},{64,320},{96,352},{128,384},{160,416},{192,448},{... | collective-permute-start | bytes 208904 | tf_op jit(solution)/shard_map/ppermute | solution.py:467
  158.6 10.7 %collective-permute-start.5 = (bf16[16,2176]{1,0:T(8,128)(2,1)S(1)}, bf16[16,2176]{1,0:T(8,128)(2,1)S(1)}, u32[]{:S(2)}, u32[]{:S(2)}) collective-permute-start(bf16[16,2176]{1,0:T(8,128)(2,1)S(1)} %get-tuple-element.49), channel_id=1, source_target_pairs={{0,384},{32,416},{64,448},{96,480},{128,0},{160,32},{192,64},{224,... | collective-permute-start | bytes 208904 | tf_op jit(solution)/shard_map/ppermute | solution.py:467
  169.3 0.8 copy-start.2

commit v6 on v5

--- a/solution.py
+++ b/solution.py
@@ -25,7 +25,6 @@
 LONG = 200_000_000_000
 
 VM = pl.BlockSpec(memory_space=pltpu.VMEM)
-SM = pl.BlockSpec(memory_space=pltpu.SMEM)
 ANY = pl.BlockSpec(memory_space=pl.ANY)
 
 
@@ -70,8 +69,7 @@
         out_ref[LANES * j : LANES * (j + 1), :] = jnp.broadcast_to(values[j : j + 1, :], (LANES, LANES)).T
 
 
-def prepare_kernel(place_ref, teach_ref, teach_out, place_out):
-    place_out[0] = place_ref[0]
+def prepare_kernel(teach_ref, teach_out):
     put(teach_out, teach_ref[...])
 
 
@@ -168,11 +166,11 @@
 
 
 def student_kernel(
-    place_ref, own_ref, other_ref, teacher_ref, cols_ref, got_ref, exp_ref, weighted_ref, raw_feat_ref, feat_out_ref, feat_inv_ref,
+    own_ref, other_ref, teacher_ref, cols_ref, got_ref, exp_ref, weighted_ref, raw_feat_ref, feat_out_ref, feat_inv_ref,
     out_ref, rows_ref, scale_ref, part_ref, cross_ref, total_ref, sum_ref,
 ):
     scale_ref[...] = col_scale_of(got_ref)
-    side = lax.rem(lax.div(place_ref[0], SIDE), 2)
+    side = lax.rem(lax.div(lax.axis_index("proto"), SIDE), 2)
     for half in range(2):
         lanes = slice(HALF * half, HALF * (half + 1))
         own, other = own_ref[:, :, :HALF].astype(F32), other_ref[:, :, :HALF].astype(F32)
@@ -212,10 +210,10 @@
 
 
 def grad_kernel(
-    place_ref, weighted_ref, exp_ref, feat_ref, got_ref, source_ref, cols_inv_ref,
+    weighted_ref, exp_ref, feat_ref, got_ref, source_ref, cols_inv_ref,
     grad_ref, own_ref, other_ref, target_ref, soft_ref, order_ref, raw_cols_ref, sems,
 ):
-    batch = lax.div(place_ref[0], PROTO)
+    batch = lax.axis_index("batch")
     core, odd = lax.rem(batch, 2), lax.rem(lax.div(batch, 2), 2)
     fetches = []
     for away in range(2):
@@ -263,16 +261,19 @@
 
 def feat_grad_kernel(grad_ref, cols_ref, raw_feat_ref, feat_inv_ref, out_ref, stage_ref, sems):
     copies = []
-    for quarter in range(4):
-        lanes = slice(QUARTER * quarter, QUARTER * (quarter + 1))
-        part = lax.dot_general(
-            cols_ref[...], grad_ref[lanes, :], (((1,), (1,)), ((), ())), preferred_element_type=F32
-        )
-        unit = raw_feat_ref[:, lanes].astype(F32) * feat_inv_ref[:, lanes]
-        part = part - unit * jnp.sum(unit * part, axis=0, keepdims=True)
-        stage_ref[quarter] = part.reshape(PROTO, 8, QUARTER).astype(BF16)
-        there = out_ref.at[:, :, pl.ds(QUARTER * quarter, QUARTER)]
-        copies.append(pltpu.make_async_copy(stage_ref.at[quarter], there, sems.at[quarter]))
+    for side in range(2):
+        parts = []
+        for half in range(2):
+            lanes = slice(HALF * half + QUARTER * side, HALF * half + QUARTER * (side + 1))
+            part = lax.dot_general(
+                cols_ref[...], grad_ref[lanes, :], (((1,), (1,)), ((), ())), preferred_element_type=F32
+            )
+            unit = raw_feat_ref[:, lanes].astype(F32) * feat_inv_ref[:, lanes]
+            part = part - unit * jnp.sum(unit * part, axis=0, keepdims=True)
+            parts.append(part.reshape(PROTO, 8, QUARTER))
+        stage_ref[side] = jnp.concatenate(parts, axis=1).astype(BF16)
+        there = out_ref.at[:, :, pl.ds(QUARTER * side, QUARTER)]
+        copies.append(pltpu.make_async_copy(stage_ref.at[side], there, sems.at[side]))
         copies[-1].start()
     for copy in copies:
         copy.wait()
@@ -296,8 +297,8 @@
     send_ref[:, :, COLS:] = spread(away[:, :, COLS:])
 
 
-def join_pairs_kernel(place_ref, own_ref, got_ref, keep_ref, *send_refs):
-    pair = lax.div(lax.div(place_ref[0], PROTO), 4)
+def join_pairs_kernel(own_ref, got_ref, keep_ref, *send_refs):
+    pair = lax.div(lax.axis_index("batch"), 4)
     for away in range(PAIRS):
         there = lax.rem(pair + away, PAIRS)
         got = got_ref[there].astype(F32)
@@ -312,7 +313,9 @@
 
 
 def feat_sum_kernel(feat_ref, feat_out_ref):
-    feat_out_ref[...] = jnp.sum(feat_ref[...].astype(F32), axis=0)
+    total = jnp.sum(feat_ref[...].astype(F32), axis=0)
+    feat_out_ref[:, :HALF] = total[:8]
+    feat_out_ref[:, HALF:] = total[8:]
 
 
 def proto_sum_kernel(keep_ref, first_ref, second_ref, third_ref, after_ref, proto_out_ref, loss_ref):
@@ -327,7 +330,6 @@
 
 
 def per_device(student_feat, teacher_feat, student_proto, teacher_proto):
-    place = (lax.axis_index("batch") * PROTO + lax.axis_index("proto")).astype(jnp.int32).reshape(1)
     swap_cores = [(i, i ^ 1) for i in range(BATCH)]
     swap_pairs = [(i, i ^ 2) for i in range(BATCH)]
     swap_sides = [(i, i ^ SIDE) for i in range(PROTO)]
@@ -338,7 +340,7 @@
     def over_proto(array):
         return lax.all_to_all(array, "proto", 0, 0)
 
-    packed = shape((PROTO, 8, ROWS), BF16)
+    packed, halved = shape((PROTO, 8, ROWS), BF16), shape((PROTO, 16, HALF), BF16)
     rounded = shape((D, COLS), BF16)
     row_shape = shape((PROTO, ROW_TILES, LANES), BF16)
     first_row_shape = shape((PROTO, ROW_TILES, HALF + LANES), BF16)
@@ -347,13 +349,7 @@
     row_tile, row_part = pltpu.VMEM((ROW_TILES, LANES), F32), pltpu.VMEM((ROWS, LANES), F32)
     col_tile, col_part = pltpu.VMEM((COL_TILES, LANES), F32), pltpu.VMEM((8, COLS), F32)
 
-    send, place = pl.pallas_call(
-        prepare_kernel,
-        out_shape=[packed, shape((1,), jnp.int32)],
-        in_specs=[SM, VM],
-        out_specs=[VM, SM],
-        name="prepare",
-    )(place, teacher_feat.T)
+    (send,) = call(prepare_kernel, [packed], [teacher_feat.T], name="prepare")
     teach = over_proto(send)
     teacher_cols, proto_round, proto_inv = call(
         unit_cols_kernel, [rounded, rounded, shape((1, COLS))], [teacher_proto, student_proto], name="unit_cols"
@@ -400,9 +396,8 @@
             shape((1, ROWS)),
             last_shape,
         ],
-        [place, own_half, other_half, pin(teacher_exp), proto_round, got],
+        [own_half, other_half, pin(teacher_exp), proto_round, got],
         [pltpu.VMEM((ROWS, D), BF16), col_tile, row_part, row_part, row_part, row_tile],
-        specs=[SM] + [VM] * 5,
         name="student_and_last_row",
     )
     got = over_proto(send)
@@ -413,7 +408,6 @@
         grad_kernel,
         [pinned((ROWS, COLS), BF16), half_shape, half_shape],
         [
-            place,
             pin(weighted),
             pin(student_exp),
             feat_round.reshape(split + (ROWS,)),
@@ -428,24 +422,24 @@
             pltpu.VMEM(order + (COLS,), BF16),
             pltpu.SemaphoreType.DMA((4,)),
         ],
-        specs=[SM] + [VM] * 4 + [ANY, VM],
+        specs=[VM] * 4 + [ANY, VM],
         vmem=16,
         name="proto_grad",
     )
     arrived = lax.ppermute(other, "batch", swap_cores)
     feat_part = pl.pallas_call(
         feat_grad_kernel,
-        out_shape=packed,
+        out_shape=halved,
         in_specs=[VM] * 4,
         out_specs=ANY,
-        scratch_shapes=[pltpu.VMEM((4, PROTO, 8, QUARTER), BF16), pltpu.SemaphoreType.DMA((4,))],
+        scratch_shapes=[pltpu.VMEM((2, PROTO, 16, QUARTER), BF16), pltpu.SemaphoreType.DMA((2,))],
         compiler_params=pltpu.CompilerParams(vmem_limit_bytes=12 * MIB),
         name="feat_grad",
     )(pin(grad_logit), proto_round, raw_feat, feat_inv)
     pair_shape = (PAIRS, D // BATCH, COLS + LANES)
     keep, send, feat_part = pl.pallas_call(
         join_cores_kernel,
-        out_shape=[shape(pair_shape), shape(pair_shape, BF16), packed],
+        out_shape=[shape(pair_shape), shape(pair_shape, BF16), halved],
         in_specs=[VM, VM, ANY],
         out_specs=[VM, VM, ANY],
         input_output_aliases={2: 2},
@@ -458,8 +452,7 @@
     keep, *sends = call(
         join_pairs_kernel,
         [shape(block)] + [shape(block, BF16)] * (PAIRS - 1),
-        [place, keep, arrived],
-        specs=[SM, VM, VM],
+        [keep, arrived],
         flops=LONG,
         name="join_pairs",
     )

time: 172 us -> 170 us (0.988)
  Pallas kernels: 20.5 us -> 18.2 us
    pallas_call x2 -> x1, Pallas kernels: 3.78 us -> 2.17 us  [per_device(): pl.pallas_call(feat_grad_kernel, out_shape=halved, in_specs=[VM] * 4, out...]
    unnamed x8 -> x10, local copies, waits for them, and re-layouts: 3.21 us -> 3.92 us
    pallas_call x11 -> x12, Pallas kernels: 16.6 us -> 15.9 us  [call(): pl.pallas_call(body, out_shape=outs, in_specs=specs or [VM] * len(args),...]
  transfers between devices with their start and end apart: 8 -> 8, of which waited for: 5 -> 5; matrix products, arithmetic and copies ran while one was open for 0% -> 0% of each run, Pallas kernels for 4% -> 3%
where the time goes in v6:
time: 170 us; the launch traced here: 169 us
  blocking collectives  93.3 us (55%)
  starting transfers between devices  33.8 us (20%)
  waiting for transfers between devices  19.2 us (11%)
  Pallas kernels  18.2 us (11%)
  local copies, waits for them, and re-layouts  3.92 us (2%)
    all_to_all x3, blocking collectives, over_batch(): return lax.all_to_all(array, 'batch', 0, 0)  48.1 us
    all_to_all x3, blocking collectives, over_proto(): return lax.all_to_all(array, 'proto', 0, 0)  45.2 us
    pallas_call x12, Pallas kernels, call(): pl.pallas_call(body, out_shape=outs, in_specs=specs or [VM] * len(args),...  15.9 us
    all_to_all x2, starting transfers between devices, over_proto(): return lax.all_to_all(array, 'proto', 0, 0)  15.5 us
    all_to_all x2, waiting for transfers between devices, over_proto(): return lax.all_to_all(array, 'proto', 0, 0)  12.6 us
    ppermute x3, starting transfers between devices, per_device(): lax.ppermute(send, 'batch', [(i, (i + 4 * away) % BATCH) for i in range(B...  9.96 us
    unnamed x10, local copies, waits for them, and re-layouts  3.92 us
    ppermute x1, starting transfers between devices, per_device(): arrived = lax.ppermute(other, 'batch', swap_cores)  3.83 us
  transfers between devices with their start and end apart: 8, of which 5 were waited for; matrix products, arithmetic and copies ran while one was open for 0% of the time, Pallas kernels for 3%

profile of v6, /device:TPU:1, one launch (start us, length us, event | category | flops | bytes accessed | tf_op | source)
XLA Modules:
  0.0 169.2 jit_solution(16597588305135321024)
XLA Ops:
  2.2 10.5 %all-to-all-start = ((bf16[32,8,1024]{2,1,0:T(8,128)(2,1)}), bf16[32,8,1024]{2,1,0:T(8,128)(2,1)S(1)}, u32[]{:S(2)}, u32[]{:S(2)}) async-start(bf16[32,8,1024]{2,1,0:T(8,128)(2,1)} %prepare.1), calls=%async_computation | async-start | bytes 1048576 | tf_op jit(solution)/shard_map/all_to_all | solution.py:341
  14.0 1.2 copy-done.1
  15.9 11.2 %all-to-all-done.feat_ref = bf16[32,8,1024]{2,1,0:T(8,128)(2,1)S(1)} async-done(((bf16[32,8,1024]{2,1,0:T(8,128)(2,1)}), bf16[32,8,1024]{2,1,0:T(8,128)(2,1)S(1)}, u32[]{:S(2)}, u32[]{:S(2)}) %all-to-all-start) | async-done | bytes 524320 | tf_op jit(solution)/shard_map/all_to_all | solution.py:341
  27.0 1.4 teacher_exp.1
  28.4 21.4 %all_to_all.40.got_ref = bf16[16,16,128]{2,1,0:T(8,128)(2,1)S(1)} all-to-all(bf16[16,16,128]{2,1,0:T(8,128)(2,1)S(1)} %get-tuple-element.28), channel_id=1, replica_groups=mesh['batch'=16,'proto'=32] {'batch'}, dimensions={0} | all-to-all | bytes 131072 | tf_op jit(solution)/shard_map/all_to_all | solution.py:338
  50.7 15.9 %all_to_all.41.got_ref.own_ref = bf16[32,8,640]{2,1,0:T(8,128)(2,1)S(1)} all-to-all(bf16[32,8,640]{2,1,0:T(8,128)(2,1)S(1)} %row_pass_1.1), channel_id=1, replica_groups=mesh['batch'=16,'proto'=32] {'proto'}, dimensions={0} | all-to-all | bytes 655360 | tf_op jit(solution)/shard_map/all_to_all | solution.py:341
  66.6 2.6 %collective-permute-start = (bf16[32,8,640]{2,1,0:T(8,128)(2,1)S(1)}, bf16[32,8,640]{2,1,0:T(8,128)(2,1)S(1)}, u32[]{:S(2)}, u32[]{:S(2)}) collective-permute-start(bf16[32,8,640]{2,1,0:T(8,128)(2,1)S(1)} %all_to_all.41.got_ref.own_ref), channel_id=1, source_target_pairs={{0,8},{1,9},{2,10},{3,11},{4,12},{5,13},{6,14},{7,15},{8,0},{9,1},... | collective-permute-start | bytes 983048 | tf_op jit(solution)/shard_map/ppermute | solution.py:373
  70.2 13.4 %all_to_all.42.got_ref = bf16[16,16,128]{2,1,0:T(8,128)(2,1)S(1)} all-to-all(bf16[16,16,128]{2,1,0:T(8,128)(2,1)S(1)} %col_pass_2.1), channel_id=1, replica_groups=mesh['batch'=16,'proto'=32] {'batch'}, dimensions={0} | all-to-all | bytes 131072 | tf_op jit(solution)/shard_map/all_to_all | solution.py:338
  84.5 14.2 %all_to_all.43.got_ref = bf16[32,8,128]{2,1,0:T(8,128)(2,1)S(1)} all-to-all(bf16[32,8,128]{2,1,0:T(8,128)(2,1)S(1)} %row_pass_2.1), channel_id=1, replica_groups=mesh['batch'=16,'proto'=32] {'proto'}, dimensions={0} | all-to-all | bytes 131072 | tf_op jit(solution)/shard_map/all_to_all | solution.py:341
  99.7 13.2 %all_to_all.44.got_ref = f32[16,16,128]{2,1,0:T(8,128)S(1)} all-to-all(f32[16,16,128]{2,1,0:T(8,128)S(1)} %col_pass_3.1), channel_id=1, replica_groups=mesh['batch'=16,'proto'=32] {'batch'}, dimensions={0} | all-to-all | bytes 262144 | tf_op jit(solution)/shard_map/all_to_all | solution.py:338
  112.9 3.3 %student_and_last_row.1 = (f32[1024,2048]{1,0:T(8,128)S(1)}, f32[1024,2048]{1,0:T(8,128)S(1)}, bf16[256,1024]{1,0:T(8,128)(2,1)S(1)}, bf16[256,1024]{1,0:T(8,128...) custom-call(bf16[32,8,640]{2,1,0:T(8,128)(2,1)S(1)} %all_to_all.41.got_ref.own_ref, ...), custom_call_target="tpu_custom_call" | custom-call | tf_op jit(solution)/shard_map/student_and_last_row/pallas_call | solution.py:48
  116.2 15.1 %all_to_all.45.got_ref = bf16[32,40,128]{2,1,0:T(8,128)(2,1)S(1)} all-to-all(bf16[32,40,128]{2,1,0:T(8,128)(2,1)S(1)} %get-tuple-element.33), channel_id=1, replica_groups=mesh['batch'=16,'proto'=32] {'proto'}, dimensions={0} | all-to-all | bytes 655360 | tf_op jit(solution)/shard_map/all_to_all | solution.py:341
  131.3 3.4 %proto_grad.1 = (bf16[1024,2048]{1,0:T(8,128)(2,1)S(1)}, f32[2,4,16,2176]{3,2,1,0:T(8,128)S(1)}, f32[2,4,16,2176]{3,2,1,0:T(8,128)S(1)}) custom-call(f32[1024,2048]{1,0:T(8,128)S(1)} %get-tuple-element.30.weighted_ref, f32[1024,2048]{1,0:T(8,128)S(1)} %get-tuple-element.31.exp_ref, bf16[4,2,2,16,1024]{4,3,2,1,0:T(8,128)(2,1)S(1)} %bitcast.7, ...), custom_call_target="tpu_custom_call" | custom-call | tf_op jit(solution)/shard_map/proto_grad/pallas_call | solution.py:48
  134.7 3.8 %collective-permute-start.1 = (f32[2,4,16,2176]{3,2,1,0:T(8,128)S(1)}, f32[2,4,16,2176]{3,2,1,0:T(8,128)S(1)}, u32[]{:S(2)}, u32[]{:S(2)}) collective-permute-start(f32[2,4,16,2176]{3,2,1,0:T(8,128)S(1)} %get-tuple-element.36), channel_id=1, source_target_pairs={{0,32},{32,0},{64,96},{96,64},{128,160},{160,128},{192,224},{224,1... | collective-permute-start | bytes 3342344 | tf_op jit(solution)/shard_map/ppermute | solution.py:429
  138.6 2.2 %feat_grad.1.feat_ref = bf16[32,16,512]{2,1,0:T(8,128)(2,1)} custom-call(bf16[1024,2048]{1,0:T(8,128)(2,1)S(1)} %get-tuple-element.37.grad_ref, bf16[256,2048]{1,0:T(8,128)(2,1)S(1)} %get-tuple-element.29.cols_ref, bf16[256,1024]{1,0:T(8,128)(2,1)S(1)} %get-tuple-element.38.raw_feat_ref, f32[1,1024]{1,0:T(1,128)S(1)} %get-tuple-element.39.feat_inv_ref), custom_call_target="tpu_custom_call" | custom-call | tf_op jit(solution)/shard_map/feat_grad/pallas_call | solution.py:430
  141.1 1.9 %collective-permute-start.2 = (bf16[4,16,2176]{2,1,0:T(8,128)(2,1)S(1)}, bf16[4,16,2176]{2,1,0:T(8,128)(2,1)S(1)}, u32[]{:S(2)}, u32[]{:S(2)}) collective-permute-start(bf16[4,16,2176]{2,1,0:T(8,128)(2,1)S(1)} %get-tuple-element.41), channel_id=1, source_target_pairs={{0,64},{32,96},{64,0},{96,32},{128,192},{160,224},{192,128},{224,1... | collective-permute-start | bytes 835592 | tf_op jit(solution)/shard_map/ppermute | solution.py:450
  143.0 5.0 %all-to-all-start.7 = ((bf16[32,16,512]{2,1,0:T(8,128)(2,1)}), bf16[32,16,512]{2,1,0:T(8,128)(2,1)}, u32[]{:S(2)}, u32[]{:S(2)}) async-start(bf16[32,16,512]{2,1,0:T(8,128)(2,1)} %get-tuple-element.46), calls=%async_computation.7 | async-start | bytes 1048576 | tf_op jit(solution)/shard_map/all_to_all | solution.py:341
  148.1 2.8 %collective-permute-done.2.got_ref = bf16[4,16,2176]{2,1,0:T(8,128)(2,1)S(1)} collective-permute-done((bf16[4,16,2176]{2,1,0:T(8,128)(2,1)S(1)}, bf16[4,16,2176]{2,1,0:T(8,128)(2,1)S(1)}, u32[]{:S(2)}, u32[]{:S(2)}) %collective-permute-start.2) | collective-permute-done | bytes 278560 | tf_op jit(solution)/shard_map/ppermute | solution.py:450
  151.0 1.9 %collective-permute-start.3 = (bf16[16,2176]{1,0:T(8,128)(2,1)S(1)}, bf16[16,2176]{1,0:T(8,128)(2,1)S(1)}, u32[]{:S(2)}, u32[]{:S(2)}) collective-permute-start(bf16[16,2176]{1,0:T(8,128)(2,1)S(1)} %get-tuple-element.43), channel_id=1, source_target_pairs={{0,128},{32,160},{64,192},{96,224},{128,256},{160,288},{192,320},{... | collective-permute-start | bytes 208904 | tf_op jit(solution)/shard_map/ppermute | solution.py:460
  153.0 4.1 %collective-permute-start.4 = (bf16[16,2176]{1,0:T(8,128)(2,1)S(1)}, bf16[16,2176]{1,0:T(8,128)(2,1)S(1)}, u32[]{:S(2)}, u32[]{:S(2)}) collective-permute-start(bf16[16,2176]{1,0:T(8,128)(2,1)S(1)} %get-tuple-element.44), channel_id=1, source_target_pairs={{0,256},{32,288},{64,320},{96,352},{128,384},{160,416},{192,448},{... | collective-permute-start | bytes 208904 | tf_op jit(solution)/shard_map/ppermute | solution.py:460
  157.1 3.9 %collective-permute-start.5 = (bf16[16,2176]{1,0:T(8,128)(2,1)S(1)}, bf16[16,2176]{1,0:T(8,128)(2,1)S(1)}, u32[]{:S(2)}, u32[]{:S(2)}) collective-permute-start(bf16[16,2176]{1,0:T(8,128)(2,1)S(1)} %get-tuple-element.45), channel_id=1, source_target_pairs={{0,384},{32,416},{64,448},{96,480},{128,0},{160,32},{192,64},{224,... | collective-permute-start | bytes 208904 | tf_op jit(solution)/shard_map/ppermute | solution.py:460
  161.0 1.4 all-to-all-done.7.feat_ref
  162.4 1.7 %feat_sum.1.after_ref = f32[8,1024]{1,0:T(8,128)} custom-call(bf16[32,16,512]{2,1,0:T(8,128)(2,1)} %all-to-all-done.7.feat_ref), custom_call_target="tpu_custom_call" | custom-call | tf_op jit(solution)/shard_map/feat_sum/pallas_call | solution.py:48
  164.2 3.6 %collective-permute-done.5.third_ref = bf16[16,2176]{1,0:T(8,128)(2,1)S(1)} collective-permute-done((bf16[16,2176]{1,0:T(8,128)(2,1)S(1)}, bf16[16,2176]{1,0:T(8,128)(2,1)S(1)}, u32[]{:S(2)}, u32[]{:S(2)}) %collective-permute-start.5) | collective-permute-done | bytes 69664 | tf_op jit(solution)/shard_map/ppermute | solution.py:460
  (22 shorter events, 9.1 us)
Async XLA Ops:
  0.6 49.2 %copy-start.3 = (bf16[1024,8]{0,1:T(8,128)(2,1)S(1)}, bf16[1024,8]{0,1:T(8,128)(2,1)}, u32[]{:S(2)}) copy-start(bf16[1024,8]{0,1:T(8,128)(2,1)} %param.4) | copy-start | bytes 49156
  0.6 0.7 copy-start.4
  2.2 24.8 %all-to-all-start = ((bf16[32,8,1024]{2,1,0:T(8,128)(2,1)}), bf16[32,8,1024]{2,1,0:T(8,128)(2,1)S(1)}, u32[]{:S(2)}, u32[]{:S(2)}) async-start(bf16[32,8,1024]{2,1,0:T(8,128)(2,1)} %prepare.1), calls=%async_computation | async-start | bytes 1048576 | tf_op jit(solution)/shard_map/all_to_all | solution.py:341
  12.7 1.2 copy-start
  14.0 1.2 copy-start.1
  66.6 17.0 %collective-permute-start = (bf16[32,8,640]{2,1,0:T(8,128)(2,1)S(1)}, bf16[32,8,640]{2,1,0:T(8,128)(2,1)S(1)}, u32[]{:S(2)}, u32[]{:S(2)}) collective-permute-start(bf16[32,8,640]{2,1,0:T(8,128)(2,1)S(1)} %all_to_all.41.got_ref.own_ref), channel_id=1, source_target_pairs={{0,8},{1,9},{2,10},{3,11},{4,12},{5,13},{6,14},{7,15},{8,0},{9,1},... | collective-permute-start | bytes 983048 | tf_op jit(solution)/shard_map/ppermute | solution.py:373
  134.7 6.2 %collective-permute-start.1 = (f32[2,4,16,2176]{3,2,1,0:T(8,128)S(1)}, f32[2,4,16,2176]{3,2,1,0:T(8,128)S(1)}, u32[]{:S(2)}, u32[]{:S(2)}) collective-permute-start(f32[2,4,16,2176]{3,2,1,0:T(8,128)S(1)} %get-tuple-element.36), channel_id=1, source_target_pairs={{0,32},{32,0},{64,96},{96,64},{128,160},{160,128},{192,224},{224,1... | collective-permute-start | bytes 3342344 | tf_op jit(solution)/shard_map/ppermute | solution.py:429
  141.1 9.8 %collective-permute-start.2 = (bf16[4,16,2176]{2,1,0:T(8,128)(2,1)S(1)}, bf16[4,16,2176]{2,1,0:T(8,128)(2,1)S(1)}, u32[]{:S(2)}, u32[]{:S(2)}) collective-permute-start(bf16[4,16,2176]{2,1,0:T(8,128)(2,1)S(1)} %get-tuple-element.41), channel_id=1, source_target_pairs={{0,64},{32,96},{64,0},{96,32},{128,192},{160,224},{192,128},{224,1... | collective-permute-start | bytes 835592 | tf_op jit(solution)/shard_map/ppermute | solution.py:450
  143.0 19.4 %all-to-all-start.7 = ((bf16[32,16,512]{2,1,0:T(8,128)(2,1)}), bf16[32,16,512]{2,1,0:T(8,128)(2,1)}, u32[]{:S(2)}, u32[]{:S(2)}) async-start(bf16[32,16,512]{2,1,0:T(8,128)(2,1)} %get-tuple-element.46), calls=%async_computation.7 | async-start | bytes 1048576 | tf_op jit(solution)/shard_map/all_to_all | solution.py:341
  151.0 13.2 %collective-permute-start.3 = (bf16[16,2176]{1,0:T(8,128)(2,1)S(1)}, bf16[16,2176]{1,0:T(8,128)(2,1)S(1)}, u32[]{:S(2)}, u32[]{:S(2)}) collective-permute-start(bf16[16,2176]{1,0:T(8,128)(2,1)S(1)} %get-tuple-element.43), channel_id=1, source_target_pairs={{0,128},{32,160},{64,192},{96,224},{128,256},{160,288},{192,320},{... | collective-permute-start | bytes 208904 | tf_op jit(solution)/shard_map/ppermute | solution.py:460
  153.0 11.2 %collective-permute-start.4 = (bf16[16,2176]{1,0:T(8,128)(2,1)S(1)}, bf16[16,2176]{1,0:T(8,128)(2,1)S(1)}, u32[]{:S(2)}, u32[]{:S(2)}) collective-permute-start(bf16[16,2176]{1,0:T(8,128)(2,1)S(1)} %get-tuple-element.44), channel_id=1, source_target_pairs={{0,256},{32,288},{64,320},{96,352},{128,384},{160,416},{192,448},{... | collective-permute-start | bytes 208904 | tf_op jit(solution)/shard_map/ppermute | solution.py:460
  157.1 10.7 %collective-permute-start.5 = (bf16[16,2176]{1,0:T(8,128)(2,1)S(1)}, bf16[16,2176]{1,0:T(8,128)(2,1)S(1)}, u32[]{:S(2)}, u32[]{:S(2)}) collective-permute-start(bf16[16,2176]{1,0:T(8,128)(2,1)S(1)} %get-tuple-element.45), channel_id=1, source_target_pairs={{0,384},{32,416},{64,448},{96,480},{128,0},{160,32},{192,64},{224,... | collective-permute-start | bytes 208904 | tf_op jit(solution)/shard_map/ppermute | solution.py:460
  167.8 0.8 copy-start.2

commit v7 on v6

--- a/solution.py
+++ b/solution.py
@@ -300,7 +300,7 @@
 def join_pairs_kernel(own_ref, got_ref, keep_ref, *send_refs):
     pair = lax.div(lax.axis_index("batch"), 4)
     for away in range(PAIRS):
-        there = lax.rem(pair + away, PAIRS)
+        there = lax.bitwise_xor(pair, jnp.int32(away))
         got = got_ref[there].astype(F32)
         total = own_ref[there, :, :COLS] + got[:, :COLS]
         tail = own_ref[there, :, COLS:] + gather_parts(got[:, COLS:])
@@ -312,8 +312,15 @@
             send_refs[away - 1][:, COLS:] = spread(tail)
 
 
-def feat_sum_kernel(feat_ref, feat_out_ref):
-    total = jnp.sum(feat_ref[...].astype(F32), axis=0)
+def feat_sum_kernel(source_ref, feat_out_ref, feat_ref, sems):
+    pieces = [pl.ds(first, PROTO // 4) for first in range(0, PROTO, PROTO // 4)]
+    fetches = [pltpu.make_async_copy(source_ref.at[at], feat_ref.at[at], sems.at[i]) for i, at in enumerate(pieces)]
+    for fetch in fetches:
+        fetch.start()
+    total = jnp.zeros((16, HALF), F32)
+    for fetch, at in zip(fetches, pieces):
+        fetch.wait()
+        total += jnp.sum(feat_ref[at].astype(F32), axis=0)
     feat_out_ref[:, :HALF] = total[:8]
     feat_out_ref[:, HALF:] = total[8:]
 
@@ -457,10 +464,17 @@
         name="join_pairs",
     )
     quads = [
-        lax.ppermute(send, "batch", [(i, (i + 4 * away) % BATCH) for i in range(BATCH)])
+        lax.ppermute(send, "batch", [(i, i ^ 4 * away) for i in range(BATCH)])
         for away, send in enumerate(sends, 1)
     ]
-    (feat_out,) = call(feat_sum_kernel, [shape((8, ROWS))], [feat_got], name="feat_sum")
+    (feat_out,) = call(
+        feat_sum_kernel,
+        [shape((8, ROWS))],
+        [stay(feat_got)],
+        [pltpu.VMEM((PROTO, 16, HALF), BF16), pltpu.SemaphoreType.DMA((4,))],
+        specs=[ANY],
+        name="feat_sum",
+    )
     proto_out, loss = call(
         proto_sum_kernel,
         [shape((D // BATCH, COLS)), shape((1, 1))],

time: 170 us -> 169 us (level)
  the two profiles are of different devices: /device:TPU:1 before, /device:TPU:8 now
where the time goes in v7:
time: 169 us
  blocking collectives  91.4 us (54%)
  starting transfers between devices  33.8 us (20%)
  waiting for transfers between devices  20.3 us (12%)
  Pallas kernels  18.2 us (11%)
  local copies, waits for them, and re-layouts  3.92 us (2%)
    all_to_all x3, blocking collectives, over_proto(): return lax.all_to_all(array, 'proto', 0, 0)  51.6 us
    all_to_all x3, blocking collectives, over_batch(): return lax.all_to_all(array, 'batch', 0, 0)  39.8 us
    all_to_all x2, waiting for transfers between devices, over_proto(): return lax.all_to_all(array, 'proto', 0, 0)  16.2 us
    pallas_call x12, Pallas kernels, call(): pl.pallas_call(body, out_shape=outs, in_specs=specs or [VM] * len(args),...  15.9 us
    all_to_all x2, starting transfers between devices, over_proto(): return lax.all_to_all(array, 'proto', 0, 0)  14.9 us
    ppermute x3, starting transfers between devices, per_device(): lax.ppermute(send, 'batch', [(i, i ^ 4 * away) for i in range(BATCH)])  12.2 us
    unnamed x10, local copies, waits for them, and re-layouts  3.92 us
    ppermute x1, waiting for transfers between devices, per_device(): arrived = lax.ppermute(send, 'batch', swap_pairs)  3.56 us
  transfers between devices with their start and end apart: 8, of which 4 were waited for; matrix products, arithmetic and copies ran while one was open for 0% of the time, Pallas kernels for 3%

profile of v7, /device:TPU:8, one launch (start us, length us, event | category | flops | bytes accessed | tf_op | source)
XLA Modules:
  0.0 168.6 jit_solution(8886952974921481621)
XLA Ops:
  2.2 10.2 %all-to-all-start = ((bf16[32,8,1024]{2,1,0:T(8,128)(2,1)}), bf16[32,8,1024]{2,1,0:T(8,128)(2,1)S(1)}, u32[]{:S(2)}, u32[]{:S(2)}) async-start(bf16[32,8,1024]{2,1,0:T(8,128)(2,1)} %prepare.1), calls=%async_computation | async-start | bytes 1048576 | tf_op jit(solution)/shard_map/all_to_all | solution.py:348
  12.4 1.2 copy-done
  13.6 1.2 copy-done.1
  15.6 14.5 %all-to-all-done.feat_ref = bf16[32,8,1024]{2,1,0:T(8,128)(2,1)S(1)} async-done(((bf16[32,8,1024]{2,1,0:T(8,128)(2,1)}), bf16[32,8,1024]{2,1,0:T(8,128)(2,1)S(1)}, u32[]{:S(2)}, u32[]{:S(2)}) %all-to-all-start) | async-done | bytes 524320 | tf_op jit(solution)/shard_map/all_to_all | solution.py:348
  30.0 1.4 teacher_exp.1
  31.4 18.1 %all_to_all.40.got_ref = bf16[16,16,128]{2,1,0:T(8,128)(2,1)S(1)} all-to-all(bf16[16,16,128]{2,1,0:T(8,128)(2,1)S(1)} %get-tuple-element.28), channel_id=1, replica_groups=mesh['batch'=16,'proto'=32] {'batch'}, dimensions={0} | all-to-all | bytes 131072 | tf_op jit(solution)/shard_map/all_to_all | solution.py:345
  50.4 18.8 %all_to_all.41.got_ref.own_ref = bf16[32,8,640]{2,1,0:T(8,128)(2,1)S(1)} all-to-all(bf16[32,8,640]{2,1,0:T(8,128)(2,1)S(1)} %row_pass_1.1), channel_id=1, replica_groups=mesh['batch'=16,'proto'=32] {'proto'}, dimensions={0} | all-to-all | bytes 655360 | tf_op jit(solution)/shard_map/all_to_all | solution.py:348
  69.1 2.5 %collective-permute-start = (bf16[32,8,640]{2,1,0:T(8,128)(2,1)S(1)}, bf16[32,8,640]{2,1,0:T(8,128)(2,1)S(1)}, u32[]{:S(2)}, u32[]{:S(2)}) collective-permute-start(bf16[32,8,640]{2,1,0:T(8,128)(2,1)S(1)} %all_to_all.41.got_ref.own_ref), channel_id=1, source_target_pairs={{0,8},{1,9},{2,10},{3,11},{4,12},{5,13},{6,14},{7,15},{8,0},{9,1},... | collective-permute-start | bytes 983048 | tf_op jit(solution)/shard_map/ppermute | solution.py:380
  72.6 10.4 %all_to_all.42.got_ref = bf16[16,16,128]{2,1,0:T(8,128)(2,1)S(1)} all-to-all(bf16[16,16,128]{2,1,0:T(8,128)(2,1)S(1)} %col_pass_2.1), channel_id=1, replica_groups=mesh['batch'=16,'proto'=32] {'batch'}, dimensions={0} | all-to-all | bytes 131072 | tf_op jit(solution)/shard_map/all_to_all | solution.py:345
  83.9 14.3 %all_to_all.43.got_ref = bf16[32,8,128]{2,1,0:T(8,128)(2,1)S(1)} all-to-all(bf16[32,8,128]{2,1,0:T(8,128)(2,1)S(1)} %row_pass_2.1), channel_id=1, replica_groups=mesh['batch'=16,'proto'=32] {'proto'}, dimensions={0} | all-to-all | bytes 131072 | tf_op jit(solution)/shard_map/all_to_all | solution.py:348
  99.2 11.3 %all_to_all.44.got_ref = f32[16,16,128]{2,1,0:T(8,128)S(1)} all-to-all(f32[16,16,128]{2,1,0:T(8,128)S(1)} %col_pass_3.1), channel_id=1, replica_groups=mesh['batch'=16,'proto'=32] {'batch'}, dimensions={0} | all-to-all | bytes 262144 | tf_op jit(solution)/shard_map/all_to_all | solution.py:345
  110.5 3.3 %student_and_last_row.1 = (f32[1024,2048]{1,0:T(8,128)S(1)}, f32[1024,2048]{1,0:T(8,128)S(1)}, bf16[256,1024]{1,0:T(8,128)(2,1)S(1)}, bf16[256,1024]{1,0:T(8,128...) custom-call(bf16[32,8,640]{2,1,0:T(8,128)(2,1)S(1)} %all_to_all.41.got_ref.own_ref, ...), custom_call_target="tpu_custom_call" | custom-call | tf_op jit(solution)/shard_map/student_and_last_row/pallas_call | solution.py:48
  113.8 18.5 %all_to_all.45.got_ref = bf16[32,40,128]{2,1,0:T(8,128)(2,1)S(1)} all-to-all(bf16[32,40,128]{2,1,0:T(8,128)(2,1)S(1)} %get-tuple-element.33), channel_id=1, replica_groups=mesh['batch'=16,'proto'=32] {'proto'}, dimensions={0} | all-to-all | bytes 655360 | tf_op jit(solution)/shard_map/all_to_all | solution.py:348
  132.3 3.4 %proto_grad.1 = (bf16[1024,2048]{1,0:T(8,128)(2,1)S(1)}, f32[2,4,16,2176]{3,2,1,0:T(8,128)S(1)}, f32[2,4,16,2176]{3,2,1,0:T(8,128)S(1)}) custom-call(f32[1024,2048]{1,0:T(8,128)S(1)} %get-tuple-element.30.weighted_ref, f32[1024,2048]{1,0:T(8,128)S(1)} %get-tuple-element.31.exp_ref, bf16[4,2,2,16,1024]{4,3,2,1,0:T(8,128)(2,1)S(1)} %bitcast.7, ...), custom_call_target="tpu_custom_call" | custom-call | tf_op jit(solution)/shard_map/proto_grad/pallas_call | solution.py:48
  135.7 1.9 %collective-permute-start.1 = (f32[2,4,16,2176]{3,2,1,0:T(8,128)S(1)}, f32[2,4,16,2176]{3,2,1,0:T(8,128)S(1)}, u32[]{:S(2)}, u32[]{:S(2)}) collective-permute-start(f32[2,4,16,2176]{3,2,1,0:T(8,128)S(1)} %get-tuple-element.36), channel_id=1, source_target_pairs={{0,32},{32,0},{64,96},{96,64},{128,160},{160,128},{192,224},{224,1... | collective-permute-start | bytes 3342344 | tf_op jit(solution)/shard_map/ppermute | solution.py:436
  137.7 2.2 %feat_grad.1.feat_ref = bf16[32,16,512]{2,1,0:T(8,128)(2,1)} custom-call(bf16[1024,2048]{1,0:T(8,128)(2,1)S(1)} %get-tuple-element.37.grad_ref, bf16[256,2048]{1,0:T(8,128)(2,1)S(1)} %get-tuple-element.29.cols_ref, bf16[256,1024]{1,0:T(8,128)(2,1)S(1)} %get-tuple-element.38.raw_feat_ref, f32[1,1024]{1,0:T(1,128)S(1)} %get-tuple-element.39.feat_inv_ref), custom_call_target="tpu_custom_call" | custom-call | tf_op jit(solution)/shard_map/feat_grad/pallas_call | solution.py:437
  140.5 2.3 %collective-permute-start.2 = (bf16[4,16,2176]{2,1,0:T(8,128)(2,1)S(1)}, bf16[4,16,2176]{2,1,0:T(8,128)(2,1)S(1)}, u32[]{:S(2)}, u32[]{:S(2)}) collective-permute-start(bf16[4,16,2176]{2,1,0:T(8,128)(2,1)S(1)} %get-tuple-element.41), channel_id=1, source_target_pairs={{0,64},{32,96},{64,0},{96,32},{128,192},{160,224},{192,128},{224,1... | collective-permute-start | bytes 835592 | tf_op jit(solution)/shard_map/ppermute | solution.py:457
  142.8 4.8 %all-to-all-start.7 = ((bf16[32,16,512]{2,1,0:T(8,128)(2,1)}), bf16[32,16,512]{2,1,0:T(8,128)(2,1)}, u32[]{:S(2)}, u32[]{:S(2)}) async-start(bf16[32,16,512]{2,1,0:T(8,128)(2,1)} %get-tuple-element.46), calls=%async_computation.7 | async-start | bytes 1048576 | tf_op jit(solution)/shard_map/all_to_all | solution.py:348
  147.6 3.6 %collective-permute-done.2.got_ref = bf16[4,16,2176]{2,1,0:T(8,128)(2,1)S(1)} collective-permute-done((bf16[4,16,2176]{2,1,0:T(8,128)(2,1)S(1)}, bf16[4,16,2176]{2,1,0:T(8,128)(2,1)S(1)}, u32[]{:S(2)}, u32[]{:S(2)}) %collective-permute-start.2) | collective-permute-done | bytes 278560 | tf_op jit(solution)/shard_map/ppermute | solution.py:457
  151.3 2.5 %collective-permute-start.3 = (bf16[16,2176]{1,0:T(8,128)(2,1)S(1)}, bf16[16,2176]{1,0:T(8,128)(2,1)S(1)}, u32[]{:S(2)}, u32[]{:S(2)}) collective-permute-start(bf16[16,2176]{1,0:T(8,128)(2,1)S(1)} %get-tuple-element.43), channel_id=1, source_target_pairs={{0,128},{32,160},{64,192},{96,224},{128,0},{160,32},{192,64},{224,... | collective-permute-start | bytes 208904 | tf_op jit(solution)/shard_map/ppermute | solution.py:467
  153.8 4.3 %collective-permute-start.4 = (bf16[16,2176]{1,0:T(8,128)(2,1)S(1)}, bf16[16,2176]{1,0:T(8,128)(2,1)S(1)}, u32[]{:S(2)}, u32[]{:S(2)}) collective-permute-start(bf16[16,2176]{1,0:T(8,128)(2,1)S(1)} %get-tuple-element.44), channel_id=1, source_target_pairs={{0,256},{32,288},{64,320},{96,352},{128,384},{160,416},{192,448},{... | collective-permute-start | bytes 208904 | tf_op jit(solution)/shard_map/ppermute | solution.py:467
  158.1 5.4 %collective-permute-start.5 = (bf16[16,2176]{1,0:T(8,128)(2,1)S(1)}, bf16[16,2176]{1,0:T(8,128)(2,1)S(1)}, u32[]{:S(2)}, u32[]{:S(2)}) collective-permute-start(bf16[16,2176]{1,0:T(8,128)(2,1)S(1)} %get-tuple-element.45), channel_id=1, source_target_pairs={{0,384},{32,416},{64,448},{96,480},{128,256},{160,288},{192,320},{... | collective-permute-start | bytes 208904 | tf_op jit(solution)/shard_map/ppermute | solution.py:467
  163.6 1.8 %all-to-all-done.7.source_ref = bf16[32,16,512]{2,1,0:T(8,128)(2,1)} async-done(((bf16[32,16,512]{2,1,0:T(8,128)(2,1)}), bf16[32,16,512]{2,1,0:T(8,128)(2,1)}, u32[]{:S(2)}, u32[]{:S(2)}) %all-to-all-start.7) | async-done | bytes 524320 | tf_op jit(solution)/shard_map/all_to_all | solution.py:348
  165.3 1.8 %feat_sum.1.after_ref = f32[8,1024]{1,0:T(8,128)} custom-call(bf16[32,16,512]{2,1,0:T(8,128)(2,1)} %all-to-all-done.7.source_ref), custom_call_target="tpu_custom_call" | custom-call | tf_op jit(solution)/shard_map/feat_sum/pallas_call | solution.py:48
  (22 shorter events, 8.3 us)
Async XLA Ops:
  0.6 48.9 %copy-start.3 = (bf16[1024,8]{0,1:T(8,128)(2,1)S(1)}, bf16[1024,8]{0,1:T(8,128)(2,1)}, u32[]{:S(2)}) copy-start(bf16[1024,8]{0,1:T(8,128)(2,1)} %param.4) | copy-start | bytes 49156
  0.6 0.7 copy-start.4
  2.2 27.8 %all-to-all-start = ((bf16[32,8,1024]{2,1,0:T(8,128)(2,1)}), bf16[32,8,1024]{2,1,0:T(8,128)(2,1)S(1)}, u32[]{:S(2)}, u32[]{:S(2)}) async-start(bf16[32,8,1024]{2,1,0:T(8,128)(2,1)} %prepare.1), calls=%async_computation | async-start | bytes 1048576 | tf_op jit(solution)/shard_map/all_to_all | solution.py:348
  12.4 1.2 copy-start
  13.6 1.2 copy-start.1
  69.1 13.9 %collective-permute-start = (bf16[32,8,640]{2,1,0:T(8,128)(2,1)S(1)}, bf16[32,8,640]{2,1,0:T(8,128)(2,1)S(1)}, u32[]{:S(2)}, u32[]{:S(2)}) collective-permute-start(bf16[32,8,640]{2,1,0:T(8,128)(2,1)S(1)} %all_to_all.41.got_ref.own_ref), channel_id=1, source_target_pairs={{0,8},{1,9},{2,10},{3,11},{4,12},{5,13},{6,14},{7,15},{8,0},{9,1},... | collective-permute-start | bytes 983048 | tf_op jit(solution)/shard_map/ppermute | solution.py:380
  135.7 4.6 %collective-permute-start.1 = (f32[2,4,16,2176]{3,2,1,0:T(8,128)S(1)}, f32[2,4,16,2176]{3,2,1,0:T(8,128)S(1)}, u32[]{:S(2)}, u32[]{:S(2)}) collective-permute-start(f32[2,4,16,2176]{3,2,1,0:T(8,128)S(1)} %get-tuple-element.36), channel_id=1, source_target_pairs={{0,32},{32,0},{64,96},{96,64},{128,160},{160,128},{192,224},{224,1... | collective-permute-start | bytes 3342344 | tf_op jit(solution)/shard_map/ppermute | solution.py:436
  140.5 10.6 %collective-permute-start.2 = (bf16[4,16,2176]{2,1,0:T(8,128)(2,1)S(1)}, bf16[4,16,2176]{2,1,0:T(8,128)(2,1)S(1)}, u32[]{:S(2)}, u32[]{:S(2)}) collective-permute-start(bf16[4,16,2176]{2,1,0:T(8,128)(2,1)S(1)} %get-tuple-element.41), channel_id=1, source_target_pairs={{0,64},{32,96},{64,0},{96,32},{128,192},{160,224},{192,128},{224,1... | collective-permute-start | bytes 835592 | tf_op jit(solution)/shard_map/ppermute | solution.py:457
  142.8 22.5 %all-to-all-start.7 = ((bf16[32,16,512]{2,1,0:T(8,128)(2,1)}), bf16[32,16,512]{2,1,0:T(8,128)(2,1)}, u32[]{:S(2)}, u32[]{:S(2)}) async-start(bf16[32,16,512]{2,1,0:T(8,128)(2,1)} %get-tuple-element.46), calls=%async_computation.7 | async-start | bytes 1048576 | tf_op jit(solution)/shard_map/all_to_all | solution.py:348
  151.3 15.8 %collective-permute-start.3 = (bf16[16,2176]{1,0:T(8,128)(2,1)S(1)}, bf16[16,2176]{1,0:T(8,128)(2,1)S(1)}, u32[]{:S(2)}, u32[]{:S(2)}) collective-permute-start(bf16[16,2176]{1,0:T(8,128)(2,1)S(1)} %get-tuple-element.43), channel_id=1, source_target_pairs={{0,128},{32,160},{64,192},{96,224},{128,0},{160,32},{192,64},{224,... | collective-permute-start | bytes 208904 | tf_op jit(solution)/shard_map/ppermute | solution.py:467
  153.8 13.3 %collective-permute-start.4 = (bf16[16,2176]{1,0:T(8,128)(2,1)S(1)}, bf16[16,2176]{1,0:T(8,128)(2,1)S(1)}, u32[]{:S(2)}, u32[]{:S(2)}) collective-permute-start(bf16[16,2176]{1,0:T(8,128)(2,1)S(1)} %get-tuple-element.44), channel_id=1, source_target_pairs={{0,256},{32,288},{64,320},{96,352},{128,384},{160,416},{192,448},{... | collective-permute-start | bytes 208904 | tf_op jit(solution)/shard_map/ppermute | solution.py:467
  158.1 9.0 %collective-permute-start.5 = (bf16[16,2176]{1,0:T(8,128)(2,1)S(1)}, bf16[16,2176]{1,0:T(8,128)(2,1)S(1)}, u32[]{:S(2)}, u32[]{:S(2)}) collective-permute-start(bf16[16,2176]{1,0:T(8,128)(2,1)S(1)} %get-tuple-element.45), channel_id=1, source_target_pairs={{0,384},{32,416},{64,448},{96,480},{128,256},{160,288},{192,320},{... | collective-permute-start | bytes 208904 | tf_op jit(solution)/shard_map/ppermute | solution.py:467
  167.1 0.8 copy-start.2

commit v8 on v7

--- a/solution.py
+++ b/solution.py
@@ -153,15 +153,16 @@
     sublane_major(1.0 / (CROPS * jnp.sum(got_ref[:, :, -LANES:].astype(F32), axis=0)), rows_ref)
     acc_ref[...] = jnp.zeros_like(acc_ref)
 
-    def block(j, carry):
-        at = row_block(j)
-        r = rows_ref[at, :]
-        for i in range(COL_TILES):
-            lanes = slice(LANES * i, LANES * (i + 1))
-            acc_ref[:, lanes] += jnp.sum((exp_ref[at, lanes] * r).reshape(LANES // 8, 8, LANES), axis=0)
+    def block(pair, carry):
+        for j in (2 * pair, 2 * pair + 1):
+            at = row_block(j)
+            r = rows_ref[at, :]
+            for i in range(COL_TILES):
+                lanes = slice(LANES * i, LANES * (i + 1))
+                acc_ref[:, lanes] += jnp.sum((exp_ref[at, lanes] * r).reshape(LANES // 8, 8, LANES), axis=0)
         return carry
 
-    lax.fori_loop(0, ROW_TILES, block, 0)
+    lax.fori_loop(0, ROW_TILES // 2, block, 0)
     put(out_ref, col_rows(acc_ref).astype(out_ref.dtype))
 
 
@@ -201,11 +202,14 @@
                 cross += weighted * logit
                 total += e
             part_ref[band, :], cross_ref[band, :], total_ref[band, :] = acc, cross, total
+    refs = (part_ref, total_ref, cross_ref)
+    for i, ref in enumerate(refs):
+        lane_major(ref, sum_ref.at[pl.ds(ROW_TILES * i, ROW_TILES)])
     sends = []
-    for ref in (part_ref, total_ref, cross_ref):
-        lane_major(ref, sum_ref)
-        high = sum_ref[...].astype(BF16).astype(F32)
-        sends += [high, sum_ref[...] - high]
+    for i in range(len(refs)):
+        sums = sum_ref[ROW_TILES * i : ROW_TILES * (i + 1), :]
+        high = sums.astype(BF16).astype(F32)
+        sends += [high, sums - high]
     put(out_ref, jnp.concatenate(sends[:5], axis=0).astype(BF16))
 
 
@@ -404,7 +408,7 @@
             last_shape,
         ],
         [own_half, other_half, pin(teacher_exp), proto_round, got],
-        [pltpu.VMEM((ROWS, D), BF16), col_tile, row_part, row_part, row_part, row_tile],
+        [pltpu.VMEM((ROWS, D), BF16), col_tile, row_part, row_part, row_part, pltpu.VMEM((3 * ROW_TILES, LANES), F32)],
         name="student_and_last_row",
     )
     got = over_proto(send)
@@ -464,8 +468,7 @@
         name="join_pairs",
     )
     quads = [
-        lax.ppermute(send, "batch", [(i, i ^ 4 * away) for i in range(BATCH)])
-        for away, send in enumerate(sends, 1)
+        lax.ppermute(sends[away - 1], "batch", [(i, i ^ 4 * away) for i in range(BATCH)]) for away in (2, 3, 1)
     ]
     (feat_out,) = call(
         feat_sum_kernel,

time: 169 us -> 169 us (level)
  transfers between devices with their start and end apart: 8 -> 8, of which waited for: 4 -> 5; matrix products, arithmetic and copies ran while one was open for 0% -> 0% of each run, Pallas kernels for 3% -> 3%
where the time goes in v8:
time: 169 us; the launch traced here: 168 us
  blocking collectives  91.4 us (54%)
  starting transfers between devices  33.8 us (20%)
  waiting for transfers between devices  20.4 us (12%)
  Pallas kernels  18.1 us (11%)
  local copies, waits for them, and re-layouts  3.92 us (2%)
    all_to_all x3, blocking collectives, over_proto(): return lax.all_to_all(array, 'proto', 0, 0)  51.6 us
    all_to_all x3, blocking collectives, over_batch(): return lax.all_to_all(array, 'batch', 0, 0)  39.8 us
    all_to_all x2, waiting for transfers between devices, over_proto(): return lax.all_to_all(array, 'proto', 0, 0)  16.2 us
    pallas_call x12, Pallas kernels, call(): pl.pallas_call(body, out_shape=outs, in_specs=specs or [VM] * len(args),...  15.8 us
    all_to_all x2, starting transfers between devices, over_proto(): return lax.all_to_all(array, 'proto', 0, 0)  14.9 us
    ppermute x3, starting transfers between devices, per_device(): lax.ppermute(sends[away - 1], 'batch', [(i, i ^ 4 * away) for i in range(...  12.2 us
    unnamed x10, local copies, waits for them, and re-layouts  3.92 us
    ppermute x1, waiting for transfers between devices, per_device(): arrived = lax.ppermute(send, 'batch', swap_pairs)  3.56 us
  transfers between devices with their start and end apart: 8, of which 5 were waited for; matrix products, arithmetic and copies ran while one was open for 0% of the time, Pallas kernels for 3%

profile of v8, /device:TPU:8, one launch (start us, length us, event | category | flops | bytes accessed | tf_op | source)
XLA Modules:
  0.0 168.5 jit_solution(969893781414120276)
XLA Ops:
  2.2 10.2 %all-to-all-start = ((bf16[32,8,1024]{2,1,0:T(8,128)(2,1)}), bf16[32,8,1024]{2,1,0:T(8,128)(2,1)S(1)}, u32[]{:S(2)}, u32[]{:S(2)}) async-start(bf16[32,8,1024]{2,1,0:T(8,128)(2,1)} %prepare.1), calls=%async_computation | async-start | bytes 1048576 | tf_op jit(solution)/shard_map/all_to_all | solution.py:352
  12.4 1.2 copy-done
  13.6 1.2 copy-done.1
  15.6 14.5 %all-to-all-done.feat_ref = bf16[32,8,1024]{2,1,0:T(8,128)(2,1)S(1)} async-done(((bf16[32,8,1024]{2,1,0:T(8,128)(2,1)}), bf16[32,8,1024]{2,1,0:T(8,128)(2,1)S(1)}, u32[]{:S(2)}, u32[]{:S(2)}) %all-to-all-start) | async-done | bytes 524320 | tf_op jit(solution)/shard_map/all_to_all | solution.py:352
  30.0 1.4 teacher_exp.1
  31.4 18.1 %all_to_all.40.got_ref = bf16[16,16,128]{2,1,0:T(8,128)(2,1)S(1)} all-to-all(bf16[16,16,128]{2,1,0:T(8,128)(2,1)S(1)} %get-tuple-element.28), channel_id=1, replica_groups=mesh['batch'=16,'proto'=32] {'batch'}, dimensions={0} | all-to-all | bytes 131072 | tf_op jit(solution)/shard_map/all_to_all | solution.py:349
  50.4 18.8 %all_to_all.41.got_ref.own_ref = bf16[32,8,640]{2,1,0:T(8,128)(2,1)S(1)} all-to-all(bf16[32,8,640]{2,1,0:T(8,128)(2,1)S(1)} %row_pass_1.1), channel_id=1, replica_groups=mesh['batch'=16,'proto'=32] {'proto'}, dimensions={0} | all-to-all | bytes 655360 | tf_op jit(solution)/shard_map/all_to_all | solution.py:352
  69.1 2.5 %collective-permute-start = (bf16[32,8,640]{2,1,0:T(8,128)(2,1)S(1)}, bf16[32,8,640]{2,1,0:T(8,128)(2,1)S(1)}, u32[]{:S(2)}, u32[]{:S(2)}) collective-permute-start(bf16[32,8,640]{2,1,0:T(8,128)(2,1)S(1)} %all_to_all.41.got_ref.own_ref), channel_id=1, source_target_pairs={{0,8},{1,9},{2,10},{3,11},{4,12},{5,13},{6,14},{7,15},{8,0},{9,1},... | collective-permute-start | bytes 983048 | tf_op jit(solution)/shard_map/ppermute | solution.py:384
  72.6 10.4 %all_to_all.42.got_ref = bf16[16,16,128]{2,1,0:T(8,128)(2,1)S(1)} all-to-all(bf16[16,16,128]{2,1,0:T(8,128)(2,1)S(1)} %col_pass_2.1), channel_id=1, replica_groups=mesh['batch'=16,'proto'=32] {'batch'}, dimensions={0} | all-to-all | bytes 131072 | tf_op jit(solution)/shard_map/all_to_all | solution.py:349
  83.8 14.3 %all_to_all.43.got_ref = bf16[32,8,128]{2,1,0:T(8,128)(2,1)S(1)} all-to-all(bf16[32,8,128]{2,1,0:T(8,128)(2,1)S(1)} %row_pass_2.1), channel_id=1, replica_groups=mesh['batch'=16,'proto'=32] {'proto'}, dimensions={0} | all-to-all | bytes 131072 | tf_op jit(solution)/shard_map/all_to_all | solution.py:352
  99.1 11.3 %all_to_all.44.got_ref = f32[16,16,128]{2,1,0:T(8,128)S(1)} all-to-all(f32[16,16,128]{2,1,0:T(8,128)S(1)} %col_pass_3.1), channel_id=1, replica_groups=mesh['batch'=16,'proto'=32] {'batch'}, dimensions={0} | all-to-all | bytes 262144 | tf_op jit(solution)/shard_map/all_to_all | solution.py:349
  110.4 3.2 %student_and_last_row.1 = (f32[1024,2048]{1,0:T(8,128)S(1)}, f32[1024,2048]{1,0:T(8,128)S(1)}, bf16[256,1024]{1,0:T(8,128)(2,1)S(1)}, bf16[256,1024]{1,0:T(8,128...) custom-call(bf16[32,8,640]{2,1,0:T(8,128)(2,1)S(1)} %all_to_all.41.got_ref.own_ref, ...), custom_call_target="tpu_custom_call" | custom-call | tf_op jit(solution)/shard_map/student_and_last_row/pallas_call | solution.py:48
  113.6 18.5 %all_to_all.45.got_ref = bf16[32,40,128]{2,1,0:T(8,128)(2,1)S(1)} all-to-all(bf16[32,40,128]{2,1,0:T(8,128)(2,1)S(1)} %get-tuple-element.33), channel_id=1, replica_groups=mesh['batch'=16,'proto'=32] {'proto'}, dimensions={0} | all-to-all | bytes 655360 | tf_op jit(solution)/shard_map/all_to_all | solution.py:352
  132.2 3.4 %proto_grad.1 = (bf16[1024,2048]{1,0:T(8,128)(2,1)S(1)}, f32[2,4,16,2176]{3,2,1,0:T(8,128)S(1)}, f32[2,4,16,2176]{3,2,1,0:T(8,128)S(1)}) custom-call(f32[1024,2048]{1,0:T(8,128)S(1)} %get-tuple-element.30.weighted_ref, f32[1024,2048]{1,0:T(8,128)S(1)} %get-tuple-element.31.exp_ref, bf16[4,2,2,16,1024]{4,3,2,1,0:T(8,128)(2,1)S(1)} %bitcast.7, ...), custom_call_target="tpu_custom_call" | custom-call | tf_op jit(solution)/shard_map/proto_grad/pallas_call | solution.py:48
  135.6 1.9 %collective-permute-start.1 = (f32[2,4,16,2176]{3,2,1,0:T(8,128)S(1)}, f32[2,4,16,2176]{3,2,1,0:T(8,128)S(1)}, u32[]{:S(2)}, u32[]{:S(2)}) collective-permute-start(f32[2,4,16,2176]{3,2,1,0:T(8,128)S(1)} %get-tuple-element.36), channel_id=1, source_target_pairs={{0,32},{32,0},{64,96},{96,64},{128,160},{160,128},{192,224},{224,1... | collective-permute-start | bytes 3342344 | tf_op jit(solution)/shard_map/ppermute | solution.py:440
  137.5 2.2 %feat_grad.1.feat_ref = bf16[32,16,512]{2,1,0:T(8,128)(2,1)} custom-call(bf16[1024,2048]{1,0:T(8,128)(2,1)S(1)} %get-tuple-element.37.grad_ref, bf16[256,2048]{1,0:T(8,128)(2,1)S(1)} %get-tuple-element.29.cols_ref, bf16[256,1024]{1,0:T(8,128)(2,1)S(1)} %get-tuple-element.38.raw_feat_ref, f32[1,1024]{1,0:T(1,128)S(1)} %get-tuple-element.39.feat_inv_ref), custom_call_target="tpu_custom_call" | custom-call | tf_op jit(solution)/shard_map/feat_grad/pallas_call | solution.py:441
  140.4 2.3 %collective-permute-start.2 = (bf16[4,16,2176]{2,1,0:T(8,128)(2,1)S(1)}, bf16[4,16,2176]{2,1,0:T(8,128)(2,1)S(1)}, u32[]{:S(2)}, u32[]{:S(2)}) collective-permute-start(bf16[4,16,2176]{2,1,0:T(8,128)(2,1)S(1)} %get-tuple-element.41), channel_id=1, source_target_pairs={{0,64},{32,96},{64,0},{96,32},{128,192},{160,224},{192,128},{224,1... | collective-permute-start | bytes 835592 | tf_op jit(solution)/shard_map/ppermute | solution.py:461
  142.7 4.8 %all-to-all-start.7 = ((bf16[32,16,512]{2,1,0:T(8,128)(2,1)}), bf16[32,16,512]{2,1,0:T(8,128)(2,1)}, u32[]{:S(2)}, u32[]{:S(2)}) async-start(bf16[32,16,512]{2,1,0:T(8,128)(2,1)} %get-tuple-element.46), calls=%async_computation.7 | async-start | bytes 1048576 | tf_op jit(solution)/shard_map/all_to_all | solution.py:352
  147.4 3.6 %collective-permute-done.2.got_ref = bf16[4,16,2176]{2,1,0:T(8,128)(2,1)S(1)} collective-permute-done((bf16[4,16,2176]{2,1,0:T(8,128)(2,1)S(1)}, bf16[4,16,2176]{2,1,0:T(8,128)(2,1)S(1)}, u32[]{:S(2)}, u32[]{:S(2)}) %collective-permute-start.2) | collective-permute-done | bytes 278560 | tf_op jit(solution)/shard_map/ppermute | solution.py:461
  151.2 2.9 %collective-permute-start.3 = (bf16[16,2176]{1,0:T(8,128)(2,1)S(1)}, bf16[16,2176]{1,0:T(8,128)(2,1)S(1)}, u32[]{:S(2)}, u32[]{:S(2)}) collective-permute-start(bf16[16,2176]{1,0:T(8,128)(2,1)S(1)} %get-tuple-element.43), channel_id=1, source_target_pairs={{0,256},{32,288},{64,320},{96,352},{128,384},{160,416},{192,448},{... | collective-permute-start | bytes 208904 | tf_op jit(solution)/shard_map/ppermute | solution.py:471
  154.1 5.1 %collective-permute-start.4 = (bf16[16,2176]{1,0:T(8,128)(2,1)S(1)}, bf16[16,2176]{1,0:T(8,128)(2,1)S(1)}, u32[]{:S(2)}, u32[]{:S(2)}) collective-permute-start(bf16[16,2176]{1,0:T(8,128)(2,1)S(1)} %get-tuple-element.44), channel_id=1, source_target_pairs={{0,384},{32,416},{64,448},{96,480},{128,256},{160,288},{192,320},{... | collective-permute-start | bytes 208904 | tf_op jit(solution)/shard_map/ppermute | solution.py:471
  159.2 4.2 %collective-permute-start.5 = (bf16[16,2176]{1,0:T(8,128)(2,1)S(1)}, bf16[16,2176]{1,0:T(8,128)(2,1)S(1)}, u32[]{:S(2)}, u32[]{:S(2)}) collective-permute-start(bf16[16,2176]{1,0:T(8,128)(2,1)S(1)} %get-tuple-element.45), channel_id=1, source_target_pairs={{0,128},{32,160},{64,192},{96,224},{128,0},{160,32},{192,64},{224,... | collective-permute-start | bytes 208904 | tf_op jit(solution)/shard_map/ppermute | solution.py:471
  163.4 1.8 %all-to-all-done.7.source_ref = bf16[32,16,512]{2,1,0:T(8,128)(2,1)} async-done(((bf16[32,16,512]{2,1,0:T(8,128)(2,1)}), bf16[32,16,512]{2,1,0:T(8,128)(2,1)}, u32[]{:S(2)}, u32[]{:S(2)}) %all-to-all-start.7) | async-done | bytes 524320 | tf_op jit(solution)/shard_map/all_to_all | solution.py:352
  165.2 1.8 %feat_sum.1.after_ref = f32[8,1024]{1,0:T(8,128)} custom-call(bf16[32,16,512]{2,1,0:T(8,128)(2,1)} %all-to-all-done.7.source_ref), custom_call_target="tpu_custom_call" | custom-call | tf_op jit(solution)/shard_map/feat_sum/pallas_call | solution.py:48
  (22 shorter events, 8.2 us)
Async XLA Ops:
  0.6 48.9 %copy-start.3 = (bf16[1024,8]{0,1:T(8,128)(2,1)S(1)}, bf16[1024,8]{0,1:T(8,128)(2,1)}, u32[]{:S(2)}) copy-start(bf16[1024,8]{0,1:T(8,128)(2,1)} %param.4) | copy-start | bytes 49156
  0.6 0.7 copy-start.4
  2.2 27.8 %all-to-all-start = ((bf16[32,8,1024]{2,1,0:T(8,128)(2,1)}), bf16[32,8,1024]{2,1,0:T(8,128)(2,1)S(1)}, u32[]{:S(2)}, u32[]{:S(2)}) async-start(bf16[32,8,1024]{2,1,0:T(8,128)(2,1)} %prepare.1), calls=%async_computation | async-start | bytes 1048576 | tf_op jit(solution)/shard_map/all_to_all | solution.py:352
  12.4 1.2 copy-start
  13.6 1.2 copy-start.1
  69.1 13.8 %collective-permute-start = (bf16[32,8,640]{2,1,0:T(8,128)(2,1)S(1)}, bf16[32,8,640]{2,1,0:T(8,128)(2,1)S(1)}, u32[]{:S(2)}, u32[]{:S(2)}) collective-permute-start(bf16[32,8,640]{2,1,0:T(8,128)(2,1)S(1)} %all_to_all.41.got_ref.own_ref), channel_id=1, source_target_pairs={{0,8},{1,9},{2,10},{3,11},{4,12},{5,13},{6,14},{7,15},{8,0},{9,1},... | collective-permute-start | bytes 983048 | tf_op jit(solution)/shard_map/ppermute | solution.py:384
  135.6 4.6 %collective-permute-start.1 = (f32[2,4,16,2176]{3,2,1,0:T(8,128)S(1)}, f32[2,4,16,2176]{3,2,1,0:T(8,128)S(1)}, u32[]{:S(2)}, u32[]{:S(2)}) collective-permute-start(f32[2,4,16,2176]{3,2,1,0:T(8,128)S(1)} %get-tuple-element.36), channel_id=1, source_target_pairs={{0,32},{32,0},{64,96},{96,64},{128,160},{160,128},{192,224},{224,1... | collective-permute-start | bytes 3342344 | tf_op jit(solution)/shard_map/ppermute | solution.py:440
  140.4 10.6 %collective-permute-start.2 = (bf16[4,16,2176]{2,1,0:T(8,128)(2,1)S(1)}, bf16[4,16,2176]{2,1,0:T(8,128)(2,1)S(1)}, u32[]{:S(2)}, u32[]{:S(2)}) collective-permute-start(bf16[4,16,2176]{2,1,0:T(8,128)(2,1)S(1)} %get-tuple-element.41), channel_id=1, source_target_pairs={{0,64},{32,96},{64,0},{96,32},{128,192},{160,224},{192,128},{224,1... | collective-permute-start | bytes 835592 | tf_op jit(solution)/shard_map/ppermute | solution.py:461
  142.7 22.5 %all-to-all-start.7 = ((bf16[32,16,512]{2,1,0:T(8,128)(2,1)}), bf16[32,16,512]{2,1,0:T(8,128)(2,1)}, u32[]{:S(2)}, u32[]{:S(2)}) async-start(bf16[32,16,512]{2,1,0:T(8,128)(2,1)} %get-tuple-element.46), calls=%async_computation.7 | async-start | bytes 1048576 | tf_op jit(solution)/shard_map/all_to_all | solution.py:352
  151.2 15.8 %collective-permute-start.3 = (bf16[16,2176]{1,0:T(8,128)(2,1)S(1)}, bf16[16,2176]{1,0:T(8,128)(2,1)S(1)}, u32[]{:S(2)}, u32[]{:S(2)}) collective-permute-start(bf16[16,2176]{1,0:T(8,128)(2,1)S(1)} %get-tuple-element.43), channel_id=1, source_target_pairs={{0,256},{32,288},{64,320},{96,352},{128,384},{160,416},{192,448},{... | collective-permute-start | bytes 208904 | tf_op jit(solution)/shard_map/ppermute | solution.py:471
  154.1 12.9 %collective-permute-start.4 = (bf16[16,2176]{1,0:T(8,128)(2,1)S(1)}, bf16[16,2176]{1,0:T(8,128)(2,1)S(1)}, u32[]{:S(2)}, u32[]{:S(2)}) collective-permute-start(bf16[16,2176]{1,0:T(8,128)(2,1)S(1)} %get-tuple-element.44), channel_id=1, source_target_pairs={{0,384},{32,416},{64,448},{96,480},{128,256},{160,288},{192,320},{... | collective-permute-start | bytes 208904 | tf_op jit(solution)/shard_map/ppermute | solution.py:471
  159.2 7.8 %collective-permute-start.5 = (bf16[16,2176]{1,0:T(8,128)(2,1)S(1)}, bf16[16,2176]{1,0:T(8,128)(2,1)S(1)}, u32[]{:S(2)}, u32[]{:S(2)}) collective-permute-start(bf16[16,2176]{1,0:T(8,128)(2,1)S(1)} %get-tuple-element.45), channel_id=1, source_target_pairs={{0,128},{32,160},{64,192},{96,224},{128,0},{160,32},{192,64},{224,... | collective-permute-start | bytes 208904 | tf_op jit(solution)/shard_map/ppermute | solution.py:471
  167.0 0.8 copy-start.2
